TPU v7x, 512 devices: a whole 4x4x16 slice. The times are simulated.
512 devices in a mesh: mp: 16 (over x, y), dp: 32 (over z, core).
Axes of the slice: x: 4, y: 4, z: 16, core: 2. Of those that a mesh axis runs over, the one named last changes fastest.
Arguments:
- inputs: bfloat16 [5120, 8192], P('dp'), may hold values from -60 to 60
- cotangent: bfloat16 [5120, 16384], P('dp', 'mp'), may hold values from -11 to 11
- weight: float32 [8192, 16384], P('dp', 'mp'), may hold values from -6 to 6
- row_moment: float32 [8192], P('dp'), may hold values from 0.05 to 0.5
- col_moment: float32 [16384], P('mp'), may hold values from 0.01 to 60
Outputs:
- new_weight: float32 [8192, 16384], P('dp', 'mp')
- update: bfloat16 [8192, 16384], P('dp', 'mp')
- new_rows: float32 [8192], P('dp')
- new_cols: float32 [16384], P('mp')
All inputs are finite; a program needn't handle non-finite values.
Results may differ from a plain program's by a relative error of at most 0.001.
Values may be sent and summed in bfloat16 or wider, within the bound.
No kernel may reach another device: no remote copies, remote signals or barrier semaphores. Data moves between devices by JAX's collectives and lax.ppermute only.
A program may use at most 64 MiB of HBM per device.

v0:
```python
import jax
import jax.numpy as jnp
from jax import lax
from jax.sharding import PartitionSpec as P

D = 8192
F = 16384


decay_rate = 1.0 - 10.0 ** (-0.8)
step_size = 0.05
tiny_eps = 1e-30


def contract(left, right):
    return lax.dot_general(
        left, right, (((0,), (0,)), ((), ())), preferred_element_type=jnp.float32
    )


def on_device(inputs, cotangent, weight, row_moment, col_moment):
    feat_rows = lax.all_to_all(inputs, "dp", split_axis=1, concat_axis=0, tiled=True)
    gradient = contract(feat_rows, lax.all_gather(cotangent, "dp", axis=0, tiled=True))
    squares = gradient * gradient + tiny_eps
    row_part = jnp.sum(squares, axis=1)
    col_part = jnp.sum(squares, axis=0)
    weight_sq = jnp.sum(weight * weight)
    row_total, weight_mp = lax.psum((row_part, weight_sq), "mp")
    new_rows = decay_rate * row_moment + (1.0 - decay_rate) * (row_total / F)
    col_total, rows_sum, weight_all = lax.psum((col_part, jnp.sum(new_rows), weight_mp), "dp")
    new_cols = decay_rate * col_moment + (1.0 - decay_rate) * (col_total / D)
    row_mean = rows_sum / D
    scaled = gradient / jnp.sqrt(new_rows[:, None] * new_cols[None, :] / row_mean)
    scaled_sq = lax.psum(jnp.sum(scaled * scaled), ("mp", "dp"))
    update_rms = jnp.sqrt(scaled_sq / (D * F))
    clipped = scaled / jnp.maximum(1.0, update_rms)
    weight_rms = jnp.sqrt(weight_all / (D * F))
    new_weight = weight - step_size * weight_rms * clipped
    return (new_weight, clipped.astype(jnp.bfloat16), new_rows, new_cols)


def solution(mesh):
    return jax.shard_map(
        on_device,
        mesh=mesh,
        in_specs=(P("dp", None), P("dp", "mp"), P("dp", "mp"), P("dp"), P("mp")),
        out_specs=(P("dp", "mp"), P("dp", "mp"), P("dp"), P("mp")),
        check_vma=False,
    )
```

profile of v0, /device:TPU:1, one launch (start us, length us, event | category | flops | bytes accessed | tf_op | source)
XLA Modules:
  0.0 413.0 jit_solution(204783504118000108)
XLA Ops:
  7.2 0.0 all-gather.2.cloned.1.call-start
  7.2 0.7 all-gather.2.cloned.1.call-update
  7.9 3.6 copy.13
  11.5 16.8 %all-to-all-start = ((bf16[160,32,256]{2,0,1:T(8,128)(2,1)}), bf16[160,32,256]{2,0,1:T(8,128)(2,1)S(1)}, u32[]{:S(2)}, u32[]{:S(2)}) async-start(bf16[160,32,256]{2,0,1:T(8,128)(2,1)} %bitcast.10), calls=%async_computation | async-start | bytes 5242880 | tf_op jit(solution)/shard_map/all_to_all | solution.py:22
  28.2 2.1 multiply_reduce_fusion.1
  30.3 149.1 %all-to-all-done = bf16[160,32,256]{2,0,1:T(8,128)(2,1)S(1)} async-done(((bf16[160,32,256]{2,0,1:T(8,128)(2,1)}), bf16[160,32,256]{2,0,1:T(8,128)(2,1)S(1)}, u32[]{:S(2)}, u32[]{:S(2)}) %all-to-all-start) | async-done | bytes 2621472 | tf_op jit(solution)/shard_map/all_to_all | solution.py:22
  179.5 24.2 %all-gather.2.cloned.1.call-done = bf16[5120,1024]{1,0:T(8,128)(2,1)} async-done(((bf16[160,1024]{1,0:T(8,128)(2,1)}), bf16[5120,1024]{1,0:T(8,128)(2,1)}) %all-gather.2.cloned.1.call-update) | async-done | bytes 10485776 | tf_op jit(solution)/shard_map/all_gather | solution.py:23
  203.7 0.0 copy-start.3
  203.7 0.0 copy-start.2
  203.7 7.9 %fusion = (f32[1024]{0:T(1024)S(1)}, f32[256]{0:T(256)S(1)}, f32[256,1024]{1,0:T(8,128)}) fusion(bf16[5120,256]{1,0:T(8,128)(2,1)S(1)} %bitcast.9, bf16[5120,1024]{1,0:T(8,128)(2,1)} %all-gather.2.cloned.1.call-done), kind=kOutput, calls=%fused_computation.6 | convolution fusion | flops 2685401856 | bytes 14160896 | tf_op jit(solution)/shard_map/dot_general | solution.py:16
  211.6 34.0 %all-reduce.1 = (f32[]{:T(128)}, f32[256]{0:T(256)S(1)}) all-reduce(f32[]{:T(128)} %multiply_reduce_fusion.1, f32[256]{0:T(256)S(1)} %get-tuple-element.5), channel_id=1, replica_groups=mesh['mp'=16,'dp'=32] {'mp'}, use_global_device_ids=true, to_apply=%region_1.0 | all-reduce | flops 257 | bytes 2056 | tf_op jit(solution)/shard_map/psum | solution.py:28
  245.6 0.0 copy-done.3
  245.6 0.6 fusion.3
  246.2 0.0 copy-start.1
  246.2 54.3 %all-reduce = (f32[]{:T(128)}, f32[]{:T(128)}, f32[1024]{0:T(1024)S(1)}) all-reduce(f32[]{:T(128)} %get-tuple-element.9, f32[]{:T(128)} %get-tuple-element.11, f32[1024]{0:T(1024)S(1)} %get-tuple-element.4), channel_id=1, replica_groups=mesh['mp'=16,'dp'=32] {'dp'}, use_global_device_ids=true, to_apply=%region_2.0 | all-reduce | flops 1026 | bytes 8208 | tf_op jit(solution)/shard_map/psum | solution.py:30
  300.4 0.0 copy-done.2
  300.4 0.0 copy-start
  301.1 2.2 multiply_reduce_fusion
  303.3 98.4 %psum.47 = f32[]{:T(128)} all-reduce(f32[]{:T(128)} %multiply_reduce_fusion), channel_id=1, replica_groups=mesh['mp'=16,'dp'=32] {'mp','dp'}, use_global_device_ids=true, to_apply=%region_10.0 | all-reduce | flops 1 | bytes 8 | tf_op jit(solution)/shard_map/psum | solution.py:34
  403.1 3.0 fusion.2
  406.2 0.0 copy-done.1
  406.2 0.0 copy-done
  (1 shorter events, 0.0 us)
Async XLA Ops:
  7.2 196.5 %all-gather.2.cloned.1.call-start = ((), (), s32[]{:S(2)}) async-start(), calls=%async_computation.1 | async-start | bytes 10813440 | tf_op jit(solution)/shard_map/all_gather | solution.py:23
  11.5 168.0 %all-to-all-start = ((bf16[160,32,256]{2,0,1:T(8,128)(2,1)}), bf16[160,32,256]{2,0,1:T(8,128)(2,1)S(1)}, u32[]{:S(2)}, u32[]{:S(2)}) async-start(bf16[160,32,256]{2,0,1:T(8,128)(2,1)} %bitcast.10), calls=%async_computation | async-start | bytes 5242880 | tf_op jit(solution)/shard_map/all_to_all | solution.py:22
  203.7 41.9 %copy-start.3 = (f32[256]{0:T(256)S(1)}, f32[256]{0:T(256)}, u32[]{:S(2)}) copy-start(f32[256]{0:T(256)} %param.8) | copy-start | bytes 3076
  203.7 96.7 %copy-start.2 = (f32[1024]{0:T(1024)S(1)}, f32[1024]{0:T(1024)}, u32[]{:S(2)}) copy-start(f32[1024]{0:T(1024)} %param.9) | copy-start | bytes 12292
  246.2 160.0 %copy-start.1 = (f32[256]{0:T(256)}, f32[256]{0:T(256)S(1)}, u32[]{:S(2)}) copy-start(f32[256]{0:T(256)S(1)} %get-tuple-element.12) | copy-start | bytes 3076
  300.4 105.7 %copy-start = (f32[1024]{0:T(1024)}, f32[1024]{0:T(1024)S(1)}, u32[]{:S(2)}) copy-start(f32[1024]{0:T(1024)S(1)} %multiply_add_fusion.1) | copy-start | bytes 12292
Sparse Core Ops, SparseCore 0:
  10.1 193.5 all-gather.1
where the time goes:
time: 413 us
  blocking collectives  187 us (45%)
  waiting for transfers between devices  174 us (42%)
  starting transfers between devices  16.8 us (4%)
  between operations  16.1 us (4%)
  other arithmetic  7.92 us (2%)
  matrix products  7.87 us (2%)
    all_to_all x1, waiting for transfers between devices, on_device(): lax.all_to_all(inputs, 'dp', split_axis=1, concat_axis=0, tiled=True)  149 us
    psum x1, blocking collectives, on_device(): scaled_sq = lax.psum(jnp.sum(scaled * scaled), ('mp', 'dp'))  98.4 us
    psum x1, blocking collectives, on_device(): lax.psum((col_part, jnp.sum(new_rows), weight_mp), 'dp')  54.3 us
    psum x1, blocking collectives, on_device(): row_total, weight_mp = lax.psum((row_part, weight_sq), 'mp')  34 us
    all_gather x1, waiting for transfers between devices, on_device(): lax.all_gather(cotangent, 'dp', axis=0, tiled=True)  24.2 us
    all_to_all x1, starting transfers between devices, on_device(): lax.all_to_all(inputs, 'dp', split_axis=1, concat_axis=0, tiled=True)  16.8 us
  transfers between devices with their start and end apart: 2, of which 2 were waited for; matrix products, arithmetic and copies ran while one was open for 1% of the time, Pallas kernels for 0%

commit v1 on v0

v1 whole, which is shorter than its diff:
```python
import jax
import jax.numpy as jnp
from jax import lax
from jax.sharding import Mesh, PartitionSpec as P

D = 8192
F = 16384

decay_rate = 1.0 - 10.0 ** (-0.8)
step_size = 0.05
tiny_eps = 1e-30

NX, NY, NZ = 4, 4, 16
XY, ZC = ("x", "y"), ("z", "c")


def contract(left, right):
    return lax.dot_general(
        left, right, (((0,), (0,)), ((), ())), preferred_element_type=jnp.float32
    )


def shift(n, k):
    return [(i, (i + k) % n) for i in range(n)]


def gather_ring(block, axis, n):
    me = lax.axis_index(axis)
    out = jnp.zeros((n,) + block.shape, block.dtype)
    out = lax.dynamic_update_index_in_dim(out, block, me, 0)
    for k in range(1, n):
        got = lax.ppermute(block, axis, shift(n, k))
        out = lax.dynamic_update_index_in_dim(out, got, lax.rem(me + n - k, n), 0)
    return out


def sum_over(value, axes, n):
    copies = jnp.broadcast_to(value[None], (n,) + value.shape)
    return jnp.sum(lax.all_to_all(copies, axes, 0, 0), axis=0)


def features_of_rows(inputs):
    x, y, c = lax.axis_index("x"), lax.axis_index("y"), lax.axis_index("c")
    tokens = inputs.shape[0] // NY
    part = lax.dynamic_slice_in_dim(inputs, y * tokens, tokens, 0)
    part = part.reshape(tokens, NZ, NX, 128)
    part = lax.dynamic_index_in_dim(part, x, 2, keepdims=False)
    part = lax.all_to_all(part.transpose(1, 0, 2), "z", 0, 0)
    part = gather_ring(part, "x", NX)
    part = gather_ring(part, "y", NY)
    own = lax.dynamic_slice_in_dim(part, 2 * c, 2, 1)
    other = lax.dynamic_slice_in_dim(part, 2 - 2 * c, 2, 1)
    other = lax.ppermute(other, "c", shift(2, 1))
    both = jnp.where(c == 0, jnp.stack([own, other]), jnp.stack([other, own]))
    both = both.transpose(3, 0, 1, 4, 2, 5)
    return both.reshape(NZ * 2 * NY * tokens, 256)


def on_device(inputs, cotangent, weight, row_moment, col_moment):
    all_cotangent = lax.all_gather(cotangent, ZC, axis=0, tiled=True)
    feat_rows = features_of_rows(inputs)
    weight_sq = jnp.sum(weight * weight)
    gradient = contract(feat_rows, all_cotangent)
    squares = gradient * gradient + tiny_eps
    row_total = sum_over(jnp.sum(squares, axis=1), XY, NX * NY)
    new_rows = decay_rate * row_moment + (1.0 - decay_rate) * (row_total / F)
    weighted = jnp.sum(gradient * gradient / new_rows[:, None], axis=0)
    scalars = jnp.stack([jnp.sum(new_rows), weight_sq])
    packed = jnp.concatenate([jnp.sum(squares, axis=0), weighted, jnp.pad(scalars, (0, 126))])
    packed = sum_over(lax.psum(packed.reshape(-1, 128), "c"), "z", NZ).reshape(-1)
    col_total, weighted = packed[:1024], packed[1024:2048]
    row_mean = packed[2048] / D
    new_cols = decay_rate * col_moment + (1.0 - decay_rate) * (col_total / D)
    lanes = jnp.arange(128)
    last = jnp.where(lanes == 0, jnp.sum(weighted / new_cols), jnp.where(lanes == 1, packed[2049], 0.0))
    last = sum_over(last[None], XY, NX * NY)[0]
    update_rms = jnp.sqrt(row_mean * last[0] / (D * F))
    weight_rms = jnp.sqrt(last[1] / (D * F))
    row_factor = jnp.sqrt(row_mean) / jnp.maximum(1.0, update_rms) / jnp.sqrt(new_rows)
    clipped = gradient * row_factor[:, None] * (1.0 / jnp.sqrt(new_cols))[None, :]
    new_weight = weight - step_size * weight_rms * clipped
    return (new_weight, clipped.astype(jnp.bfloat16), new_rows, new_cols)


def solution(mesh):
    fine = Mesh(mesh.devices.reshape(NX, NY, NZ, 2), ("x", "y", "z", "c"))
    return jax.shard_map(
        on_device,
        mesh=fine,
        in_specs=(P(ZC, None), P(ZC, XY), P(ZC, XY), P(ZC), P(XY)),
        out_specs=(P(ZC, XY), P(ZC, XY), P(ZC), P(XY)),
        check_vma=False,
    )
```

time: 413 us -> 220 us (0.53)
  the two profiles are of different devices: /device:TPU:1 before, /device:TPU:32 now
where the time goes in v1:
time: 220 us; the launch traced here: 217 us
  blocking collectives  57.1 us (26%)
  local copies, waits for them, and re-layouts  49.6 us (23%)
  waiting for transfers between devices  33.9 us (15%)
  starting transfers between devices  32.9 us (15%)
  other arithmetic  18.7 us (8%)
  between operations  16.5 us (8%)
  matrix products  8.65 us (4%)
    all_to_all x1, blocking collectives, features_of_rows(): part = lax.all_to_all(part.transpose(1, 0, 2), 'z', 0, 0)  30.4 us
    dynamic_update_slice x6, local copies, waits for them, and re-layouts, gather_ring(): out = lax.dynamic_update_index_in_dim(out, got, lax.rem(me + n - k, n), 0)  23.7 us
    all_to_all x1, blocking collectives, sum_over(): return jnp.sum(lax.all_to_all(copies, axes, 0, 0), axis=0)  23.5 us
    ppermute x6, starting transfers between devices, gather_ring(): got = lax.ppermute(block, axis, shift(n, k))  22.9 us
    ppermute x6, waiting for transfers between devices, gather_ring(): got = lax.ppermute(block, axis, shift(n, k))  17.9 us
    all_to_all x2, waiting for transfers between devices, sum_over(): return jnp.sum(lax.all_to_all(copies, axes, 0, 0), axis=0)  12.2 us
    dot_general x1, matrix products, contract(): lax.dot_general(left, right, (((0,), (0,)), ((), ())), preferred_element_...  8.65 us
    select_n x1, other arithmetic, features_of_rows(): both = jnp.where(c == 0, jnp.stack([own, other]), jnp.stack([other, own]))  8.34 us
  transfers between devices with their start and end apart: 10, of which 5 were waited for; matrix products, arithmetic and copies ran while one was open for 26% of the time, Pallas kernels for 0%

profile of v1, /device:TPU:32, one launch (start us, length us, event | category | flops | bytes accessed | tf_op | source)
XLA Modules:
  0.0 217.4 jit_solution(12759100499605548960)
XLA Ops:
  7.2 0.7 all-gather.2.cloned.1.call-update
  7.9 1.0 copy-done
  9.0 1.3 reshape.56
  10.3 1.4 constant_dynamic-slice_fusion.1
  11.8 30.4 %all_to_all.21 = bf16[16,40,128]{2,1,0:T(8,128)(2,1)S(1)} all-to-all(bf16[16,40,128]{2,1,0:T(8,128)(2,1)S(1)} %bitcast.60), channel_id=1, replica_groups=mesh['x'=4,'y'=4,'z'=16,'c'=2] {'z'}, dimensions={0} | all-to-all | bytes 327680 | tf_op jit(solution)/shard_map/all_to_all | solution.py:48
  42.2 3.3 %collective-permute-start = (bf16[16,40,128]{2,1,0:T(8,128)(2,1)S(1)}, bf16[16,40,128]{2,1,0:T(8,128)(2,1)}, u32[]{:S(2)}, u32[]{:S(2)}) collective-permute-start(bf16[16,40,128]{2,1,0:T(8,128)(2,1)S(1)} %all_to_all.21), channel_id=1, source_target_pairs={{0,128},{128,256},{256,384},{384,0},{1,129},{129,257},{257,385},{3... | collective-permute-start | bytes 491528 | tf_op jit(solution)/shard_map/ppermute | solution.py:32
  45.4 4.7 %collective-permute-start.1 = (bf16[16,40,128]{2,1,0:T(8,128)(2,1)S(1)}, bf16[16,40,128]{2,1,0:T(8,128)(2,1)}, u32[]{:S(2)}, u32[]{:S(2)}) collective-permute-start(bf16[16,40,128]{2,1,0:T(8,128)(2,1)S(1)} %all_to_all.21), channel_id=1, source_target_pairs={{0,256},{128,384},{256,0},{384,128},{1,257},{129,385},{257,1},{385... | collective-permute-start | bytes 491528 | tf_op jit(solution)/shard_map/ppermute | solution.py:32
  50.1 3.3 %collective-permute-start.2 = (bf16[16,40,128]{2,1,0:T(8,128)(2,1)S(1)}, bf16[16,40,128]{2,1,0:T(8,128)(2,1)}, u32[]{:S(2)}, u32[]{:S(2)}) collective-permute-start(bf16[16,40,128]{2,1,0:T(8,128)(2,1)S(1)} %all_to_all.21), channel_id=1, source_target_pairs={{0,384},{128,0},{256,128},{384,256},{1,385},{129,1},{257,129},{385... | collective-permute-start | bytes 491528 | tf_op jit(solution)/shard_map/ppermute | solution.py:32
  53.5 1.0 copy.40
  54.6 6.9 %dynamic_update_slice.26 = bf16[4,16,40,128]{3,0,2,1:T(4,128)(2,1)S(1)} dynamic-update-slice(bf16[4,16,40,128]{3,0,2,1:T(4,128)(2,1)S(1)} %broadcast_in_dim.65, bf16[1,16,40,128]{3,0,2,1:T(2,128)(2,1)} %copy.40, s32[]{:T(128)S(6)} %select_n.63, s32[]{:T(128)} %constant.94.clone.1, s32[]{:T(128)} %constant.94.clone.1, s32[]{:T(128)} %constant.94.clone.1) | dynamic-update-slice | bytes 327684 | tf_op jit(solution)/shard_map/jit(dynamic_update_index_in_dim)/dynamic_update_slice | solution.py:30
  61.6 1.9 copy.41
  63.5 1.9 copy.42
  65.4 1.9 copy.43
  67.3 6.9 %dynamic_update_slice.27 = bf16[4,16,40,128]{3,0,2,1:T(4,128)(2,1)S(1)} dynamic-update-slice(bf16[4,16,40,128]{3,0,2,1:T(4,128)(2,1)S(1)} %dynamic_update_slice.26, bf16[1,16,40,128]{3,0,2,1:T(2,128)(2,1)} %copy.41, s32[]{:T(128)S(6)} %select_n.64, s32[]{:T(128)} %constant.94.clone.1, s32[]{:T(128)} %constant.94.clone.1, s32[]{:T(128)} %constant.94.clone.1) | dynamic-update-slice | bytes 327684 | tf_op jit(solution)/shard_map/jit(dynamic_update_index_in_dim)/dynamic_update_slice | solution.py:33
  74.2 6.9 %dynamic_update_slice.28 = bf16[4,16,40,128]{3,0,2,1:T(4,128)(2,1)S(1)} dynamic-update-slice(bf16[4,16,40,128]{3,0,2,1:T(4,128)(2,1)S(1)} %dynamic_update_slice.27, bf16[1,16,40,128]{3,0,2,1:T(2,128)(2,1)} %copy.42, s32[]{:T(128)S(6)} %select_n.65, s32[]{:T(128)} %constant.94.clone.1, s32[]{:T(128)} %constant.94.clone.1, s32[]{:T(128)} %constant.94.clone.1) | dynamic-update-slice | bytes 327684 | tf_op jit(solution)/shard_map/jit(dynamic_update_index_in_dim)/dynamic_update_slice | solution.py:33
  81.1 6.9 %dynamic_update_slice.29 = bf16[4,16,40,128]{3,0,2,1:T(4,128)(2,1)S(1)} dynamic-update-slice(bf16[4,16,40,128]{3,0,2,1:T(4,128)(2,1)S(1)} %dynamic_update_slice.28, bf16[1,16,40,128]{3,0,2,1:T(2,128)(2,1)} %copy.43, s32[]{:T(128)S(6)} %select_n.66, s32[]{:T(128)} %constant.94.clone.1, s32[]{:T(128)} %constant.94.clone.1, s32[]{:T(128)} %constant.94.clone.1) | dynamic-update-slice | bytes 327684 | tf_op jit(solution)/shard_map/jit(dynamic_update_index_in_dim)/dynamic_update_slice | solution.py:33
  88.0 3.5 %collective-permute-start.3 = (bf16[4,16,40,128]{3,0,2,1:T(4,128)(2,1)S(1)}, bf16[4,16,40,128]{3,0,2,1:T(4,128)(2,1)}, u32[]{:S(2)}, u32[]{:S(2)}) collective-permute-start(bf16[4,16,40,128]{3,0,2,1:T(4,128)(2,1)S(1)} %dynamic_update_slice.29), channel_id=1, source_target_pairs={{0,32},{32,64},{64,96},{96,0},{1,33},{33,65},{65,97},{97,1},{2,34}... | collective-permute-start | bytes 1966088 | tf_op jit(solution)/shard_map/ppermute | solution.py:32
  91.6 4.7 %collective-permute-start.4 = (bf16[4,16,40,128]{3,0,2,1:T(4,128)(2,1)S(1)}, bf16[4,16,40,128]{3,0,2,1:T(4,128)(2,1)}, u32[]{:S(2)}, u32[]{:S(2)}) collective-permute-start(bf16[4,16,40,128]{3,0,2,1:T(4,128)(2,1)S(1)} %dynamic_update_slice.29), channel_id=1, source_target_pairs={{0,64},{32,96},{64,0},{96,32},{1,65},{33,97},{65,1},{97,33},{2,66}... | collective-permute-start | bytes 1966088 | tf_op jit(solution)/shard_map/ppermute | solution.py:32
  96.3 3.3 %collective-permute-start.5 = (bf16[4,16,40,128]{3,0,2,1:T(4,128)(2,1)S(1)}, bf16[4,16,40,128]{3,0,2,1:T(4,128)(2,1)S(1)}, u32[]{:S(2)}, u32[]{:S(2)}) collective-permute-start(bf16[4,16,40,128]{3,0,2,1:T(4,128)(2,1)S(1)} %dynamic_update_slice.29), channel_id=1, source_target_pairs={{0,96},{32,0},{64,32},{96,64},{1,97},{33,1},{65,33},{97,65},{2,98}... | collective-permute-start | bytes 1966088 | tf_op jit(solution)/shard_map/ppermute | solution.py:32
  99.6 1.0 broadcast_in_dim.64
  100.7 0.3 bitcast_dynamic-update-slice_fusion.2
  100.9 6.8 %collective-permute-done.3 = bf16[4,16,40,128]{3,0,2,1:T(4,128)(2,1)} collective-permute-done((bf16[4,16,40,128]{3,0,2,1:T(4,128)(2,1)S(1)}, bf16[4,16,40,128]{3,0,2,1:T(4,128)(2,1)}, u32[]{:S(2)}, u32[]{:S(2)}) %collective-permute-start.3) | collective-permute-done | bytes 655392 | tf_op jit(solution)/shard_map/ppermute | solution.py:32
  107.7 1.4 bitcast_dynamic-update-slice_fusion.1
  109.1 11.0 %collective-permute-done.4 = bf16[4,16,40,128]{3,0,2,1:T(4,128)(2,1)} collective-permute-done((bf16[4,16,40,128]{3,0,2,1:T(4,128)(2,1)S(1)}, bf16[4,16,40,128]{3,0,2,1:T(4,128)(2,1)}, u32[]{:S(2)}, u32[]{:S(2)}) %collective-permute-start.4) | collective-permute-done | bytes 655392 | tf_op jit(solution)/shard_map/ppermute | solution.py:32
  120.2 1.4 bitcast_dynamic-update-slice_fusion
  121.5 0.3 bitcast_dynamic-update-slice_fusion.3
  121.8 4.6 %dynamic-slice_bitcast_fusion = (bf16[1,4,2,16,40,128]{5,2,4,1,0,3:T(2,128)(2,1)}, bf16[4,2,16,40,128]{4,1,3,0,2:T(2,128)(2,1)}) fusion(bf16[4,4,16,40,128]{4,1,3,0,2:T(4,128)(2,1)S(1)} %bitcast_dynamic-update-slice_fusion.3, s32[]{:T(128)S(6)} %select_n.71, s32[]{:T(128)S(6)} %select_n.72), kind=kLoop, calls=%fused_computation.4 | loop fusion | bytes 5242888 | tf_op jit(solution)/shard_map/stack | solution.py:54
  126.4 2.1 collective-permute-start.6
  128.5 3.2 %collective-permute-done.6 = bf16[4,2,16,40,128]{4,1,3,0,2:T(2,128)(2,1)} collective-permute-done((bf16[4,2,16,40,128]{4,1,3,0,2:T(2,128)(2,1)}, bf16[4,2,16,40,128]{4,1,3,0,2:T(2,128)(2,1)}, u32[]{:S(2)}, u32[]{:S(2)}) %collective-permute-start.6) | collective-permute-done | bytes 1310752 | tf_op jit(solution)/shard_map/ppermute | solution.py:53
  131.7 8.3 %broadcast_select_fusion = bf16[2,4,2,16,40,128]{5,2,4,1,0,3:T(2,128)(2,1)} fusion(pred[]{:T(512)S(6)} %eq.25, bf16[1,4,2,16,40,128]{5,2,4,1,0,3:T(2,128)(2,1)} %bitcast.13, bf16[1,4,2,16,40,128]{5,2,4,1,0,3:T(2,128)(2,1)} %get-tuple-element.10), kind=kLoop, calls=%fused_computation | loop fusion | flops 3932160 | bytes 5242881 | tf_op jit(solution)/shard_map/jit(_where)/select_n | solution.py:54
  140.0 8.6 %add_reduce_fusion = (f32[256]{0:T(256)S(1)}, f32[256,1024]{1,0:T(8,128)}) fusion(bf16[5120,1024]{1,0:T(8,128)(2,1)} %all-gather.2.cloned.1.call-done, bf16[640,8,2,128]{3,2,1,0:T(2,128)(2,1)} %bitcast.58), kind=kOutput, calls=%fused_computation.9 | convolution fusion | flops 2685140736 | bytes 14156800 | tf_op jit(solution)/shard_map/dot_general | solution.py:18
  148.6 0.6 broadcast_in_dim.74
  149.3 4.4 %all-to-all-start.1 = ((f32[16,1,256]{2,1,0:T(1,128)}), f32[16,1,256]{2,1,0:T(1,128)S(1)}, u32[]{:S(2)}, u32[]{:S(2)}) async-start(f32[16,1,256]{2,1,0:T(1,128)} %broadcast_in_dim.74), calls=%async_computation.1 | async-start | bytes 32768 | tf_op jit(solution)/shard_map/all_to_all | solution.py:39
  153.7 2.1 multiply_reduce_fusion
  155.8 5.5 %all-to-all-done.1 = f32[16,1,256]{2,1,0:T(1,128)S(1)} async-done(((f32[16,1,256]{2,1,0:T(1,128)}), f32[16,1,256]{2,1,0:T(1,128)S(1)}, u32[]{:S(2)}, u32[]{:S(2)}) %all-to-all-start.1) | async-done | bytes 16416 | tf_op jit(solution)/shard_map/all_to_all | solution.py:39
  161.3 0.6 fusion.10
  161.9 1.4 add_reduce_fusion.1
  163.4 1.4 fusion.8
  164.7 3.3 %psum.7 = f32[17,128]{1,0:T(8,128)S(1)} all-reduce(f32[17,128]{1,0:T(8,128)S(1)} %maximum_bitcast_fusion), channel_id=1, replica_groups=mesh['x'=4,'y'=4,'z'=16,'c'=2] {'c'}, use_global_device_ids=true, to_apply=%region_6.7 | all-reduce | flops 2176 | bytes 17408 | tf_op jit(solution)/shard_map/psum | solution.py:70
  168.0 23.5 %all_to_all.22 = f32[16,17,128]{2,1,0:T(8,128)S(1)} all-to-all(f32[16,17,128]{2,1,0:T(8,128)S(1)} %broadcast_in_dim.75), channel_id=1, replica_groups=mesh['x'=4,'y'=4,'z'=16,'c'=2] {'z'}, dimensions={0} | all-to-all | bytes 278528 | tf_op jit(solution)/shard_map/all_to_all | solution.py:39
  191.6 0.6 fusion.7
  192.2 0.6 fusion.11
  192.8 1.2 compare_select_fusion.1
  194.0 0.6 broadcast_in_dim.79
  194.6 3.5 %all-to-all-start.3 = ((f32[16,1,128]{2,1,0:T(1,128)}), f32[16,1,128]{2,1,0:T(1,128)S(1)}, u32[]{:S(2)}, u32[]{:S(2)}) async-start(f32[16,1,128]{2,1,0:T(1,128)} %broadcast_in_dim.79), calls=%async_computation.3 | async-start | bytes 16384 | tf_op jit(solution)/shard_map/all_to_all | solution.py:39
  198.8 6.7 %all-to-all-done.3 = f32[16,1,128]{2,1,0:T(1,128)S(1)} async-done(((f32[16,1,128]{2,1,0:T(1,128)}), f32[16,1,128]{2,1,0:T(1,128)S(1)}, u32[]{:S(2)}, u32[]{:S(2)}) %all-to-all-start.3) | async-done | bytes 8224 | tf_op jit(solution)/shard_map/all_to_all | solution.py:39
  205.5 0.6 fusion.12
  207.6 2.9 %fusion.3 = (bf16[256,1024]{1,0:T(8,128)(2,1)}, f32[256,1024]{1,0:T(8,128)}) fusion(f32[256,1024]{1,0:T(8,128)} %get-tuple-element.19, f32[1024]{0:T(1024)S(1)} %sqrt.20, f32[256]{0:T(256)S(1)} %rsqrt_multiply_fusion, f32[256,1024]{1,0:T(8,128)} %param.7, f32[]{:T(128)} %bitcast.24), kind=kLoop, calls=%fused_computation.11 | loop fusion | flops 1310720 | bytes 3675140 | tf_op jit(solution)/shard_map/convert_element_type | solution.py:82
  (25 shorter events, 0.5 us)
Async XLA Ops:
  7.2 1.7 copy-start
  7.2 132.8 %all-gather.2.cloned.1.call-start = ((), (), s32[]{:S(2)}) async-start(), calls=%async_computation.4 | async-start | bytes 10813440 | tf_op jit(solution)/shard_map/all_gather | solution.py:60
  42.2 19.4 %collective-permute-start = (bf16[16,40,128]{2,1,0:T(8,128)(2,1)S(1)}, bf16[16,40,128]{2,1,0:T(8,128)(2,1)}, u32[]{:S(2)}, u32[]{:S(2)}) collective-permute-start(bf16[16,40,128]{2,1,0:T(8,128)(2,1)S(1)} %all_to_all.21), channel_id=1, source_target_pairs={{0,128},{128,256},{256,384},{384,0},{1,129},{129,257},{257,385},{3... | collective-permute-start | bytes 491528 | tf_op jit(solution)/shard_map/ppermute | solution.py:32
  45.4 18.0 %collective-permute-start.1 = (bf16[16,40,128]{2,1,0:T(8,128)(2,1)S(1)}, bf16[16,40,128]{2,1,0:T(8,128)(2,1)}, u32[]{:S(2)}, u32[]{:S(2)}) collective-permute-start(bf16[16,40,128]{2,1,0:T(8,128)(2,1)S(1)} %all_to_all.21), channel_id=1, source_target_pairs={{0,256},{128,384},{256,0},{384,128},{1,257},{129,385},{257,1},{385... | collective-permute-start | bytes 491528 | tf_op jit(solution)/shard_map/ppermute | solution.py:32
  50.1 15.2 %collective-permute-start.2 = (bf16[16,40,128]{2,1,0:T(8,128)(2,1)S(1)}, bf16[16,40,128]{2,1,0:T(8,128)(2,1)}, u32[]{:S(2)}, u32[]{:S(2)}) collective-permute-start(bf16[16,40,128]{2,1,0:T(8,128)(2,1)S(1)} %all_to_all.21), channel_id=1, source_target_pairs={{0,384},{128,0},{256,128},{384,256},{1,385},{129,1},{257,129},{385... | collective-permute-start | bytes 491528 | tf_op jit(solution)/shard_map/ppermute | solution.py:32
  88.0 19.7 %collective-permute-start.3 = (bf16[4,16,40,128]{3,0,2,1:T(4,128)(2,1)S(1)}, bf16[4,16,40,128]{3,0,2,1:T(4,128)(2,1)}, u32[]{:S(2)}, u32[]{:S(2)}) collective-permute-start(bf16[4,16,40,128]{3,0,2,1:T(4,128)(2,1)S(1)} %dynamic_update_slice.29), channel_id=1, source_target_pairs={{0,32},{32,64},{64,96},{96,0},{1,33},{33,65},{65,97},{97,1},{2,34}... | collective-permute-start | bytes 1966088 | tf_op jit(solution)/shard_map/ppermute | solution.py:32
  91.6 28.6 %collective-permute-start.4 = (bf16[4,16,40,128]{3,0,2,1:T(4,128)(2,1)S(1)}, bf16[4,16,40,128]{3,0,2,1:T(4,128)(2,1)}, u32[]{:S(2)}, u32[]{:S(2)}) collective-permute-start(bf16[4,16,40,128]{3,0,2,1:T(4,128)(2,1)S(1)} %dynamic_update_slice.29), channel_id=1, source_target_pairs={{0,64},{32,96},{64,0},{96,32},{1,65},{33,97},{65,1},{97,33},{2,66}... | collective-permute-start | bytes 1966088 | tf_op jit(solution)/shard_map/ppermute | solution.py:32
  96.3 25.2 %collective-permute-start.5 = (bf16[4,16,40,128]{3,0,2,1:T(4,128)(2,1)S(1)}, bf16[4,16,40,128]{3,0,2,1:T(4,128)(2,1)S(1)}, u32[]{:S(2)}, u32[]{:S(2)}) collective-permute-start(bf16[4,16,40,128]{3,0,2,1:T(4,128)(2,1)S(1)} %dynamic_update_slice.29), channel_id=1, source_target_pairs={{0,96},{32,0},{64,32},{96,64},{1,97},{33,1},{65,33},{97,65},{2,98}... | collective-permute-start | bytes 1966088 | tf_op jit(solution)/shard_map/ppermute | solution.py:32
  126.4 5.3 %collective-permute-start.6 = (bf16[4,2,16,40,128]{4,1,3,0,2:T(2,128)(2,1)}, bf16[4,2,16,40,128]{4,1,3,0,2:T(2,128)(2,1)}, u32[]{:S(2)}, u32[]{:S(2)}) collective-permute-start(bf16[4,2,16,40,128]{4,1,3,0,2:T(2,128)(2,1)} %get-tuple-element.11), channel_id=1, source_target_pairs={{0,1},{1,0},{2,3},{3,2},{4,5},{5,4},{6,7},{7,6},{8,9},{9,8},{10,11... | collective-permute-start | bytes 3932168 | tf_op jit(solution)/shard_map/ppermute | solution.py:53
  140.0 21.3 %copy-start.4 = (f32[256]{0:T(256)S(1)}, f32[256]{0:T(256)}, u32[]{:S(2)}) copy-start(f32[256]{0:T(256)} %param.8) | copy-start | bytes 3076
  148.6 42.9 %copy-start.3 = (f32[1024]{0:T(1024)S(1)}, f32[1024]{0:T(1024)}, u32[]{:S(2)}) copy-start(f32[1024]{0:T(1024)} %param.9) | copy-start | bytes 12292
  149.3 12.0 %all-to-all-start.1 = ((f32[16,1,256]{2,1,0:T(1,128)}), f32[16,1,256]{2,1,0:T(1,128)S(1)}, u32[]{:S(2)}, u32[]{:S(2)}) async-start(f32[16,1,256]{2,1,0:T(1,128)} %broadcast_in_dim.74), calls=%async_computation.1 | async-start | bytes 32768 | tf_op jit(solution)/shard_map/all_to_all | solution.py:39
  161.9 48.6 %copy-start.2 = (f32[256]{0:T(256)}, f32[256]{0:T(256)S(1)}, u32[]{:S(2)}) copy-start(f32[256]{0:T(256)S(1)} %get-tuple-element.9) | copy-start | bytes 3076
  192.2 18.3 %copy-start.1 = (f32[1024]{0:T(1024)}, f32[1024]{0:T(1024)S(1)}, u32[]{:S(2)}) copy-start(f32[1024]{0:T(1024)S(1)} %get-tuple-element.7) | copy-start | bytes 12292
  194.6 10.9 %all-to-all-start.3 = ((f32[16,1,128]{2,1,0:T(1,128)}), f32[16,1,128]{2,1,0:T(1,128)S(1)}, u32[]{:S(2)}, u32[]{:S(2)}) async-start(f32[16,1,128]{2,1,0:T(1,128)} %broadcast_in_dim.79), calls=%async_computation.3 | async-start | bytes 16384 | tf_op jit(solution)/shard_map/all_to_all | solution.py:39
Sparse Core Ops, SparseCore 0:
  10.1 88.0 all-gather.1

commit v2 on v1

v2 whole, which is shorter than its diff:
```python
import jax
import jax.numpy as jnp
from jax import lax
from jax.sharding import Mesh, PartitionSpec as P

D = 8192
F = 16384

decay_rate = 1.0 - 10.0 ** (-0.8)
step_size = 0.05
tiny_eps = 1e-30

NX, NY, NZ = 4, 4, 16
XY, ZC = ("x", "y"), ("z", "c")


def contract(left, right):
    return lax.dot_general(
        left, right, (((0,), (0,)), ((), ())), preferred_element_type=jnp.float32
    )


def shift(n, k):
    return [(i, (i + k) % n) for i in range(n)]


def sum_over(value, axes, n):
    copies = jnp.broadcast_to(value[None], (n,) + value.shape)
    return jnp.sum(lax.all_to_all(copies, axes, 0, 0), axis=0)


def features_of_rows(inputs):
    x, y, c = lax.axis_index("x"), lax.axis_index("y"), lax.axis_index("c")
    tokens = inputs.shape[0] // NY
    part = lax.dynamic_slice_in_dim(inputs, y * tokens, tokens, 0)
    part = part.reshape(tokens, NZ, NX, 128)
    part = lax.dynamic_index_in_dim(part, x, 2, keepdims=False)
    part = lax.all_to_all(part.transpose(1, 0, 2), "z", 0, 0)
    part = lax.all_gather(part, "x", axis=0)
    low, high = part[:2], part[2:]
    own = jnp.where(c == 0, low, high)
    other = lax.ppermute(jnp.where(c == 0, high, low), "c", shift(2, 1))
    first, second = jnp.where(c == 0, own, other), jnp.where(c == 0, other, own)
    both = jnp.stack([first, second]).transpose(2, 0, 3, 1, 4)
    both = both.reshape(NZ, 2, tokens, 256)
    groups = [both] + [lax.ppermute(both, "y", shift(NY, k)) for k in range(1, NY)]
    return jnp.concatenate(groups, axis=2).reshape(NZ * 2 * NY * tokens, 256)


def rotated(cotangent):
    y = lax.axis_index("y")
    groups = cotangent.reshape(NY, -1, cotangent.shape[1])
    backward = jnp.concatenate([groups[::-1], groups[::-1][:3]])
    return lax.dynamic_slice_in_dim(backward, 3 - y, NY, 0).reshape(cotangent.shape)


def on_device(inputs, cotangent, weight, row_moment, col_moment):
    c = lax.axis_index("c")
    all_cotangent = lax.all_gather(rotated(cotangent), ZC, axis=0, tiled=True)
    feat_rows = features_of_rows(inputs)
    weight_sq = jnp.sum(weight * weight)
    gradient = contract(feat_rows, all_cotangent)
    squares = gradient * gradient + tiny_eps
    row_total = sum_over(jnp.sum(squares, axis=1)[None], XY, NX * NY)[0]
    new_rows = decay_rate * row_moment + (1.0 - decay_rate) * (row_total / F)
    weighted = jnp.sum(gradient * gradient / new_rows[:, None], axis=0)
    scalars = jnp.pad(jnp.stack([jnp.sum(new_rows), weight_sq]), (0, 126))
    columns = jnp.stack([jnp.sum(squares, axis=0), weighted])
    columns = columns.reshape(2, 2, 512).transpose(1, 0, 2).reshape(2, 1024)
    packed = jnp.concatenate([columns, jnp.stack([scalars, scalars])], axis=1)
    packed = lax.dynamic_slice_in_dim(lax.psum(packed, "c"), c, 1, 0)
    packed = sum_over(packed, "z", NZ)[0]
    row_mean = packed[1024] / D
    half_moment = lax.dynamic_slice_in_dim(col_moment, c * 512, 512, 0)
    half_cols = decay_rate * half_moment + (1.0 - decay_rate) * (packed[:512] / D)
    new_cols = lax.all_gather(half_cols, "c", axis=0, tiled=True)
    lanes = jnp.arange(128)
    scaled_sq = row_mean * jnp.sum(packed[512:1024] / half_cols)
    last = jnp.where(lanes == 0, scaled_sq, jnp.where(lanes == 1, 0.5 * packed[1025], 0.0))
    last = sum_over(last[None], ("x", "y", "c"), NX * NY * 2)[0]
    update_rms = jnp.sqrt(last[0] / (D * F))
    weight_rms = jnp.sqrt(last[1] / (D * F))
    row_factor = jnp.sqrt(row_mean) / jnp.maximum(1.0, update_rms) / jnp.sqrt(new_rows)
    clipped = gradient * row_factor[:, None] * (1.0 / jnp.sqrt(new_cols))[None, :]
    new_weight = weight - step_size * weight_rms * clipped
    return (new_weight, clipped.astype(jnp.bfloat16), new_rows, new_cols)


def solution(mesh):
    fine = Mesh(mesh.devices.reshape(NX, NY, NZ, 2), ("x", "y", "z", "c"))
    return jax.shard_map(
        on_device,
        mesh=fine,
        in_specs=(P(ZC, None), P(ZC, XY), P(ZC, XY), P(ZC), P(XY)),
        out_specs=(P(ZC, XY), P(ZC, XY), P(ZC), P(XY)),
        check_vma=False,
    )
```

time: 220 us -> 183 us (0.83)
  the two profiles are of different devices: /device:TPU:32 before, /device:TPU:1 now
where the time goes in v2:
time: 183 us; the launch traced here: 182 us
  waiting for transfers between devices  59.4 us (32%)
  starting transfers between devices  51.8 us (28%)
  blocking collectives  18.8 us (10%)
  between operations  17.7 us (10%)
  other arithmetic  14.2 us (8%)
  local copies, waits for them, and re-layouts  12 us (7%)
  matrix products  8.67 us (5%)
    ppermute x3, waiting for transfers between devices, features_of_rows(): lax.ppermute(both, 'y', shift(NY, k))  24.7 us
    all_to_all x3, waiting for transfers between devices, sum_over(): return jnp.sum(lax.all_to_all(copies, axes, 0, 0), axis=0)  21.2 us
    all_to_all x3, starting transfers between devices, sum_over(): return jnp.sum(lax.all_to_all(copies, axes, 0, 0), axis=0)  16.2 us
    all_to_all x1, starting transfers between devices, features_of_rows(): part = lax.all_to_all(part.transpose(1, 0, 2), 'z', 0, 0)  15.7 us
    all_gather x1, blocking collectives, features_of_rows(): part = lax.all_gather(part, 'x', axis=0)  12.4 us
    all_to_all x1, waiting for transfers between devices, features_of_rows(): part = lax.all_to_all(part.transpose(1, 0, 2), 'z', 0, 0)  12.2 us
    ppermute x3, starting transfers between devices, features_of_rows(): lax.ppermute(both, 'y', shift(NY, k))  10.7 us
    ppermute x1, starting transfers between devices, features_of_rows(): other = lax.ppermute(jnp.where(c == 0, high, low), 'c', shift(2, 1))  9.05 us
  transfers between devices with their start and end apart: 9, of which 8 were waited for; matrix products, arithmetic and copies ran while one was open for 7% of the time, Pallas kernels for 0%

profile of v2, /device:TPU:1, one launch (start us, length us, event | category | flops | bytes accessed | tf_op | source)
XLA Modules:
  0.0 182.5 jit_solution(12611383159090596369)
XLA Ops:
  7.2 0.0 copy-start
  7.2 0.0 all-gather.4.cloned.1.call-start
  7.2 1.1 slice.43
  8.4 1.0 rev.4
  9.4 0.8 fusion.1
  10.2 0.0 all-gather.4.cloned.1.call-update
  10.3 0.1 constant_dynamic-slice_fusion.1
  10.3 1.3 reshape.81
  11.6 1.4 constant_dynamic-slice_fusion
  13.1 0.8 copy.47
  13.8 15.7 %all-to-all-start = ((bf16[16,40,128]{2,1,0:T(8,128)(2,1)}), bf16[16,40,128]{2,1,0:T(8,128)(2,1)S(1)}, u32[]{:S(2)}, u32[]{:S(2)}) async-start(bf16[16,40,128]{2,1,0:T(8,128)(2,1)} %bitcast.38), calls=%async_computation | async-start | bytes 327680 | tf_op jit(solution)/shard_map/all_to_all | solution.py:38
  29.6 12.2 %all-to-all-done = bf16[16,40,128]{2,1,0:T(8,128)(2,1)S(1)} async-done(((bf16[16,40,128]{2,1,0:T(8,128)(2,1)}), bf16[16,40,128]{2,1,0:T(8,128)(2,1)S(1)}, u32[]{:S(2)}, u32[]{:S(2)}) %all-to-all-start) | async-done | bytes 163872 | tf_op jit(solution)/shard_map/all_to_all | solution.py:38
  41.8 12.4 %all-gather = bf16[64,40,128]{2,1,0:T(8,128)(2,1)S(1)} all-gather(bf16[16,40,128]{2,1,0:T(8,128)(2,1)S(1)} %all-to-all-done), channel_id=2, replica_groups=mesh['x'=4,'y'=4,'z'=16,'c'=2] {'x'}, dimensions={0}, use_global_device_ids=true | all-gather | bytes 819200 | tf_op jit(solution)/shard_map/all_gather | solution.py:39
  54.3 0.3 copy.33
  54.6 9.1 %collective-permute-start = (bf16[2,16,40,128]{3,0,2,1:T(2,128)(2,1)S(1)}, bf16[2,16,40,128]{3,0,2,1:T(2,128)(2,1)S(1)}, u32[]{:S(2)}, u32[]{:S(2)}) collective-permute-start(bf16[2,16,40,128]{3,0,2,1:T(2,128)(2,1)S(1)} %copy.33), channel_id=1, source_target_pairs={{0,1},{1,0},{2,3},{3,2},{4,5},{5,4},{6,7},{7,6},{8,9},{9,8},{10,11... | collective-permute-start | bytes 983048 | tf_op jit(solution)/shard_map/ppermute | solution.py:42
  63.7 1.2 collective-permute-done
  64.9 0.7 fusion.2
  65.6 1.7 maximum_bitcast_fusion
  67.3 2.2 %reshape.82 = bf16[16,2,40,256]{3,2,1,0:T(8,128)(2,1)S(1)} reshape(bf16[16,2,40,2,128]{4,3,2,1,0:T(2,128)(2,1)} %maximum_bitcast_fusion) | data formatting | bytes 1310720 | tf_op jit(solution)/shard_map/reshape | solution.py:45
  69.5 3.2 %collective-permute-start.1 = (bf16[16,2,40,256]{3,2,1,0:T(8,128)(2,1)S(1)}, bf16[16,2,40,256]{3,2,1,0:T(8,128)(2,1)S(1)}, u32[]{:S(2)}, u32[]{:S(2)}) collective-permute-start(bf16[16,2,40,256]{3,2,1,0:T(8,128)(2,1)S(1)} %reshape.82), channel_id=1, source_target_pairs={{0,32},{32,64},{64,96},{96,0},{1,33},{33,65},{65,97},{97,1},{2,34}... | collective-permute-start | bytes 1966088 | tf_op jit(solution)/shard_map/ppermute | solution.py:46
  72.7 4.5 %collective-permute-start.2 = (bf16[16,2,40,256]{3,2,1,0:T(8,128)(2,1)S(1)}, bf16[16,2,40,256]{3,2,1,0:T(8,128)(2,1)S(1)}, u32[]{:S(2)}, u32[]{:S(2)}) collective-permute-start(bf16[16,2,40,256]{3,2,1,0:T(8,128)(2,1)S(1)} %reshape.82), channel_id=1, source_target_pairs={{0,64},{32,96},{64,0},{96,32},{1,65},{33,97},{65,1},{97,33},{2,66}... | collective-permute-start | bytes 1966088 | tf_op jit(solution)/shard_map/ppermute | solution.py:46
  77.3 3.0 %collective-permute-start.3 = (bf16[16,2,40,256]{3,2,1,0:T(8,128)(2,1)S(1)}, bf16[16,2,40,256]{3,2,1,0:T(8,128)(2,1)S(1)}, u32[]{:S(2)}, u32[]{:S(2)}) collective-permute-start(bf16[16,2,40,256]{3,2,1,0:T(8,128)(2,1)S(1)} %reshape.82), channel_id=1, source_target_pairs={{0,96},{32,0},{64,32},{96,64},{1,97},{33,1},{65,33},{97,65},{2,98}... | collective-permute-start | bytes 1966088 | tf_op jit(solution)/shard_map/ppermute | solution.py:46
  80.3 8.6 %collective-permute-done.1 = bf16[16,2,40,256]{3,2,1,0:T(8,128)(2,1)S(1)} collective-permute-done((bf16[16,2,40,256]{3,2,1,0:T(8,128)(2,1)S(1)}, bf16[16,2,40,256]{3,2,1,0:T(8,128)(2,1)S(1)}, u32[]{:S(2)}, u32[]{:S(2)}) %collective-permute-start.1) | collective-permute-done | bytes 655392 | tf_op jit(solution)/shard_map/ppermute | solution.py:46
  88.8 15.0 %collective-permute-done.2 = bf16[16,2,40,256]{3,2,1,0:T(8,128)(2,1)S(1)} collective-permute-done((bf16[16,2,40,256]{3,2,1,0:T(8,128)(2,1)S(1)}, bf16[16,2,40,256]{3,2,1,0:T(8,128)(2,1)S(1)}, u32[]{:S(2)}, u32[]{:S(2)}) %collective-permute-start.2) | collective-permute-done | bytes 655392 | tf_op jit(solution)/shard_map/ppermute | solution.py:46
  103.8 1.1 collective-permute-done.3
  105.0 1.6 pad_maximum_fusion
  106.6 8.7 %add_reduce_fusion = (f32[256]{0:T(256)S(1)}, f32[256,1024]{1,0:T(8,128)}) fusion(bf16[5120,256]{1,0:T(8,128)(2,1)} %bitcast.39, bf16[5120,1024]{1,0:T(8,128)(2,1)} %all-gather.4.cloned.1.call-done), kind=kOutput, calls=%fused_computation.5 | convolution fusion | flops 2685140736 | bytes 14156800 | tf_op jit(solution)/shard_map/dot_general | solution.py:18
  115.3 0.6 broadcast_in_dim.33
  115.9 6.5 %all-to-all-start.1 = ((f32[16,1,256]{2,1,0:T(1,128)}), f32[16,1,256]{2,1,0:T(1,128)S(1)}, u32[]{:S(2)}, u32[]{:S(2)}) async-start(f32[16,1,256]{2,1,0:T(1,128)} %broadcast_in_dim.33), calls=%async_computation.1 | async-start | bytes 32768 | tf_op jit(solution)/shard_map/all_to_all | solution.py:29
  122.4 2.1 %multiply_reduce_fusion = f32[]{:T(128)} fusion(f32[256,1024]{1,0:T(8,128)} %param.7), kind=kLoop, calls=%fused_computation.3 | loop fusion | flops 524287 | bytes 1048580 | tf_op jit(solution)/shard_map/reduce_sum | solution.py:61
  124.5 4.3 %all-to-all-done.1 = f32[16,1,256]{2,1,0:T(1,128)S(1)} async-done(((f32[16,1,256]{2,1,0:T(1,128)}), f32[16,1,256]{2,1,0:T(1,128)S(1)}, u32[]{:S(2)}, u32[]{:S(2)}) %all-to-all-start.1) | async-done | bytes 16416 | tf_op jit(solution)/shard_map/all_to_all | solution.py:29
  128.9 0.6 fusion.6
  129.5 1.4 add_reduce_fusion.1
  131.0 1.4 fusion.5
  132.4 4.6 %psum.7 = f32[2,1152]{1,0:T(2,128)S(1)} all-reduce(f32[2,1152]{1,0:T(2,128)S(1)} %maximum_maximum_fusion), channel_id=1, replica_groups=mesh['x'=4,'y'=4,'z'=16,'c'=2] {'c'}, use_global_device_ids=true, to_apply=%region_6.7 | all-reduce | flops 2304 | bytes 18432 | tf_op jit(solution)/shard_map/psum | solution.py:71
  137.0 0.7 broadcast_in_dim.35
  137.7 4.2 %all-to-all-start.2 = ((f32[16,1,1152]{2,1,0:T(1,128)}), f32[16,1,1152]{2,1,0:T(1,128)S(1)}, u32[]{:S(2)}, u32[]{:S(2)}) async-start(f32[16,1,1152]{2,1,0:T(1,128)} %broadcast_in_dim.35), calls=%async_computation.2 | async-start | bytes 147456 | tf_op jit(solution)/shard_map/all_to_all | solution.py:29
  141.9 11.7 %all-to-all-done.2 = f32[16,1,1152]{2,1,0:T(1,128)S(1)} async-done(((f32[16,1,1152]{2,1,0:T(1,128)}), f32[16,1,1152]{2,1,0:T(1,128)S(1)}, u32[]{:S(2)}, u32[]{:S(2)}) %all-to-all-start.2) | async-done | bytes 73760 | tf_op jit(solution)/shard_map/all_to_all | solution.py:29
  153.6 0.1 reduce_sum.91
  153.7 0.6 fusion.7
  155.0 0.7 divide_reduce_fusion.1
  157.0 0.6 broadcast_in_dim.39
  157.6 5.5 %all-to-all-start.3 = ((f32[32,1,128]{2,1,0:T(1,128)}), f32[32,1,128]{2,1,0:T(1,128)S(1)}, u32[]{:S(2)}, u32[]{:S(2)}) async-start(f32[32,1,128]{2,1,0:T(1,128)} %broadcast_in_dim.39), calls=%async_computation.3 | async-start | bytes 32768 | tf_op jit(solution)/shard_map/all_to_all | solution.py:29
  163.1 1.8 %all-gather.1 = f32[2,1,512]{2,1,0:T(1,128)S(1)} all-gather(f32[1,1,512]{2,1,0:T(1,128)S(1)} %bitcast.49), channel_id=1, replica_groups=mesh['x'=4,'y'=4,'z'=16,'c'=2] {'c'}, dimensions={0}, use_global_device_ids=true | all-gather | bytes 6144 | tf_op jit(solution)/shard_map/all_gather | solution.py:76
  164.9 5.1 %all-to-all-done.3 = f32[32,1,128]{2,1,0:T(1,128)S(1)} async-done(((f32[32,1,128]{2,1,0:T(1,128)}), f32[32,1,128]{2,1,0:T(1,128)S(1)}, u32[]{:S(2)}, u32[]{:S(2)}) %all-to-all-start.3) | async-done | bytes 16416 | tf_op jit(solution)/shard_map/all_to_all | solution.py:29
  170.1 0.6 fusion.8
  172.1 2.9 %fusion = (bf16[256,1024]{1,0:T(8,128)(2,1)}, f32[256,1024]{1,0:T(8,128)}) fusion(f32[256,1024]{1,0:T(8,128)} %get-tuple-element.23, f32[1024]{0:T(1024)S(1)} %sqrt.21, f32[256]{0:T(256)S(1)} %rsqrt_multiply_fusion, f32[256,1024]{1,0:T(8,128)} %param.7, f32[]{:T(128)} %bitcast.22), kind=kLoop, calls=%fused_computation.7 | loop fusion | flops 1310720 | bytes 3675140 | tf_op jit(solution)/shard_map/convert_element_type | solution.py:86
  175.0 0.6 copy.49
  (22 shorter events, 0.2 us)
Async XLA Ops:
  7.2 3.1 %copy-start = (bf16[160,8192]{1,0:T(8,128)(2,1)S(1)}, bf16[160,8192]{1,0:T(8,128)(2,1)}, u32[]{:S(2)}) copy-start(bf16[160,8192]{1,0:T(8,128)(2,1)} %param.5) | copy-start | bytes 7864324
  7.2 99.4 %all-gather.4.cloned.1.call-start = ((), (), s32[]{:S(2)}) async-start(), calls=%async_computation.4 | async-start | bytes 10813440 | tf_op jit(solution)/shard_map/all_gather | solution.py:59
  13.8 28.0 %all-to-all-start = ((bf16[16,40,128]{2,1,0:T(8,128)(2,1)}), bf16[16,40,128]{2,1,0:T(8,128)(2,1)S(1)}, u32[]{:S(2)}, u32[]{:S(2)}) async-start(bf16[16,40,128]{2,1,0:T(8,128)(2,1)} %bitcast.38), calls=%async_computation | async-start | bytes 327680 | tf_op jit(solution)/shard_map/all_to_all | solution.py:38
  54.6 10.3 %collective-permute-start = (bf16[2,16,40,128]{3,0,2,1:T(2,128)(2,1)S(1)}, bf16[2,16,40,128]{3,0,2,1:T(2,128)(2,1)S(1)}, u32[]{:S(2)}, u32[]{:S(2)}) collective-permute-start(bf16[2,16,40,128]{3,0,2,1:T(2,128)(2,1)S(1)} %copy.33), channel_id=1, source_target_pairs={{0,1},{1,0},{2,3},{3,2},{4,5},{5,4},{6,7},{7,6},{8,9},{9,8},{10,11... | collective-permute-start | bytes 983048 | tf_op jit(solution)/shard_map/ppermute | solution.py:42
  69.5 19.3 %collective-permute-start.1 = (bf16[16,2,40,256]{3,2,1,0:T(8,128)(2,1)S(1)}, bf16[16,2,40,256]{3,2,1,0:T(8,128)(2,1)S(1)}, u32[]{:S(2)}, u32[]{:S(2)}) collective-permute-start(bf16[16,2,40,256]{3,2,1,0:T(8,128)(2,1)S(1)} %reshape.82), channel_id=1, source_target_pairs={{0,32},{32,64},{64,96},{96,0},{1,33},{33,65},{65,97},{97,1},{2,34}... | collective-permute-start | bytes 1966088 | tf_op jit(solution)/shard_map/ppermute | solution.py:46
  72.7 31.1 %collective-permute-start.2 = (bf16[16,2,40,256]{3,2,1,0:T(8,128)(2,1)S(1)}, bf16[16,2,40,256]{3,2,1,0:T(8,128)(2,1)S(1)}, u32[]{:S(2)}, u32[]{:S(2)}) collective-permute-start(bf16[16,2,40,256]{3,2,1,0:T(8,128)(2,1)S(1)} %reshape.82), channel_id=1, source_target_pairs={{0,64},{32,96},{64,0},{96,32},{1,65},{33,97},{65,1},{97,33},{2,66}... | collective-permute-start | bytes 1966088 | tf_op jit(solution)/shard_map/ppermute | solution.py:46
  77.3 27.7 %collective-permute-start.3 = (bf16[16,2,40,256]{3,2,1,0:T(8,128)(2,1)S(1)}, bf16[16,2,40,256]{3,2,1,0:T(8,128)(2,1)S(1)}, u32[]{:S(2)}, u32[]{:S(2)}) collective-permute-start(bf16[16,2,40,256]{3,2,1,0:T(8,128)(2,1)S(1)} %reshape.82), channel_id=1, source_target_pairs={{0,96},{32,0},{64,32},{96,64},{1,97},{33,1},{65,33},{97,65},{2,98}... | collective-permute-start | bytes 1966088 | tf_op jit(solution)/shard_map/ppermute | solution.py:46
  106.6 22.3 %copy-start.2 = (f32[256]{0:T(256)S(1)}, f32[256]{0:T(256)}, u32[]{:S(2)}) copy-start(f32[256]{0:T(256)} %param.8) | copy-start | bytes 3076
  106.6 48.3 %copy-start.3 = (f32[1024]{0:T(1024)S(1)}, f32[1024]{0:T(1024)}, u32[]{:S(2)}) copy-start(f32[1024]{0:T(1024)} %param.9) | copy-start | bytes 12292
  115.9 13.0 %all-to-all-start.1 = ((f32[16,1,256]{2,1,0:T(1,128)}), f32[16,1,256]{2,1,0:T(1,128)S(1)}, u32[]{:S(2)}, u32[]{:S(2)}) async-start(f32[16,1,256]{2,1,0:T(1,128)} %broadcast_in_dim.33), calls=%async_computation.1 | async-start | bytes 32768 | tf_op jit(solution)/shard_map/all_to_all | solution.py:29
  129.5 46.1 %copy-start.1 = (f32[256]{0:T(256)}, f32[256]{0:T(256)S(1)}, u32[]{:S(2)}) copy-start(f32[256]{0:T(256)S(1)} %get-tuple-element.30) | copy-start | bytes 3076
  137.7 15.9 %all-to-all-start.2 = ((f32[16,1,1152]{2,1,0:T(1,128)}), f32[16,1,1152]{2,1,0:T(1,128)S(1)}, u32[]{:S(2)}, u32[]{:S(2)}) async-start(f32[16,1,1152]{2,1,0:T(1,128)} %broadcast_in_dim.35), calls=%async_computation.2 | async-start | bytes 147456 | tf_op jit(solution)/shard_map/all_to_all | solution.py:29
  157.6 12.5 %all-to-all-start.3 = ((f32[32,1,128]{2,1,0:T(1,128)}), f32[32,1,128]{2,1,0:T(1,128)S(1)}, u32[]{:S(2)}, u32[]{:S(2)}) async-start(f32[32,1,128]{2,1,0:T(1,128)} %broadcast_in_dim.39), calls=%async_computation.3 | async-start | bytes 32768 | tf_op jit(solution)/shard_map/all_to_all | solution.py:29
Sparse Core Ops, SparseCore 0:
  10.7 91.8 all-gather.3

commit v3 on v0

v3 whole, which is shorter than its diff:
```python
import jax
import jax.numpy as jnp
from jax import lax
from jax.experimental import pallas as pl
from jax.experimental.pallas import tpu as pltpu
from jax.sharding import Mesh, PartitionSpec as P

D = 8192
F = 16384

decay_rate = 1.0 - 10.0 ** (-0.8)
step_size = 0.05
tiny_eps = 1e-30

NX, NY, NZ = 4, 4, 16
XY, ZC = ("x", "y"), ("z", "c")


def pairs(n, flip):
    return [(i, i ^ flip) for i in range(n)]


def in_order(y, own, one, two, three):
    odd, upper = (y & 1) == 1, (y & 2) == 2
    near = [jnp.where(odd, one, own), jnp.where(odd, own, one)]
    far = [jnp.where(odd, three, two), jnp.where(odd, two, three)]
    first = [jnp.where(upper, q, p) for p, q in zip(near, far)]
    second = [jnp.where(upper, p, q) for p, q in zip(near, far)]
    return jnp.concatenate(first + second, axis=2)


def features_of_rows(inputs, weight_sq):
    x, y, c = lax.axis_index("x"), lax.axis_index("y"), lax.axis_index("c")
    tokens = inputs.shape[0] // NY
    part = lax.dynamic_slice_in_dim(inputs, y * tokens, tokens, 0)
    part = part.reshape(tokens, NZ, NX, 128)
    part = lax.dynamic_index_in_dim(part, x, 2, keepdims=False)
    part = lax.all_to_all(part.transpose(1, 0, 2), "z", 0, 0)
    part, weight_sq = lax.optimization_barrier((part, weight_sq))
    part = lax.all_gather(part, "x", axis=0)
    low, high = part[:2], part[2:]
    own = jnp.where(c == 0, low, high)
    other = lax.ppermute(jnp.where(c == 0, high, low), "c", pairs(2, 1))
    first, second = jnp.where(c == 0, own, other), jnp.where(c == 0, other, own)

    def swap(block, flip):
        return lax.ppermute(block, "y", pairs(NY, flip))

    first_one, second_three = swap(first, 1), swap(second, 3)
    first_three, second_one = swap(first, 3), swap(second, 1)
    first_two, second_two = swap(first_one, 3), swap(second_three, 1)
    return (
        in_order(y, first, first_one, first_two, first_three),
        in_order(y, second, second_one, second_two, second_three),
        weight_sq,
    )


PLANES = 4


def gradient_kernel(first_ref, second_ref, cot_ref, grad_ref, rows_ref):
    step = pl.program_id(0)

    @pl.when(step == 0)
    def _():
        grad_ref[...] = jnp.zeros_like(grad_ref)

    feat = [
        jnp.concatenate([ref[0, plane], ref[1, plane]], axis=1)
        for plane in range(PLANES)
        for ref in (first_ref, second_ref)
    ]
    grad_ref[...] += lax.dot_general(
        jnp.concatenate(feat, axis=0),
        cot_ref[...].reshape(PLANES * 320, 1024),
        (((0,), (0,)), ((), ())),
        preferred_element_type=jnp.float32,
    )

    @pl.when(step == pl.num_programs(0) - 1)
    def _():
        squares = jnp.zeros((256, 128), jnp.float32)
        for j in range(8):
            part = grad_ref[:, j * 128 : (j + 1) * 128]
            squares += part * part + tiny_eps
        row = jnp.sum(squares.T, axis=0, keepdims=True)
        for i in range(NX * NY):
            rows_ref[i] = row


LARGE = pltpu.CompilerParams(vmem_limit_bytes=56 * 2**20)
SMALL = pltpu.CompilerParams(vmem_limit_bytes=16 * 2**20)


def gradient_of(first, second, all_cotangent):
    feat_spec = pl.BlockSpec((2, PLANES, 160, 128), lambda i: (0, i, 0, 0))
    return pl.pallas_call(
        gradient_kernel,
        grid=(NZ // PLANES,),
        in_specs=[feat_spec, feat_spec, pl.BlockSpec((PLANES, 2, 160, 1024), lambda i: (i, 0, 0, 0))],
        out_specs=[
            pl.BlockSpec((256, 1024), lambda i: (0, 0)),
            pl.BlockSpec((NX * NY, 1, 256), lambda i: (0, 0, 0)),
        ],
        out_shape=[
            jax.ShapeDtypeStruct((256, 1024), jnp.float32),
            jax.ShapeDtypeStruct((NX * NY, 1, 256), jnp.float32),
        ],
        cost_estimate=pl.CostEstimate(
            flops=2 * 256 * 1024 * 5120, bytes_accessed=15_000_000, transcendentals=0
        ),
        compiler_params=LARGE,
        name="gradient",
    )(first, second, all_cotangent)


def rows_kernel(
    got_ref, moment_ref, weight_sq_ref, grad_hbm, new_rows_ref, factor_ref, out_ref, grad, sem
):
    fetch = pltpu.make_async_copy(grad_hbm, grad, sem)
    fetch.start()
    total = jnp.sum(got_ref[...], axis=0)
    new_rows = decay_rate * moment_ref[...] + (1.0 - decay_rate) * (total / F)
    new_rows_ref[...] = new_rows
    down = jnp.broadcast_to(new_rows, (128, 256)).T
    factor_ref[...] = lax.rsqrt(down)
    inverse = 1.0 / down
    lanes = lax.broadcasted_iota(jnp.int32, (1, 128), 1)
    rows_sum = jnp.sum(new_rows, axis=1, keepdims=True)
    scalars = jnp.where(lanes == 0, rows_sum, jnp.where(lanes == 1, weight_sq_ref[0, 0], 0.0))
    fetch.wait()
    squares, weighted = [], []
    for j in range(8):
        part = grad[:, j * 128 : (j + 1) * 128]
        part = part * part
        squares.append(jnp.sum(part + tiny_eps, axis=0, keepdims=True))
        weighted.append(jnp.sum(part * inverse, axis=0, keepdims=True))
    for half in range(2):
        mine = slice(4 * half, 4 * half + 4)
        out_ref[half : half + 1] = jnp.concatenate(squares[mine] + weighted[mine] + [scalars], axis=1)


VMEM = pl.BlockSpec(memory_space=pltpu.VMEM)
SMEM = pl.BlockSpec(memory_space=pltpu.SMEM)
HBM = pl.BlockSpec(memory_space=pltpu.HBM)


def rows_call(row_sums, row_moment, weight_sq, gradient):
    return pl.pallas_call(
        rows_kernel,
        in_specs=[VMEM, VMEM, SMEM, HBM],
        out_specs=[VMEM] * 3,
        out_shape=[
            jax.ShapeDtypeStruct((1, 256), jnp.float32),
            jax.ShapeDtypeStruct((256, 128), jnp.float32),
            jax.ShapeDtypeStruct((2, 1152), jnp.float32),
        ],
        scratch_shapes=[pltpu.VMEM((256, 1024), jnp.float32), pltpu.SemaphoreType.DMA],
        compiler_params=SMALL,
        name="rows",
    )(row_sums, row_moment, weight_sq, gradient)


def columns_kernel(got_ref, moment_ref, new_cols_ref, scalars_ref, out_ref):
    total = jnp.sum(got_ref[...], axis=0)
    new_cols = decay_rate * moment_ref[...] + (1.0 - decay_rate) * (total[:, :512] / D)
    new_cols_ref[...] = new_cols
    row_mean = total[:, 1024:1025] / D
    scaled_sq = row_mean * jnp.sum(total[:, 512:1024] / new_cols, axis=1, keepdims=True)
    lanes = lax.broadcasted_iota(jnp.int32, (1, 128), 1)
    scalars_ref[...] = jnp.broadcast_to(row_mean, (1, 128))
    half_sq = 0.5 * total[:, 1025:1026]
    row = jnp.where(lanes == 0, scaled_sq, jnp.where(lanes == 1, half_sq, 0.0))
    for i in range(2 * NX * NY):
        out_ref[i] = row


def columns_call(packed, half_moment):
    return pl.pallas_call(
        columns_kernel,
        in_specs=[VMEM] * 2,
        out_specs=[VMEM] * 3,
        out_shape=[
            jax.ShapeDtypeStruct((1, 512), jnp.float32),
            jax.ShapeDtypeStruct((1, 128), jnp.float32),
            jax.ShapeDtypeStruct((2 * NX * NY, 1, 128), jnp.float32),
        ],
        compiler_params=SMALL,
        name="columns",
    )(packed, half_moment)


PARTS = 4


def update_kernel(
    got_ref, mean_ref, factor_ref, cols_ref, grad_hbm, weight_hbm, new_weight_hbm, update_hbm,
    cols_hbm, grad, weight, new_weight, update, in_sems, out_sems, cols_sem,
):
    height = 256 // PARTS
    blocks = [pl.ds(i * height, height) for i in range(PARTS)]
    fetches, stores = [], []
    for i, rows in enumerate(blocks):
        fetches.append(pltpu.make_async_copy(grad_hbm.at[rows], grad.at[rows], in_sems.at[0, i]))
        fetches.append(pltpu.make_async_copy(weight_hbm.at[rows], weight.at[rows], in_sems.at[1, i]))
    for fetch in fetches:
        fetch.start()
    stores.append(pltpu.make_async_copy(cols_ref, cols_hbm, cols_sem))
    stores[0].start()
    total = jnp.sum(got_ref[...], axis=0)
    update_rms = jnp.sqrt(total[:, 0:1] / (D * F))
    weight_rms = jnp.sqrt(total[:, 1:2] / (D * F))
    scale = jnp.sqrt(mean_ref[:, 0:1]) / jnp.maximum(1.0, update_rms)
    step = step_size * weight_rms
    cols = [lax.rsqrt(cols_ref[half]) * scale for half in range(2)]
    for i, rows in enumerate(blocks):
        fetches[2 * i].wait()
        fetches[2 * i + 1].wait()
        factor = factor_ref[rows]
        for j in range(8):
            here = slice(j * 128, (j + 1) * 128)
            half = slice((j % 4) * 128, (j % 4 + 1) * 128)
            clipped = grad[rows, here] * factor * cols[j // 4][:, half]
            update[rows, here] = clipped.astype(jnp.bfloat16)
            new_weight[rows, here] = weight[rows, here] - step * clipped
        out = [
            pltpu.make_async_copy(new_weight.at[rows], new_weight_hbm.at[rows], out_sems.at[0, i]),
            pltpu.make_async_copy(update.at[rows], update_hbm.at[rows], out_sems.at[1, i]),
        ]
        for store in out:
            store.start()
        stores += out
    for store in stores:
        store.wait()


def update_call(last, row_mean, row_factor, new_cols, gradient, weight):
    whole = lambda dtype: pltpu.VMEM((256, 1024), dtype)
    return pl.pallas_call(
        update_kernel,
        in_specs=[VMEM] * 4 + [HBM] * 2,
        out_specs=[HBM] * 3,
        out_shape=[
            jax.ShapeDtypeStruct((256, 1024), jnp.float32),
            jax.ShapeDtypeStruct((256, 1024), jnp.bfloat16),
            jax.ShapeDtypeStruct((2, 1, 512), jnp.float32),
        ],
        scratch_shapes=[
            whole(jnp.float32),
            whole(jnp.float32),
            whole(jnp.float32),
            whole(jnp.bfloat16),
            pltpu.SemaphoreType.DMA((2, PARTS)),
            pltpu.SemaphoreType.DMA((2, PARTS)),
            pltpu.SemaphoreType.DMA,
        ],
        compiler_params=SMALL,
        name="update",
    )(last, row_mean, row_factor, new_cols, gradient, weight)


def on_device(inputs, cotangent, weight, row_moment, col_moment):
    c = lax.axis_index("c")
    all_cotangent = lax.all_gather(cotangent, ZC, axis=0).reshape(NZ, 2, *cotangent.shape)
    first, second, weight_sq = features_of_rows(inputs, jnp.sum(weight * weight))
    gradient, row_sums = gradient_of(first, second, all_cotangent)
    row_sums = lax.all_to_all(row_sums, XY, 0, 0)
    new_rows, row_factor, packed = rows_call(
        row_sums, row_moment[None], weight_sq.reshape(1, 1), gradient
    )
    packed = lax.dynamic_slice_in_dim(lax.psum(packed, "c"), c, 1, 0)
    packed = lax.all_to_all(jnp.broadcast_to(packed[None], (NZ, 1, 1152)), "z", 0, 0)
    half_moment = jnp.where(c == 0, col_moment[:512], col_moment[512:])
    half_cols, row_mean, last = columns_call(packed, half_moment[None])
    last = lax.all_to_all(last, ("x", "y", "c"), 0, 0)
    new_cols = lax.all_gather(half_cols, "c", axis=0)
    new_weight, update, new_cols = update_call(last, row_mean, row_factor, new_cols, gradient, weight)
    return (new_weight, update, new_rows[0], new_cols.reshape(1024))


def solution(mesh):
    fine = Mesh(mesh.devices.reshape(NX, NY, NZ, 2), ("x", "y", "z", "c"))
    return jax.shard_map(
        on_device,
        mesh=fine,
        in_specs=(P(ZC, None), P(ZC, XY), P(ZC, XY), P(ZC), P(XY)),
        out_specs=(P(ZC, XY), P(ZC, XY), P(ZC), P(XY)),
        check_vma=False,
    )
```

time: 413 us -> 173 us (0.42)
  blocking collectives: 187 us -> 17.8 us
  waiting for transfers between devices: 174 us -> 50.9 us
  starting transfers between devices: 16.8 us -> 62.2 us
  Pallas kernels: 0 us -> 12 us
  matrix products: 7.87 us -> 0 us
  local copies, waits for them, and re-layouts: 3.59 us -> 8.93 us
    psum x3 -> x1, blocking collectives: 187 us -> 3.87 us  [on_device(): packed = lax.dynamic_slice_in_dim(lax.psum(packed, 'c'), c, 1, 0)]
    all_to_all x1 -> x4, waiting for transfers between devices: 149 us -> 33.4 us  [the longest x1 11.7 us: on_device(): lax.all_to_all(jnp.broadcast_to(packed[None], (NZ, 1, 1152)), 'z', 0, 0)]
    ppermute x0 -> x7, starting transfers between devices: none -> 27.3 us  [the longest x6 18.7 us: swap(): return lax.ppermute(block, 'y', pairs(NY, flip))]
    all_gather x1, waiting for transfers between devices: 24.2 us -> 2.58 us  [on_device(): lax.all_gather(cotangent, ZC, axis=0).reshape(NZ, 2, *cotangent.shape)]
    all_to_all x1 -> x4, starting transfers between devices: 16.8 us -> 34.8 us  [the longest x1 15.7 us: features_of_rows(): part = lax.all_to_all(part.transpose(1, 0, 2), 'z', 0, 0)]
    ppermute x0 -> x7, waiting for transfers between devices: none -> 14.2 us  [the longest x6 13 us: swap(): return lax.ppermute(block, 'y', pairs(NY, flip))]
    all_gather x0 -> x2, blocking collectives: none -> 14 us  [the longest x1 12.1 us: features_of_rows(): part = lax.all_gather(part, 'x', axis=0)]
    pallas_call x0 -> x4, Pallas kernels: none -> 12 us  [the longest x1 8.07 us: gradient_of(): pl.pallas_call(gradient_kernel, grid=(NZ // PLANES,), in_specs=[feat_spec...]
  transfers between devices with their start and end apart: 2 -> 12, of which waited for: 2 -> 10; matrix products, arithmetic and copies ran while one was open for 1% -> 6% of each run, Pallas kernels for 0% -> 0%
where the time goes in v3:
time: 173 us
  starting transfers between devices  62.2 us (36%)
  waiting for transfers between devices  50.9 us (29%)
  blocking collectives  17.8 us (10%)
  between operations  14.2 us (8%)
  Pallas kernels  12 us (7%)
  local copies, waits for them, and re-layouts  8.93 us (5%)
  other arithmetic  6.5 us (4%)
    ppermute x6, starting transfers between devices, swap(): return lax.ppermute(block, 'y', pairs(NY, flip))  18.7 us
    all_to_all x1, starting transfers between devices, features_of_rows(): part = lax.all_to_all(part.transpose(1, 0, 2), 'z', 0, 0)  15.7 us
    ppermute x6, waiting for transfers between devices, swap(): return lax.ppermute(block, 'y', pairs(NY, flip))  13 us
    all_gather x1, blocking collectives, features_of_rows(): part = lax.all_gather(part, 'x', axis=0)  12.1 us
    all_to_all x1, waiting for transfers between devices, on_device(): lax.all_to_all(jnp.broadcast_to(packed[None], (NZ, 1, 1152)), 'z', 0, 0)  11.7 us
    all_to_all x1, waiting for transfers between devices, features_of_rows(): part = lax.all_to_all(part.transpose(1, 0, 2), 'z', 0, 0)  10.1 us
    ppermute x1, starting transfers between devices, features_of_rows(): other = lax.ppermute(jnp.where(c == 0, high, low), 'c', pairs(2, 1))  8.58 us
    pallas_call x1, Pallas kernels, gradient_of(): pl.pallas_call(gradient_kernel, grid=(NZ // PLANES,), in_specs=[feat_spec...  8.07 us
  transfers between devices with their start and end apart: 12, of which 10 were waited for; matrix products, arithmetic and copies ran while one was open for 6% of the time, Pallas kernels for 0%

profile of v3, /device:TPU:1, one launch (start us, length us, event | category | flops | bytes accessed | tf_op | source)
XLA Modules:
  0.0 172.6 jit_solution(13995454258317447411)
XLA Ops:
  7.2 0.0 copy-start
  7.2 0.0 all-gather.6.cloned.1.call-start
  7.2 0.7 all-gather.6.cloned.1.call-update
  7.9 1.0 copy-done
  9.0 1.3 reshape.23
  10.3 1.4 constant_dynamic-slice_fusion
  11.7 0.8 copy.16
  12.5 15.7 %all-to-all-start = ((bf16[16,40,128]{2,1,0:T(8,128)(2,1)}), bf16[16,40,128]{2,1,0:T(8,128)(2,1)S(1)}, u32[]{:S(2)}, u32[]{:S(2)}) async-start(bf16[16,40,128]{2,1,0:T(8,128)(2,1)} %bitcast.14), calls=%async_computation | async-start | bytes 327680 | tf_op jit(solution)/shard_map/all_to_all | solution.py:38
  28.2 2.1 %multiply_reduce_fusion = f32[]{:T(128)} fusion(f32[256,1024]{1,0:T(8,128)} %weight_hbm.1), kind=kLoop, calls=%fused_computation.2 | loop fusion | flops 524287 | bytes 1048580 | tf_op jit(solution)/shard_map/reduce_sum | solution.py:266
  30.3 10.1 %all-to-all-done = bf16[16,40,128]{2,1,0:T(8,128)(2,1)S(1)} async-done(((bf16[16,40,128]{2,1,0:T(8,128)(2,1)}), bf16[16,40,128]{2,1,0:T(8,128)(2,1)S(1)}, u32[]{:S(2)}, u32[]{:S(2)}) %all-to-all-start) | async-done | bytes 163872 | tf_op jit(solution)/shard_map/all_to_all | solution.py:38
  40.5 12.1 %all-gather = bf16[64,40,128]{2,1,0:T(8,128)(2,1)S(1)} all-gather(bf16[16,40,128]{2,1,0:T(8,128)(2,1)S(1)} %all-to-all-done), channel_id=2, replica_groups=mesh['x'=4,'y'=4,'z'=16,'c'=2] {'x'}, dimensions={0}, use_global_device_ids=true | all-gather | bytes 819200 | tf_op jit(solution)/shard_map/all_gather | solution.py:40
  52.6 8.6 %collective-permute-start = (bf16[2,16,40,128]{3,2,1,0:T(8,128)(2,1)S(1)}, bf16[2,16,40,128]{3,2,1,0:T(8,128)(2,1)S(1)}, u32[]{:S(2)}, u32[]{:S(2)}) collective-permute-start(bf16[2,16,40,128]{3,2,1,0:T(8,128)(2,1)S(1)} %bitcast.20), channel_id=1, source_target_pairs={{0,1},{1,0},{2,3},{3,2},{4,5},{5,4},{6,7},{7,6},{8,9},{9,8},{10,11... | collective-permute-start | bytes 983048 | tf_op jit(solution)/shard_map/ppermute | solution.py:43
  61.2 1.2 collective-permute-done
  62.5 5.0 %collective-permute-start.4 = (bf16[2,16,40,128]{3,2,1,0:T(8,128)(2,1)S(1)}, bf16[2,16,40,128]{3,2,1,0:T(8,128)(2,1)}, u32[]{:S(2)}, u32[]{:S(2)}) collective-permute-start(bf16[2,16,40,128]{3,2,1,0:T(8,128)(2,1)S(1)} %get-tuple-element.38), channel_id=1, source_target_pairs={{0,96},{32,64},{64,32},{96,0},{1,97},{33,65},{65,33},{97,1},{2,98}... | collective-permute-start | bytes 983048 | tf_op jit(solution)/shard_map/ppermute | solution.py:47
  67.6 1.9 %collective-permute-start.2 = (bf16[2,16,40,128]{3,2,1,0:T(8,128)(2,1)S(1)}, bf16[2,16,40,128]{3,2,1,0:T(8,128)(2,1)}, u32[]{:S(2)}, u32[]{:S(2)}) collective-permute-start(bf16[2,16,40,128]{3,2,1,0:T(8,128)(2,1)S(1)} %get-tuple-element.39), channel_id=1, source_target_pairs={{0,32},{32,0},{64,96},{96,64},{1,33},{33,1},{65,97},{97,65},{2,34}... | collective-permute-start | bytes 983048 | tf_op jit(solution)/shard_map/ppermute | solution.py:47
  69.5 3.4 %collective-permute-start.6 = (bf16[2,16,40,128]{3,2,1,0:T(8,128)(2,1)S(1)}, bf16[2,16,40,128]{3,2,1,0:T(8,128)(2,1)}, u32[]{:S(2)}, u32[]{:S(2)}) collective-permute-start(bf16[2,16,40,128]{3,2,1,0:T(8,128)(2,1)S(1)} %get-tuple-element.38), channel_id=1, source_target_pairs={{0,32},{32,0},{64,96},{96,64},{1,33},{33,1},{65,97},{97,65},{2,34}... | collective-permute-start | bytes 983048 | tf_op jit(solution)/shard_map/ppermute | solution.py:47
  72.9 2.6 %collective-permute-done.4 = bf16[2,16,40,128]{3,2,1,0:T(8,128)(2,1)} collective-permute-done((bf16[2,16,40,128]{3,2,1,0:T(8,128)(2,1)S(1)}, bf16[2,16,40,128]{3,2,1,0:T(8,128)(2,1)}, u32[]{:S(2)}, u32[]{:S(2)}) %collective-permute-start.4) | collective-permute-done | bytes 327712 | tf_op jit(solution)/shard_map/ppermute | solution.py:47
  75.4 1.9 %collective-permute-start.5 = (bf16[2,16,40,128]{3,2,1,0:T(8,128)(2,1)}, bf16[2,16,40,128]{3,2,1,0:T(8,128)(2,1)}, u32[]{:S(2)}, u32[]{:S(2)}) collective-permute-start(bf16[2,16,40,128]{3,2,1,0:T(8,128)(2,1)} %collective-permute-done.4), channel_id=1, source_target_pairs={{0,32},{32,0},{64,96},{96,64},{1,33},{33,1},{65,97},{97,65},{2,34}... | collective-permute-start | bytes 983048 | tf_op jit(solution)/shard_map/ppermute | solution.py:47
  77.4 4.3 %collective-permute-start.1 = (bf16[2,16,40,128]{3,2,1,0:T(8,128)(2,1)S(1)}, bf16[2,16,40,128]{3,2,1,0:T(8,128)(2,1)}, u32[]{:S(2)}, u32[]{:S(2)}) collective-permute-start(bf16[2,16,40,128]{3,2,1,0:T(8,128)(2,1)S(1)} %get-tuple-element.39), channel_id=1, source_target_pairs={{0,96},{32,64},{64,32},{96,0},{1,97},{33,65},{65,33},{97,1},{2,98}... | collective-permute-start | bytes 983048 | tf_op jit(solution)/shard_map/ppermute | solution.py:47
  81.6 0.0 collective-permute-done.2
  81.6 2.2 %collective-permute-start.3 = (bf16[2,16,40,128]{3,2,1,0:T(8,128)(2,1)}, bf16[2,16,40,128]{3,2,1,0:T(8,128)(2,1)}, u32[]{:S(2)}, u32[]{:S(2)}) collective-permute-start(bf16[2,16,40,128]{3,2,1,0:T(8,128)(2,1)} %collective-permute-done.2), channel_id=1, source_target_pairs={{0,96},{32,64},{64,32},{96,0},{1,97},{33,65},{65,33},{97,1},{2,98}... | collective-permute-start | bytes 983048 | tf_op jit(solution)/shard_map/ppermute | solution.py:47
  83.9 1.3 collective-permute-done.6
  85.2 7.0 %collective-permute-done.5 = bf16[2,16,40,128]{3,2,1,0:T(8,128)(2,1)} collective-permute-done((bf16[2,16,40,128]{3,2,1,0:T(8,128)(2,1)}, bf16[2,16,40,128]{3,2,1,0:T(8,128)(2,1)}, u32[]{:S(2)}, u32[]{:S(2)}) %collective-permute-start.5) | collective-permute-done | bytes 327712 | tf_op jit(solution)/shard_map/ppermute | solution.py:47
  92.2 1.3 broadcast_select_fusion.15
  93.5 0.0 collective-permute-done.1
  93.5 2.1 %collective-permute-done.3 = bf16[2,16,40,128]{3,2,1,0:T(8,128)(2,1)} collective-permute-done((bf16[2,16,40,128]{3,2,1,0:T(8,128)(2,1)}, bf16[2,16,40,128]{3,2,1,0:T(8,128)(2,1)}, u32[]{:S(2)}, u32[]{:S(2)}) %collective-permute-start.3) | collective-permute-done | bytes 327712 | tf_op jit(solution)/shard_map/ppermute | solution.py:47
  95.6 1.3 broadcast_select_fusion.19
  96.9 1.7 %pad_maximum_fusion = (bf16[2,16,160,128]{3,2,1,0:T(8,128)(2,1)}, bf16[2,16,160,128]{3,2,1,0:T(8,128)(2,1)}) fusion(bf16[2,16,40,128]{3,2,1,0:T(8,128)(2,1)S(1)} %get-tuple-element.37, bf16[2,16,40,128]{3,2,1,0:T(8,128)(2,1)S(1)} %get-tuple-element.36, bf16[2,16,40,128]{3,2,1,0:T(8,128)(2,1)S(1)} %get-tuple-element.35, ...), kind=kLoop, calls=%fused_computation | loop fusion | flops 10485760 | bytes 5242880 | tf_op jit(solution)/shard_map/concatenate | solution.py:29
  98.6 2.6 %all-gather.6.cloned.1.call-done = bf16[5120,1024]{1,0:T(8,128)(2,1)} async-done(((bf16[160,1024]{1,0:T(8,128)(2,1)}), bf16[5120,1024]{1,0:T(8,128)(2,1)}) %all-gather.6.cloned.1.call-update) | async-done | bytes 10485776 | tf_op jit(solution)/shard_map/all_gather | solution.py:265
  101.2 0.0 copy-start.4
  101.2 8.1 %gradient.1 = (f32[256,1024]{1,0:T(8,128)}, f32[16,1,256]{2,1,0:T(1,128)}) custom-call(bf16[2,16,160,128]{3,2,1,0:T(8,128)(2,1)} %get-tuple-element.42.first_ref, bf16[2,16,160,128]{3,2,1,0:T(8,128)(2,1)} %get-tuple-element.43.second_ref, bf16[16,2,160,1024]{3,2,1,0:T(8,128)(2,1)} %bitcast.18), custom_call_target="tpu_custom_call" | custom-call | flops 2684354560 | bytes 15000000 | tf_op jit(solution)/shard_map/gradient/pallas_call | solution.py:98
  109.3 7.1 %all-to-all-start.1 = ((f32[16,1,256]{2,1,0:T(1,128)}), f32[16,1,256]{2,1,0:T(1,128)S(1)}, u32[]{:S(2)}, u32[]{:S(2)}) async-start(f32[16,1,256]{2,1,0:T(1,128)} %get-tuple-element.18), calls=%async_computation.1 | async-start | bytes 32768 | tf_op jit(solution)/shard_map/all_to_all | solution.py:268
  116.4 6.4 %all-to-all-done.1.got_ref = f32[16,1,256]{2,1,0:T(1,128)S(1)} async-done(((f32[16,1,256]{2,1,0:T(1,128)}), f32[16,1,256]{2,1,0:T(1,128)S(1)}, u32[]{:S(2)}, u32[]{:S(2)}) %all-to-all-start.1) | async-done | bytes 16416 | tf_op jit(solution)/shard_map/all_to_all | solution.py:268
  122.9 0.0 copy-done.4
  122.9 1.2 copy-done.2
  124.1 1.4 rows.1
  125.5 3.9 %psum.7 = f32[2,1152]{1,0:T(2,128)S(1)} all-reduce(f32[2,1152]{1,0:T(2,128)S(1)} %get-tuple-element.21), channel_id=1, replica_groups=mesh['x'=4,'y'=4,'z'=16,'c'=2] {'c'}, use_global_device_ids=true, to_apply=%region_1.2 | all-reduce | flops 2304 | bytes 18432 | tf_op jit(solution)/shard_map/psum | solution.py:272
  129.4 0.7 broadcast_in_dim.16
  130.1 6.5 %all-to-all-start.2 = ((f32[16,1,1152]{2,1,0:T(1,128)}), f32[16,1,1152]{2,1,0:T(1,128)S(1)}, u32[]{:S(2)}, u32[]{:S(2)}) async-start(f32[16,1,1152]{2,1,0:T(1,128)} %broadcast_in_dim.16), calls=%async_computation.2 | async-start | bytes 147456 | tf_op jit(solution)/shard_map/all_to_all | solution.py:273
  136.6 0.0 copy-done.5
  136.6 11.7 %all-to-all-done.2.got_ref = f32[16,1,1152]{2,1,0:T(1,128)S(1)} async-done(((f32[16,1,1152]{2,1,0:T(1,128)}), f32[16,1,1152]{2,1,0:T(1,128)S(1)}, u32[]{:S(2)}, u32[]{:S(2)}) %all-to-all-start.2) | async-done | bytes 73760 | tf_op jit(solution)/shard_map/all_to_all | solution.py:273
  148.3 0.8 columns.1
  149.1 5.5 %all-to-all-start.3 = ((f32[32,1,128]{2,1,0:T(1,128)}), f32[32,1,128]{2,1,0:T(1,128)S(1)}, u32[]{:S(2)}, u32[]{:S(2)}) async-start(f32[32,1,128]{2,1,0:T(1,128)} %get-tuple-element.22), calls=%async_computation.3 | async-start | bytes 32768 | tf_op jit(solution)/shard_map/all_to_all | solution.py:276
  154.6 1.8 %all-gather.3.cols_ref = f32[2,1,512]{2,1,0:T(1,128)S(1)} all-gather(f32[1,1,512]{2,1,0:T(1,128)S(1)} %bitcast.16), channel_id=4, replica_groups=mesh['x'=4,'y'=4,'z'=16,'c'=2] {'c'}, dimensions={0}, use_global_device_ids=true | all-gather | bytes 6144 | tf_op jit(solution)/shard_map/all_gather | solution.py:277
  156.5 5.2 %all-to-all-done.3.got_ref = f32[32,1,128]{2,1,0:T(1,128)S(1)} async-done(((f32[32,1,128]{2,1,0:T(1,128)}), f32[32,1,128]{2,1,0:T(1,128)S(1)}, u32[]{:S(2)}, u32[]{:S(2)}) %all-to-all-start.3) | async-done | bytes 16416 | tf_op jit(solution)/shard_map/all_to_all | solution.py:276
  161.6 1.2 copy-done.1
  162.8 1.2 copy-done.3
  164.1 1.7 update.1
  (9 shorter events, 0.2 us)
Async XLA Ops:
  7.2 1.7 %copy-start = (bf16[160,8192]{1,0:T(8,128)(2,1)S(1)}, bf16[160,8192]{1,0:T(8,128)(2,1)}, u32[]{:S(2)}) copy-start(bf16[160,8192]{1,0:T(8,128)(2,1)} %param.5) | copy-start | bytes 7864324
  7.2 94.0 %all-gather.6.cloned.1.call-start = ((), (), s32[]{:S(2)}) async-start(), calls=%async_computation.4 | async-start | bytes 10813440 | tf_op jit(solution)/shard_map/all_gather | solution.py:265
  12.5 28.0 %all-to-all-start = ((bf16[16,40,128]{2,1,0:T(8,128)(2,1)}), bf16[16,40,128]{2,1,0:T(8,128)(2,1)S(1)}, u32[]{:S(2)}, u32[]{:S(2)}) async-start(bf16[16,40,128]{2,1,0:T(8,128)(2,1)} %bitcast.14), calls=%async_computation | async-start | bytes 327680 | tf_op jit(solution)/shard_map/all_to_all | solution.py:38
  52.6 9.8 %collective-permute-start = (bf16[2,16,40,128]{3,2,1,0:T(8,128)(2,1)S(1)}, bf16[2,16,40,128]{3,2,1,0:T(8,128)(2,1)S(1)}, u32[]{:S(2)}, u32[]{:S(2)}) collective-permute-start(bf16[2,16,40,128]{3,2,1,0:T(8,128)(2,1)S(1)} %bitcast.20), channel_id=1, source_target_pairs={{0,1},{1,0},{2,3},{3,2},{4,5},{5,4},{6,7},{7,6},{8,9},{9,8},{10,11... | collective-permute-start | bytes 983048 | tf_op jit(solution)/shard_map/ppermute | solution.py:43
  62.5 12.9 %collective-permute-start.4 = (bf16[2,16,40,128]{3,2,1,0:T(8,128)(2,1)S(1)}, bf16[2,16,40,128]{3,2,1,0:T(8,128)(2,1)}, u32[]{:S(2)}, u32[]{:S(2)}) collective-permute-start(bf16[2,16,40,128]{3,2,1,0:T(8,128)(2,1)S(1)} %get-tuple-element.38), channel_id=1, source_target_pairs={{0,96},{32,64},{64,32},{96,0},{1,97},{33,65},{65,33},{97,1},{2,98}... | collective-permute-start | bytes 983048 | tf_op jit(solution)/shard_map/ppermute | solution.py:47
  67.6 14.1 %collective-permute-start.2 = (bf16[2,16,40,128]{3,2,1,0:T(8,128)(2,1)S(1)}, bf16[2,16,40,128]{3,2,1,0:T(8,128)(2,1)}, u32[]{:S(2)}, u32[]{:S(2)}) collective-permute-start(bf16[2,16,40,128]{3,2,1,0:T(8,128)(2,1)S(1)} %get-tuple-element.39), channel_id=1, source_target_pairs={{0,32},{32,0},{64,96},{96,64},{1,33},{33,1},{65,97},{97,65},{2,34}... | collective-permute-start | bytes 983048 | tf_op jit(solution)/shard_map/ppermute | solution.py:47
  69.5 15.7 %collective-permute-start.6 = (bf16[2,16,40,128]{3,2,1,0:T(8,128)(2,1)S(1)}, bf16[2,16,40,128]{3,2,1,0:T(8,128)(2,1)}, u32[]{:S(2)}, u32[]{:S(2)}) collective-permute-start(bf16[2,16,40,128]{3,2,1,0:T(8,128)(2,1)S(1)} %get-tuple-element.38), channel_id=1, source_target_pairs={{0,32},{32,0},{64,96},{96,64},{1,33},{33,1},{65,97},{97,65},{2,34}... | collective-permute-start | bytes 983048 | tf_op jit(solution)/shard_map/ppermute | solution.py:47
  75.4 16.8 %collective-permute-start.5 = (bf16[2,16,40,128]{3,2,1,0:T(8,128)(2,1)}, bf16[2,16,40,128]{3,2,1,0:T(8,128)(2,1)}, u32[]{:S(2)}, u32[]{:S(2)}) collective-permute-start(bf16[2,16,40,128]{3,2,1,0:T(8,128)(2,1)} %collective-permute-done.4), channel_id=1, source_target_pairs={{0,32},{32,0},{64,96},{96,64},{1,33},{33,1},{65,97},{97,65},{2,34}... | collective-permute-start | bytes 983048 | tf_op jit(solution)/shard_map/ppermute | solution.py:47
  77.4 16.1 %collective-permute-start.1 = (bf16[2,16,40,128]{3,2,1,0:T(8,128)(2,1)S(1)}, bf16[2,16,40,128]{3,2,1,0:T(8,128)(2,1)}, u32[]{:S(2)}, u32[]{:S(2)}) collective-permute-start(bf16[2,16,40,128]{3,2,1,0:T(8,128)(2,1)S(1)} %get-tuple-element.39), channel_id=1, source_target_pairs={{0,96},{32,64},{64,32},{96,0},{1,97},{33,65},{65,33},{97,1},{2,98}... | collective-permute-start | bytes 983048 | tf_op jit(solution)/shard_map/ppermute | solution.py:47
  81.6 14.0 %collective-permute-start.3 = (bf16[2,16,40,128]{3,2,1,0:T(8,128)(2,1)}, bf16[2,16,40,128]{3,2,1,0:T(8,128)(2,1)}, u32[]{:S(2)}, u32[]{:S(2)}) collective-permute-start(bf16[2,16,40,128]{3,2,1,0:T(8,128)(2,1)} %collective-permute-done.2), channel_id=1, source_target_pairs={{0,96},{32,64},{64,32},{96,0},{1,97},{33,65},{65,33},{97,1},{2,98}... | collective-permute-start | bytes 983048 | tf_op jit(solution)/shard_map/ppermute | solution.py:47
  101.2 21.7 %copy-start.4 = (f32[256]{0:T(256)S(1)}, f32[256]{0:T(256)}, u32[]{:S(2)}) copy-start(f32[256]{0:T(256)} %param.8) | copy-start | bytes 3076
  101.2 35.4 %copy-start.5 = (f32[1024]{0:T(1024)S(1)}, f32[1024]{0:T(1024)}, u32[]{:S(2)}) copy-start(f32[1024]{0:T(1024)} %param.9) | copy-start | bytes 12292
  109.3 13.6 %all-to-all-start.1 = ((f32[16,1,256]{2,1,0:T(1,128)}), f32[16,1,256]{2,1,0:T(1,128)S(1)}, u32[]{:S(2)}, u32[]{:S(2)}) async-start(f32[16,1,256]{2,1,0:T(1,128)} %get-tuple-element.18), calls=%async_computation.1 | async-start | bytes 32768 | tf_op jit(solution)/shard_map/all_to_all | solution.py:268
  122.9 1.2 copy-start.2
  130.1 18.2 %all-to-all-start.2 = ((f32[16,1,1152]{2,1,0:T(1,128)}), f32[16,1,1152]{2,1,0:T(1,128)S(1)}, u32[]{:S(2)}, u32[]{:S(2)}) async-start(f32[16,1,1152]{2,1,0:T(1,128)} %broadcast_in_dim.16), calls=%async_computation.2 | async-start | bytes 147456 | tf_op jit(solution)/shard_map/all_to_all | solution.py:273
  149.1 12.5 %all-to-all-start.3 = ((f32[32,1,128]{2,1,0:T(1,128)}), f32[32,1,128]{2,1,0:T(1,128)S(1)}, u32[]{:S(2)}, u32[]{:S(2)}) async-start(f32[32,1,128]{2,1,0:T(1,128)} %get-tuple-element.22), calls=%async_computation.3 | async-start | bytes 32768 | tf_op jit(solution)/shard_map/all_to_all | solution.py:276
  161.6 1.2 copy-start.1
  162.8 1.2 copy-start.3
Sparse Core Ops, SparseCore 0:
  10.1 91.0 all-gather.5

commit v4 on v3

--- a/solution.py
+++ b/solution.py
@@ -29,14 +29,14 @@
     return jnp.concatenate(first + second, axis=2)
 
 
-def features_of_rows(inputs, weight_sq):
+def features_of_rows(inputs, early):
     x, y, c = lax.axis_index("x"), lax.axis_index("y"), lax.axis_index("c")
     tokens = inputs.shape[0] // NY
     part = lax.dynamic_slice_in_dim(inputs, y * tokens, tokens, 0)
     part = part.reshape(tokens, NZ, NX, 128)
     part = lax.dynamic_index_in_dim(part, x, 2, keepdims=False)
     part = lax.all_to_all(part.transpose(1, 0, 2), "z", 0, 0)
-    part, weight_sq = lax.optimization_barrier((part, weight_sq))
+    part, early = lax.optimization_barrier((part, early))
     part = lax.all_gather(part, "x", axis=0)
     low, high = part[:2], part[2:]
     own = jnp.where(c == 0, low, high)
@@ -52,14 +52,14 @@
     return (
         in_order(y, first, first_one, first_two, first_three),
         in_order(y, second, second_one, second_two, second_three),
-        weight_sq,
+        early,
     )
 
 
 PLANES = 4
 
 
-def gradient_kernel(first_ref, second_ref, cot_ref, grad_ref, rows_ref):
+def gradient_kernel(core_ref, first_ref, second_ref, cot_ref, grad_ref, rows_ref, other_ref):
     step = pl.program_id(0)
 
     @pl.when(step == 0)
@@ -85,81 +85,96 @@
             part = grad_ref[:, j * 128 : (j + 1) * 128]
             squares += part * part + tiny_eps
         row = jnp.sum(squares.T, axis=0, keepdims=True)
-        for i in range(NX * NY):
+        for i in range(2 * NX * NY):
             rows_ref[i] = row
+        other_ref[...] = grad_ref[:, pl.ds(pl.multiple_of(512 * (1 - core_ref[0, 0]), 512), 512)]
 
 
 LARGE = pltpu.CompilerParams(vmem_limit_bytes=56 * 2**20)
+STREAM = pltpu.CompilerParams(vmem_limit_bytes=52 * 2**20 + 943_104)
 SMALL = pltpu.CompilerParams(vmem_limit_bytes=16 * 2**20)
 
 
-def gradient_of(first, second, all_cotangent):
+VMEM = pl.BlockSpec(memory_space=pltpu.VMEM)
+SMEM = pl.BlockSpec(memory_space=pltpu.SMEM)
+HBM = pl.BlockSpec(memory_space=pltpu.HBM)
+
+
+def gradient_of(core, first, second, all_cotangent):
     feat_spec = pl.BlockSpec((2, PLANES, 160, 128), lambda i: (0, i, 0, 0))
+    cot_spec = pl.BlockSpec((PLANES, 2, 160, 1024), lambda i: (i, 0, 0, 0))
     return pl.pallas_call(
         gradient_kernel,
         grid=(NZ // PLANES,),
-        in_specs=[feat_spec, feat_spec, pl.BlockSpec((PLANES, 2, 160, 1024), lambda i: (i, 0, 0, 0))],
+        in_specs=[SMEM, feat_spec, feat_spec, cot_spec],
         out_specs=[
             pl.BlockSpec((256, 1024), lambda i: (0, 0)),
-            pl.BlockSpec((NX * NY, 1, 256), lambda i: (0, 0, 0)),
+            pl.BlockSpec((2 * NX * NY, 1, 256), lambda i: (0, 0, 0)),
+            pl.BlockSpec((256, 512), lambda i: (0, 0)),
         ],
         out_shape=[
             jax.ShapeDtypeStruct((256, 1024), jnp.float32),
-            jax.ShapeDtypeStruct((NX * NY, 1, 256), jnp.float32),
+            jax.ShapeDtypeStruct((2 * NX * NY, 1, 256), jnp.float32),
+            jax.ShapeDtypeStruct((256, 512), jnp.float32),
         ],
         cost_estimate=pl.CostEstimate(
             flops=2 * 256 * 1024 * 5120, bytes_accessed=15_000_000, transcendentals=0
         ),
         compiler_params=LARGE,
         name="gradient",
-    )(first, second, all_cotangent)
+    )(core, first, second, all_cotangent)
 
 
 def rows_kernel(
-    got_ref, moment_ref, weight_sq_ref, grad_hbm, new_rows_ref, factor_ref, out_ref, grad, sem
+    core_ref, got_ref, moment_ref, weight_sq_ref, grad_hbm, swapped_ref, new_rows_ref, factor_ref, out_ref, grad, sem
 ):
-    fetch = pltpu.make_async_copy(grad_hbm, grad, sem)
+    core = core_ref[0, 0]
+    columns = pl.ds(pl.multiple_of(512 * core, 512), 512)
+    fetch = pltpu.make_async_copy(grad_hbm.at[:, columns], grad, sem)
     fetch.start()
-    total = jnp.sum(got_ref[...], axis=0)
-    new_rows = decay_rate * moment_ref[...] + (1.0 - decay_rate) * (total / F)
-    new_rows_ref[...] = new_rows
-    down = jnp.broadcast_to(new_rows, (128, 256)).T
+    new_rows = []
+    for half in range(2):
+        total = got_ref[half]
+        for i in range(1, NX * NY):
+            total += got_ref[2 * i + half]
+        new_rows.append(decay_rate * moment_ref[half] + (1.0 - decay_rate) * (total / F))
+    own = jnp.where(core == 0, new_rows[0], new_rows[1])
+    other = jnp.where(core == 0, new_rows[1], new_rows[0])
+    new_rows_ref[...] = own
+    down = jnp.broadcast_to(own, (128, 256)).T
     factor_ref[...] = lax.rsqrt(down)
     inverse = 1.0 / down
+    inverse_other = 1.0 / jnp.broadcast_to(other, (128, 256)).T
     lanes = lax.broadcasted_iota(jnp.int32, (1, 128), 1)
-    rows_sum = jnp.sum(new_rows, axis=1, keepdims=True)
+    rows_sum = jnp.sum(own + other, axis=1, keepdims=True)
     scalars = jnp.where(lanes == 0, rows_sum, jnp.where(lanes == 1, weight_sq_ref[0, 0], 0.0))
     fetch.wait()
     squares, weighted = [], []
-    for j in range(8):
-        part = grad[:, j * 128 : (j + 1) * 128]
-        part = part * part
-        squares.append(jnp.sum(part + tiny_eps, axis=0, keepdims=True))
-        weighted.append(jnp.sum(part * inverse, axis=0, keepdims=True))
-    for half in range(2):
-        mine = slice(4 * half, 4 * half + 4)
-        out_ref[half : half + 1] = jnp.concatenate(squares[mine] + weighted[mine] + [scalars], axis=1)
-
-
-VMEM = pl.BlockSpec(memory_space=pltpu.VMEM)
-SMEM = pl.BlockSpec(memory_space=pltpu.SMEM)
-HBM = pl.BlockSpec(memory_space=pltpu.HBM)
-
-
-def rows_call(row_sums, row_moment, weight_sq, gradient):
+    for j in range(4):
+        here = slice(128 * j, 128 * (j + 1))
+        mine, theirs = grad[:, here], swapped_ref[:, here]
+        mine, theirs = mine * mine, theirs * theirs
+        squares.append(jnp.sum((mine + tiny_eps) + (theirs + tiny_eps), axis=0, keepdims=True))
+        weighted.append(jnp.sum(mine * inverse + theirs * inverse_other, axis=0, keepdims=True))
+    row = jnp.concatenate(squares + weighted + [scalars], axis=1)
+    for i in range(NZ):
+        out_ref[i] = row
+
+
+def rows_call(core, row_sums, row_moment, weight_sq, gradient, swapped):
     return pl.pallas_call(
         rows_kernel,
-        in_specs=[VMEM, VMEM, SMEM, HBM],
+        in_specs=[SMEM, VMEM, VMEM, SMEM, HBM, VMEM],
         out_specs=[VMEM] * 3,
         out_shape=[
             jax.ShapeDtypeStruct((1, 256), jnp.float32),
             jax.ShapeDtypeStruct((256, 128), jnp.float32),
-            jax.ShapeDtypeStruct((2, 1152), jnp.float32),
-        ],
-        scratch_shapes=[pltpu.VMEM((256, 1024), jnp.float32), pltpu.SemaphoreType.DMA],
-        compiler_params=SMALL,
+            jax.ShapeDtypeStruct((NZ, 1, 1152), jnp.float32),
+        ],
+        scratch_shapes=[pltpu.VMEM((256, 512), jnp.float32), pltpu.SemaphoreType.DMA],
+        compiler_params=STREAM,
         name="rows",
-    )(row_sums, row_moment, weight_sq, gradient)
+    )(core, row_sums, row_moment, weight_sq, gradient, swapped)
 
 
 def columns_kernel(got_ref, moment_ref, new_cols_ref, scalars_ref, out_ref):
@@ -170,8 +185,8 @@
     scaled_sq = row_mean * jnp.sum(total[:, 512:1024] / new_cols, axis=1, keepdims=True)
     lanes = lax.broadcasted_iota(jnp.int32, (1, 128), 1)
     scalars_ref[...] = jnp.broadcast_to(row_mean, (1, 128))
-    half_sq = 0.5 * total[:, 1025:1026]
-    row = jnp.where(lanes == 0, scaled_sq, jnp.where(lanes == 1, half_sq, 0.0))
+    weight_sq = total[:, 1025:1026]
+    row = jnp.where(lanes == 0, scaled_sq, jnp.where(lanes == 1, weight_sq, 0.0))
     for i in range(2 * NX * NY):
         out_ref[i] = row
 
@@ -255,27 +270,31 @@
             pltpu.SemaphoreType.DMA((2, PARTS)),
             pltpu.SemaphoreType.DMA,
         ],
-        compiler_params=SMALL,
+        compiler_params=STREAM,
         name="update",
     )(last, row_mean, row_factor, new_cols, gradient, weight)
 
 
 def on_device(inputs, cotangent, weight, row_moment, col_moment):
     c = lax.axis_index("c")
+    core = c.astype(jnp.int32).reshape(1, 1)
     all_cotangent = lax.all_gather(cotangent, ZC, axis=0).reshape(NZ, 2, *cotangent.shape)
-    first, second, weight_sq = features_of_rows(inputs, jnp.sum(weight * weight))
-    gradient, row_sums = gradient_of(first, second, all_cotangent)
-    row_sums = lax.all_to_all(row_sums, XY, 0, 0)
+    early = (jnp.sum(weight * weight), lax.all_gather(row_moment[None], "c", axis=0))
+    first, second, (weight_sq, row_moments) = features_of_rows(inputs, early)
+    gradient, row_sums, swapped = gradient_of(core, first, second, all_cotangent)
+    row_sums = lax.all_to_all(row_sums, ("x", "y", "c"), 0, 0)
+    swapped = lax.ppermute(swapped, "c", pairs(2, 1))
     new_rows, row_factor, packed = rows_call(
-        row_sums, row_moment[None], weight_sq.reshape(1, 1), gradient
-    )
-    packed = lax.dynamic_slice_in_dim(lax.psum(packed, "c"), c, 1, 0)
-    packed = lax.all_to_all(jnp.broadcast_to(packed[None], (NZ, 1, 1152)), "z", 0, 0)
+        core, row_sums, row_moments, weight_sq.reshape(1, 1), gradient, swapped
+    )
+    packed = lax.all_to_all(packed, "z", 0, 0)
     half_moment = jnp.where(c == 0, col_moment[:512], col_moment[512:])
     half_cols, row_mean, last = columns_call(packed, half_moment[None])
     last = lax.all_to_all(last, ("x", "y", "c"), 0, 0)
     new_cols = lax.all_gather(half_cols, "c", axis=0)
-    new_weight, update, new_cols = update_call(last, row_mean, row_factor, new_cols, gradient, weight)
+    new_weight, update, new_cols = update_call(
+        last, row_mean, row_factor, new_cols, gradient, weight
+    )
     return (new_weight, update, new_rows[0], new_cols.reshape(1024))
 
 

time: 173 us -> 171 us (0.988)
  blocking collectives: 17.8 us -> 31.2 us
  waiting for transfers between devices: 50.9 us -> 41.8 us
  starting transfers between devices: 62.2 us -> 57.2 us
  local copies, waits for them, and re-layouts: 8.93 us -> 4.55 us
  Pallas kernels: 12 us -> 14.1 us
    all_to_all x0 -> x1, blocking collectives: none -> 14.8 us  [on_device(): row_sums = lax.all_to_all(row_sums, ('x', 'y', 'c'), 0, 0)]
    all_to_all x2 -> x1, starting transfers between devices: 13.6 us -> 6.46 us  [on_device(): packed = lax.all_to_all(packed, 'z', 0, 0)]
    all_to_all x2 -> x1, waiting for transfers between devices: 18.2 us -> 11.7 us  [on_device(): packed = lax.all_to_all(packed, 'z', 0, 0)]
    psum x1 -> x0, blocking collectives: 3.87 us -> none  [on_device(): packed = lax.dynamic_slice_in_dim(lax.psum(packed, 'c'), c, 1, 0)]
    unnamed x12 -> x6, local copies, waits for them, and re-layouts: 4.68 us -> 1 us
    all_to_all x1, waiting for transfers between devices: 10.1 us -> 7.69 us  [features_of_rows(): part = lax.all_to_all(part.transpose(1, 0, 2), 'z', 0, 0)]
    all_gather x0 -> x1, blocking collectives: none -> 2.42 us  [on_device(): lax.all_gather(row_moment[None], 'c', axis=0)]
    ppermute x0 -> x1, starting transfers between devices: none -> 2.15 us  [on_device(): swapped = lax.ppermute(swapped, 'c', pairs(2, 1))]
  transfers between devices with their start and end apart: 12 -> 12, of which waited for: 10 -> 9; matrix products, arithmetic and copies ran while one was open for 6% -> 6% of each run, Pallas kernels for 0% -> 0%
where the time goes in v4:
time: 171 us; the launch traced here: 170 us
  starting transfers between devices  57.2 us (33%)
  waiting for transfers between devices  41.8 us (24%)
  blocking collectives  31.2 us (18%)
  between operations  14.2 us (8%)
  Pallas kernels  14.1 us (8%)
  other arithmetic  6.6 us (4%)
  local copies, waits for them, and re-layouts  4.55 us (3%)
    ppermute x6, starting transfers between devices, swap(): return lax.ppermute(block, 'y', pairs(NY, flip))  18.7 us
    all_to_all x1, starting transfers between devices, features_of_rows(): part = lax.all_to_all(part.transpose(1, 0, 2), 'z', 0, 0)  15.7 us
    all_to_all x1, blocking collectives, on_device(): row_sums = lax.all_to_all(row_sums, ('x', 'y', 'c'), 0, 0)  14.8 us
    ppermute x6, waiting for transfers between devices, swap(): return lax.ppermute(block, 'y', pairs(NY, flip))  12.9 us
    all_gather x1, blocking collectives, features_of_rows(): part = lax.all_gather(part, 'x', axis=0)  12.1 us
    all_to_all x1, waiting for transfers between devices, on_device(): packed = lax.all_to_all(packed, 'z', 0, 0)  11.7 us
    ppermute x1, starting transfers between devices, features_of_rows(): other = lax.ppermute(jnp.where(c == 0, high, low), 'c', pairs(2, 1))  8.58 us
    pallas_call x1, Pallas kernels, gradient_of(): pl.pallas_call(gradient_kernel, grid=(NZ // PLANES,), in_specs=[SMEM, fea...  8.24 us
  transfers between devices with their start and end apart: 12, of which 9 were waited for; matrix products, arithmetic and copies ran while one was open for 6% of the time, Pallas kernels for 0%

profile of v4, /device:TPU:1, one launch (start us, length us, event | category | flops | bytes accessed | tf_op | source)
XLA Modules:
  0.0 169.7 jit_solution(7067759756934686646)
XLA Ops:
  7.2 0.0 copy-start
  7.2 0.0 copy-start.2
  7.2 0.0 all-gather.8.cloned.1.call-start
  7.2 0.7 all-gather.8.cloned.1.call-update
  7.9 1.0 copy-done
  9.0 1.3 reshape.24
  10.3 1.4 constant_dynamic-slice_fusion
  11.7 0.8 copy.16
  12.5 15.7 %all-to-all-start = ((bf16[16,40,128]{2,1,0:T(8,128)(2,1)}), bf16[16,40,128]{2,1,0:T(8,128)(2,1)S(1)}, u32[]{:S(2)}, u32[]{:S(2)}) async-start(bf16[16,40,128]{2,1,0:T(8,128)(2,1)} %bitcast.15), calls=%async_computation | async-start | bytes 327680 | tf_op jit(solution)/shard_map/all_to_all | solution.py:38
  28.2 0.0 copy-done.2
  28.2 2.4 %all-gather.4.moment_ref = f32[2,1,256]{2,1,0:T(1,128)S(1)} all-gather(f32[1,1,256]{2,1,0:T(1,128)S(1)} %bitcast.21), channel_id=2, replica_groups=mesh['x'=4,'y'=4,'z'=16,'c'=2] {'c'}, dimensions={0}, use_global_device_ids=true | all-gather | bytes 3072 | tf_op jit(solution)/shard_map/all_gather | solution.py:282
  30.7 2.1 %multiply_reduce_fusion = f32[]{:T(128)} fusion(f32[256,1024]{1,0:T(8,128)} %weight_hbm.1), kind=kLoop, calls=%fused_computation.2 | loop fusion | flops 524287 | bytes 1048580 | tf_op jit(solution)/shard_map/reduce_sum | solution.py:282
  32.8 7.7 %all-to-all-done = bf16[16,40,128]{2,1,0:T(8,128)(2,1)S(1)} async-done(((bf16[16,40,128]{2,1,0:T(8,128)(2,1)}), bf16[16,40,128]{2,1,0:T(8,128)(2,1)S(1)}, u32[]{:S(2)}, u32[]{:S(2)}) %all-to-all-start) | async-done | bytes 163872 | tf_op jit(solution)/shard_map/all_to_all | solution.py:38
  40.5 12.1 %all-gather.1 = bf16[64,40,128]{2,1,0:T(8,128)(2,1)S(1)} all-gather(bf16[16,40,128]{2,1,0:T(8,128)(2,1)S(1)} %all-to-all-done), channel_id=3, replica_groups=mesh['x'=4,'y'=4,'z'=16,'c'=2] {'x'}, dimensions={0}, use_global_device_ids=true | all-gather | bytes 819200 | tf_op jit(solution)/shard_map/all_gather | solution.py:40
  52.6 8.6 %collective-permute-start = (bf16[2,16,40,128]{3,2,1,0:T(8,128)(2,1)S(1)}, bf16[2,16,40,128]{3,2,1,0:T(8,128)(2,1)S(1)}, u32[]{:S(2)}, u32[]{:S(2)}) collective-permute-start(bf16[2,16,40,128]{3,2,1,0:T(8,128)(2,1)S(1)} %bitcast.20), channel_id=1, source_target_pairs={{0,1},{1,0},{2,3},{3,2},{4,5},{5,4},{6,7},{7,6},{8,9},{9,8},{10,11... | collective-permute-start | bytes 983048 | tf_op jit(solution)/shard_map/ppermute | solution.py:43
  61.2 1.2 collective-permute-done
  62.5 5.1 %collective-permute-start.4 = (bf16[2,16,40,128]{3,2,1,0:T(8,128)(2,1)S(1)}, bf16[2,16,40,128]{3,2,1,0:T(8,128)(2,1)}, u32[]{:S(2)}, u32[]{:S(2)}) collective-permute-start(bf16[2,16,40,128]{3,2,1,0:T(8,128)(2,1)S(1)} %get-tuple-element.42), channel_id=1, source_target_pairs={{0,96},{32,64},{64,32},{96,0},{1,97},{33,65},{65,33},{97,1},{2,98}... | collective-permute-start | bytes 983048 | tf_op jit(solution)/shard_map/ppermute | solution.py:47
  67.6 1.9 %collective-permute-start.2 = (bf16[2,16,40,128]{3,2,1,0:T(8,128)(2,1)S(1)}, bf16[2,16,40,128]{3,2,1,0:T(8,128)(2,1)}, u32[]{:S(2)}, u32[]{:S(2)}) collective-permute-start(bf16[2,16,40,128]{3,2,1,0:T(8,128)(2,1)S(1)} %get-tuple-element.43), channel_id=1, source_target_pairs={{0,32},{32,0},{64,96},{96,64},{1,33},{33,1},{65,97},{97,65},{2,34}... | collective-permute-start | bytes 983048 | tf_op jit(solution)/shard_map/ppermute | solution.py:47
  69.5 3.4 %collective-permute-start.6 = (bf16[2,16,40,128]{3,2,1,0:T(8,128)(2,1)S(1)}, bf16[2,16,40,128]{3,2,1,0:T(8,128)(2,1)}, u32[]{:S(2)}, u32[]{:S(2)}) collective-permute-start(bf16[2,16,40,128]{3,2,1,0:T(8,128)(2,1)S(1)} %get-tuple-element.42), channel_id=1, source_target_pairs={{0,32},{32,0},{64,96},{96,64},{1,33},{33,1},{65,97},{97,65},{2,34}... | collective-permute-start | bytes 983048 | tf_op jit(solution)/shard_map/ppermute | solution.py:47
  72.9 2.6 %collective-permute-done.4 = bf16[2,16,40,128]{3,2,1,0:T(8,128)(2,1)} collective-permute-done((bf16[2,16,40,128]{3,2,1,0:T(8,128)(2,1)S(1)}, bf16[2,16,40,128]{3,2,1,0:T(8,128)(2,1)}, u32[]{:S(2)}, u32[]{:S(2)}) %collective-permute-start.4) | collective-permute-done | bytes 327712 | tf_op jit(solution)/shard_map/ppermute | solution.py:47
  75.4 1.9 %collective-permute-start.5 = (bf16[2,16,40,128]{3,2,1,0:T(8,128)(2,1)}, bf16[2,16,40,128]{3,2,1,0:T(8,128)(2,1)}, u32[]{:S(2)}, u32[]{:S(2)}) collective-permute-start(bf16[2,16,40,128]{3,2,1,0:T(8,128)(2,1)} %collective-permute-done.4), channel_id=1, source_target_pairs={{0,32},{32,0},{64,96},{96,64},{1,33},{33,1},{65,97},{97,65},{2,34}... | collective-permute-start | bytes 983048 | tf_op jit(solution)/shard_map/ppermute | solution.py:47
  77.4 4.3 %collective-permute-start.1 = (bf16[2,16,40,128]{3,2,1,0:T(8,128)(2,1)S(1)}, bf16[2,16,40,128]{3,2,1,0:T(8,128)(2,1)}, u32[]{:S(2)}, u32[]{:S(2)}) collective-permute-start(bf16[2,16,40,128]{3,2,1,0:T(8,128)(2,1)S(1)} %get-tuple-element.43), channel_id=1, source_target_pairs={{0,96},{32,64},{64,32},{96,0},{1,97},{33,65},{65,33},{97,1},{2,98}... | collective-permute-start | bytes 983048 | tf_op jit(solution)/shard_map/ppermute | solution.py:47
  81.6 0.0 collective-permute-done.2
  81.6 2.2 %collective-permute-start.3 = (bf16[2,16,40,128]{3,2,1,0:T(8,128)(2,1)}, bf16[2,16,40,128]{3,2,1,0:T(8,128)(2,1)}, u32[]{:S(2)}, u32[]{:S(2)}) collective-permute-start(bf16[2,16,40,128]{3,2,1,0:T(8,128)(2,1)} %collective-permute-done.2), channel_id=1, source_target_pairs={{0,96},{32,64},{64,32},{96,0},{1,97},{33,65},{65,33},{97,1},{2,98}... | collective-permute-start | bytes 983048 | tf_op jit(solution)/shard_map/ppermute | solution.py:47
  83.9 1.3 collective-permute-done.6
  85.2 7.0 %collective-permute-done.5 = bf16[2,16,40,128]{3,2,1,0:T(8,128)(2,1)} collective-permute-done((bf16[2,16,40,128]{3,2,1,0:T(8,128)(2,1)}, bf16[2,16,40,128]{3,2,1,0:T(8,128)(2,1)}, u32[]{:S(2)}, u32[]{:S(2)}) %collective-permute-start.5) | collective-permute-done | bytes 327712 | tf_op jit(solution)/shard_map/ppermute | solution.py:47
  92.2 1.3 broadcast_select_fusion.15
  93.6 0.0 collective-permute-done.1
  93.6 2.0 %collective-permute-done.3 = bf16[2,16,40,128]{3,2,1,0:T(8,128)(2,1)} collective-permute-done((bf16[2,16,40,128]{3,2,1,0:T(8,128)(2,1)}, bf16[2,16,40,128]{3,2,1,0:T(8,128)(2,1)}, u32[]{:S(2)}, u32[]{:S(2)}) %collective-permute-start.3) | collective-permute-done | bytes 327712 | tf_op jit(solution)/shard_map/ppermute | solution.py:47
  95.6 1.3 broadcast_select_fusion.19
  96.9 1.7 %pad_maximum_fusion = (bf16[2,16,160,128]{3,2,1,0:T(8,128)(2,1)}, bf16[2,16,160,128]{3,2,1,0:T(8,128)(2,1)}) fusion(bf16[2,16,40,128]{3,2,1,0:T(8,128)(2,1)S(1)} %get-tuple-element.41, bf16[2,16,40,128]{3,2,1,0:T(8,128)(2,1)S(1)} %get-tuple-element.40, bf16[2,16,40,128]{3,2,1,0:T(8,128)(2,1)S(1)} %get-tuple-element.39, ...), kind=kLoop, calls=%fused_computation | loop fusion | flops 10485760 | bytes 5242880 | tf_op jit(solution)/shard_map/concatenate | solution.py:29
  98.6 2.4 %all-gather.8.cloned.1.call-done = bf16[5120,1024]{1,0:T(8,128)(2,1)} async-done(((bf16[160,1024]{1,0:T(8,128)(2,1)}), bf16[5120,1024]{1,0:T(8,128)(2,1)}) %all-gather.8.cloned.1.call-update) | async-done | bytes 10485776 | tf_op jit(solution)/shard_map/all_gather | solution.py:281
  101.1 0.0 copy-start.1
  101.1 8.2 %gradient.1 = (f32[256,1024]{1,0:T(8,128)}, f32[32,1,256]{2,1,0:T(1,128)}, f32[256,512]{1,0:T(8,128)}) custom-call(s32[1,1]{1,0:T(1,128)} %bitcast.core_ref, bf16[2,16,160,128]{3,2,1,0:T(8,128)(2,1)} %get-tuple-element.46.first_ref, bf16[2,16,160,128]{3,2,1,0:T(8,128)(2,1)} %get-tuple-element.47.second_ref, bf16[16,2,160,1024]{3,2,1,0:T(8,128)(2,1)} %bitcast.18), custom_call_target="tpu_custom_call" | custom-call | flops 2684354560 | bytes 15000000 | tf_op jit(solution)/shard_map/gradient/pallas_call | solution.py:106
  109.3 2.2 %collective-permute-start.7 = (f32[256,512]{1,0:T(8,128)}, f32[256,512]{1,0:T(8,128)S(1)}, u32[]{:S(2)}, u32[]{:S(2)}) collective-permute-start(f32[256,512]{1,0:T(8,128)} %get-tuple-element.24), channel_id=1, source_target_pairs={{0,1},{1,0},{2,3},{3,2},{4,5},{5,4},{6,7},{7,6},{8,9},{9,8},{10,11... | collective-permute-start | bytes 1572872 | tf_op jit(solution)/shard_map/ppermute | solution.py:286
  111.5 14.8 %all_to_all.20.got_ref = f32[32,1,256]{2,1,0:T(1,128)S(1)} all-to-all(f32[32,1,256]{2,1,0:T(1,128)} %get-tuple-element.20), channel_id=1, replica_groups=mesh['x'=4,'y'=4,'z'=16,'c'=2] {'x','y','c'}, dimensions={0} | all-to-all | bytes 65536 | tf_op jit(solution)/shard_map/all_to_all | solution.py:285
  126.3 0.0 collective-permute-done.7.swapped_ref
  126.3 2.6 %rows.1 = (f32[1,256]{1,0:T(1,128)}, f32[256,128]{1,0:T(8,128)S(1)}, f32[16,1,1152]{2,1,0:T(1,128)}) custom-call(s32[1,1]{1,0:T(1,128)} %bitcast.core_ref, f32[32,1,256]{2,1,0:T(1,128)S(1)} %all_to_all.20.got_ref, f32[2,1,256]{2,1,0:T(1,128)S(1)} %all-gather.4.moment_ref, f32[1,1]{1,0:T(1,128)} %bitcast.6.weight_sq_ref, ...), custom_call_target="tpu_custom_call" | custom-call | tf_op jit(solution)/shard_map/rows/pallas_call | solution.py:165
  128.9 6.5 %all-to-all-start.2 = ((f32[16,1,1152]{2,1,0:T(1,128)}), f32[16,1,1152]{2,1,0:T(1,128)S(1)}, u32[]{:S(2)}, u32[]{:S(2)}) async-start(f32[16,1,1152]{2,1,0:T(1,128)} %get-tuple-element.25), calls=%async_computation.2 | async-start | bytes 147456 | tf_op jit(solution)/shard_map/all_to_all | solution.py:290
  135.3 0.0 copy-done.1
  135.4 11.7 %all-to-all-done.2.got_ref = f32[16,1,1152]{2,1,0:T(1,128)S(1)} async-done(((f32[16,1,1152]{2,1,0:T(1,128)}), f32[16,1,1152]{2,1,0:T(1,128)S(1)}, u32[]{:S(2)}, u32[]{:S(2)}) %all-to-all-start.2) | async-done | bytes 73760 | tf_op jit(solution)/shard_map/all_to_all | solution.py:290
  147.1 0.8 columns.1
  147.9 5.5 %all-to-all-start.3 = ((f32[32,1,128]{2,1,0:T(1,128)}), f32[32,1,128]{2,1,0:T(1,128)S(1)}, u32[]{:S(2)}, u32[]{:S(2)}) async-start(f32[32,1,128]{2,1,0:T(1,128)} %get-tuple-element.26), calls=%async_computation.3 | async-start | bytes 32768 | tf_op jit(solution)/shard_map/all_to_all | solution.py:293
  153.4 1.8 %all-gather.5.cols_ref = f32[2,1,512]{2,1,0:T(1,128)S(1)} all-gather(f32[1,1,512]{2,1,0:T(1,128)S(1)} %bitcast.17), channel_id=5, replica_groups=mesh['x'=4,'y'=4,'z'=16,'c'=2] {'c'}, dimensions={0}, use_global_device_ids=true | all-gather | bytes 6144 | tf_op jit(solution)/shard_map/all_gather | solution.py:294
  155.2 5.2 %all-to-all-done.3.got_ref = f32[32,1,128]{2,1,0:T(1,128)S(1)} async-done(((f32[32,1,128]{2,1,0:T(1,128)}), f32[32,1,128]{2,1,0:T(1,128)S(1)}, u32[]{:S(2)}, u32[]{:S(2)}) %all-to-all-start.3) | async-done | bytes 16416 | tf_op jit(solution)/shard_map/all_to_all | solution.py:293
  160.4 2.4 %update.1 = (f32[256,1024]{1,0:T(8,128)}, bf16[256,1024]{1,0:T(8,128)(2,1)}, f32[2,1,512]{2,1,0:T(1,128)}) custom-call(f32[32,1,128]{2,1,0:T(1,128)S(1)} %all-to-all-done.3.got_ref, f32[1,128]{1,0:T(1,128)S(1)} %get-tuple-element.27.mean_ref, f32[256,128]{1,0:T(8,128)S(1)} %get-tuple-element.28.factor_ref, f32[2,1,512]{2,1,0:T(1,128)S(1)} %all-gather.5.cols_ref, ...), custom_call_target="tpu_custom_call" | custom-call | tf_op jit(solution)/shard_map/update/pallas_call | solution.py:255
  (4 shorter events, 0.1 us)
Async XLA Ops:
  7.2 1.7 %copy-start = (bf16[160,8192]{1,0:T(8,128)(2,1)S(1)}, bf16[160,8192]{1,0:T(8,128)(2,1)}, u32[]{:S(2)}) copy-start(bf16[160,8192]{1,0:T(8,128)(2,1)} %param.5) | copy-start | bytes 7864324
  7.2 21.1 %copy-start.2 = (f32[256]{0:T(256)S(1)}, f32[256]{0:T(256)}, u32[]{:S(2)}) copy-start(f32[256]{0:T(256)} %param.8) | copy-start | bytes 3076
  7.2 93.9 %all-gather.8.cloned.1.call-start = ((), (), s32[]{:S(2)}) async-start(), calls=%async_computation.4 | async-start | bytes 10813440 | tf_op jit(solution)/shard_map/all_gather | solution.py:281
  12.5 28.0 %all-to-all-start = ((bf16[16,40,128]{2,1,0:T(8,128)(2,1)}), bf16[16,40,128]{2,1,0:T(8,128)(2,1)S(1)}, u32[]{:S(2)}, u32[]{:S(2)}) async-start(bf16[16,40,128]{2,1,0:T(8,128)(2,1)} %bitcast.15), calls=%async_computation | async-start | bytes 327680 | tf_op jit(solution)/shard_map/all_to_all | solution.py:38
  52.6 9.8 %collective-permute-start = (bf16[2,16,40,128]{3,2,1,0:T(8,128)(2,1)S(1)}, bf16[2,16,40,128]{3,2,1,0:T(8,128)(2,1)S(1)}, u32[]{:S(2)}, u32[]{:S(2)}) collective-permute-start(bf16[2,16,40,128]{3,2,1,0:T(8,128)(2,1)S(1)} %bitcast.20), channel_id=1, source_target_pairs={{0,1},{1,0},{2,3},{3,2},{4,5},{5,4},{6,7},{7,6},{8,9},{9,8},{10,11... | collective-permute-start | bytes 983048 | tf_op jit(solution)/shard_map/ppermute | solution.py:43
  62.5 12.9 %collective-permute-start.4 = (bf16[2,16,40,128]{3,2,1,0:T(8,128)(2,1)S(1)}, bf16[2,16,40,128]{3,2,1,0:T(8,128)(2,1)}, u32[]{:S(2)}, u32[]{:S(2)}) collective-permute-start(bf16[2,16,40,128]{3,2,1,0:T(8,128)(2,1)S(1)} %get-tuple-element.42), channel_id=1, source_target_pairs={{0,96},{32,64},{64,32},{96,0},{1,97},{33,65},{65,33},{97,1},{2,98}... | collective-permute-start | bytes 983048 | tf_op jit(solution)/shard_map/ppermute | solution.py:47
  67.6 14.1 %collective-permute-start.2 = (bf16[2,16,40,128]{3,2,1,0:T(8,128)(2,1)S(1)}, bf16[2,16,40,128]{3,2,1,0:T(8,128)(2,1)}, u32[]{:S(2)}, u32[]{:S(2)}) collective-permute-start(bf16[2,16,40,128]{3,2,1,0:T(8,128)(2,1)S(1)} %get-tuple-element.43), channel_id=1, source_target_pairs={{0,32},{32,0},{64,96},{96,64},{1,33},{33,1},{65,97},{97,65},{2,34}... | collective-permute-start | bytes 983048 | tf_op jit(solution)/shard_map/ppermute | solution.py:47
  69.5 15.7 %collective-permute-start.6 = (bf16[2,16,40,128]{3,2,1,0:T(8,128)(2,1)S(1)}, bf16[2,16,40,128]{3,2,1,0:T(8,128)(2,1)}, u32[]{:S(2)}, u32[]{:S(2)}) collective-permute-start(bf16[2,16,40,128]{3,2,1,0:T(8,128)(2,1)S(1)} %get-tuple-element.42), channel_id=1, source_target_pairs={{0,32},{32,0},{64,96},{96,64},{1,33},{33,1},{65,97},{97,65},{2,34}... | collective-permute-start | bytes 983048 | tf_op jit(solution)/shard_map/ppermute | solution.py:47
  75.4 16.8 %collective-permute-start.5 = (bf16[2,16,40,128]{3,2,1,0:T(8,128)(2,1)}, bf16[2,16,40,128]{3,2,1,0:T(8,128)(2,1)}, u32[]{:S(2)}, u32[]{:S(2)}) collective-permute-start(bf16[2,16,40,128]{3,2,1,0:T(8,128)(2,1)} %collective-permute-done.4), channel_id=1, source_target_pairs={{0,32},{32,0},{64,96},{96,64},{1,33},{33,1},{65,97},{97,65},{2,34}... | collective-permute-start | bytes 983048 | tf_op jit(solution)/shard_map/ppermute | solution.py:47
  77.4 16.2 %collective-permute-start.1 = (bf16[2,16,40,128]{3,2,1,0:T(8,128)(2,1)S(1)}, bf16[2,16,40,128]{3,2,1,0:T(8,128)(2,1)}, u32[]{:S(2)}, u32[]{:S(2)}) collective-permute-start(bf16[2,16,40,128]{3,2,1,0:T(8,128)(2,1)S(1)} %get-tuple-element.43), channel_id=1, source_target_pairs={{0,96},{32,64},{64,32},{96,0},{1,97},{33,65},{65,33},{97,1},{2,98}... | collective-permute-start | bytes 983048 | tf_op jit(solution)/shard_map/ppermute | solution.py:47
  81.6 14.0 %collective-permute-start.3 = (bf16[2,16,40,128]{3,2,1,0:T(8,128)(2,1)}, bf16[2,16,40,128]{3,2,1,0:T(8,128)(2,1)}, u32[]{:S(2)}, u32[]{:S(2)}) collective-permute-start(bf16[2,16,40,128]{3,2,1,0:T(8,128)(2,1)} %collective-permute-done.2), channel_id=1, source_target_pairs={{0,96},{32,64},{64,32},{96,0},{1,97},{33,65},{65,33},{97,1},{2,98}... | collective-permute-start | bytes 983048 | tf_op jit(solution)/shard_map/ppermute | solution.py:47
  101.1 34.2 %copy-start.1 = (f32[1024]{0:T(1024)S(1)}, f32[1024]{0:T(1024)}, u32[]{:S(2)}) copy-start(f32[1024]{0:T(1024)} %param.9) | copy-start | bytes 12292
  109.3 16.9 %collective-permute-start.7 = (f32[256,512]{1,0:T(8,128)}, f32[256,512]{1,0:T(8,128)S(1)}, u32[]{:S(2)}, u32[]{:S(2)}) collective-permute-start(f32[256,512]{1,0:T(8,128)} %get-tuple-element.24), channel_id=1, source_target_pairs={{0,1},{1,0},{2,3},{3,2},{4,5},{5,4},{6,7},{7,6},{8,9},{9,8},{10,11... | collective-permute-start | bytes 1572872 | tf_op jit(solution)/shard_map/ppermute | solution.py:286
  128.9 18.2 %all-to-all-start.2 = ((f32[16,1,1152]{2,1,0:T(1,128)}), f32[16,1,1152]{2,1,0:T(1,128)S(1)}, u32[]{:S(2)}, u32[]{:S(2)}) async-start(f32[16,1,1152]{2,1,0:T(1,128)} %get-tuple-element.25), calls=%async_computation.2 | async-start | bytes 147456 | tf_op jit(solution)/shard_map/all_to_all | solution.py:290
  147.9 12.5 %all-to-all-start.3 = ((f32[32,1,128]{2,1,0:T(1,128)}), f32[32,1,128]{2,1,0:T(1,128)S(1)}, u32[]{:S(2)}, u32[]{:S(2)}) async-start(f32[32,1,128]{2,1,0:T(1,128)} %get-tuple-element.26), calls=%async_computation.3 | async-start | bytes 32768 | tf_op jit(solution)/shard_map/all_to_all | solution.py:293
Sparse Core Ops, SparseCore 0:
  10.1 90.8 all-gather.7

commit v5 on v4

--- a/solution.py
+++ b/solution.py
@@ -56,38 +56,59 @@
     )
 
 
-PLANES = 4
-
-
-def gradient_kernel(core_ref, first_ref, second_ref, cot_ref, grad_ref, rows_ref, other_ref):
-    step = pl.program_id(0)
-
-    @pl.when(step == 0)
-    def _():
-        grad_ref[...] = jnp.zeros_like(grad_ref)
-
-    feat = [
-        jnp.concatenate([ref[0, plane], ref[1, plane]], axis=1)
-        for plane in range(PLANES)
-        for ref in (first_ref, second_ref)
+CHUNKS = ((0, 2), (2, 4), (6, 4), (10, 4), (14, 2))
+
+
+def gradient_kernel(
+    core_ref, first_hbm, second_hbm, cot_hbm, grad_hbm, rows_ref, other_hbm,
+    first, second, cot, grad, in_sems, out_sems,
+):
+    fetches = []
+    for i, (start, count) in enumerate(CHUNKS):
+        planes = pl.ds(start, count)
+        fetches.append(
+            [
+                pltpu.make_async_copy(first_hbm.at[:, planes], first.at[:, planes], in_sems.at[0, i]),
+                pltpu.make_async_copy(second_hbm.at[:, planes], second.at[:, planes], in_sems.at[1, i]),
+                pltpu.make_async_copy(cot_hbm.at[planes], cot.at[planes], in_sems.at[2, i]),
+            ]
+        )
+        for fetch in fetches[i]:
+            fetch.start()
+    for i, (start, count) in enumerate(CHUNKS):
+        for fetch in fetches[i]:
+            fetch.wait()
+        feat = [
+            jnp.concatenate([ref[0, plane], ref[1, plane]], axis=1)
+            for plane in range(start, start + count)
+            for ref in (first, second)
+        ]
+        part = lax.dot_general(
+            jnp.concatenate(feat, axis=0),
+            cot[start : start + count].reshape(count * 320, 1024),
+            (((0,), (0,)), ((), ())),
+            preferred_element_type=jnp.float32,
+        )
+        if i == 0:
+            grad[...] = part
+        else:
+            grad[...] += part
+    columns = pl.ds(pl.multiple_of(512 * (1 - core_ref[0, 0]), 512), 512)
+    stores = [
+        pltpu.make_async_copy(grad.at[:, columns], other_hbm, out_sems.at[0]),
+        pltpu.make_async_copy(grad, grad_hbm, out_sems.at[1]),
     ]
-    grad_ref[...] += lax.dot_general(
-        jnp.concatenate(feat, axis=0),
-        cot_ref[...].reshape(PLANES * 320, 1024),
-        (((0,), (0,)), ((), ())),
-        preferred_element_type=jnp.float32,
-    )
-
-    @pl.when(step == pl.num_programs(0) - 1)
-    def _():
-        squares = jnp.zeros((256, 128), jnp.float32)
-        for j in range(8):
-            part = grad_ref[:, j * 128 : (j + 1) * 128]
-            squares += part * part + tiny_eps
-        row = jnp.sum(squares.T, axis=0, keepdims=True)
-        for i in range(2 * NX * NY):
-            rows_ref[i] = row
-        other_ref[...] = grad_ref[:, pl.ds(pl.multiple_of(512 * (1 - core_ref[0, 0]), 512), 512)]
+    for store in stores:
+        store.start()
+    squares = jnp.zeros((256, 128), jnp.float32)
+    for j in range(8):
+        part = grad[:, j * 128 : (j + 1) * 128]
+        squares += part * part + tiny_eps
+    row = jnp.sum(squares.T, axis=0, keepdims=True)
+    for i in range(2 * NX * NY):
+        rows_ref[i] = row
+    for store in stores:
+        store.wait()
 
 
 LARGE = pltpu.CompilerParams(vmem_limit_bytes=56 * 2**20)
@@ -101,21 +122,22 @@
 
 
 def gradient_of(core, first, second, all_cotangent):
-    feat_spec = pl.BlockSpec((2, PLANES, 160, 128), lambda i: (0, i, 0, 0))
-    cot_spec = pl.BlockSpec((PLANES, 2, 160, 1024), lambda i: (i, 0, 0, 0))
     return pl.pallas_call(
         gradient_kernel,
-        grid=(NZ // PLANES,),
-        in_specs=[SMEM, feat_spec, feat_spec, cot_spec],
-        out_specs=[
-            pl.BlockSpec((256, 1024), lambda i: (0, 0)),
-            pl.BlockSpec((2 * NX * NY, 1, 256), lambda i: (0, 0, 0)),
-            pl.BlockSpec((256, 512), lambda i: (0, 0)),
-        ],
+        in_specs=[SMEM, HBM, HBM, HBM],
+        out_specs=[HBM, VMEM, HBM],
         out_shape=[
             jax.ShapeDtypeStruct((256, 1024), jnp.float32),
             jax.ShapeDtypeStruct((2 * NX * NY, 1, 256), jnp.float32),
             jax.ShapeDtypeStruct((256, 512), jnp.float32),
+        ],
+        scratch_shapes=[
+            pltpu.VMEM(first.shape, first.dtype),
+            pltpu.VMEM(second.shape, second.dtype),
+            pltpu.VMEM(all_cotangent.shape, all_cotangent.dtype),
+            pltpu.VMEM((256, 1024), jnp.float32),
+            pltpu.SemaphoreType.DMA((3, len(CHUNKS))),
+            pltpu.SemaphoreType.DMA((2,)),
         ],
         cost_estimate=pl.CostEstimate(
             flops=2 * 256 * 1024 * 5120, bytes_accessed=15_000_000, transcendentals=0
@@ -126,12 +148,16 @@
 
 
 def rows_kernel(
-    core_ref, got_ref, moment_ref, weight_sq_ref, grad_hbm, swapped_ref, new_rows_ref, factor_ref, out_ref, grad, sem
+    core_ref, got_ref, moment_ref, weight_sq_ref, grad_hbm, swapped_ref, new_rows_ref, factor_ref, out_ref, grad, sems
 ):
     core = core_ref[0, 0]
     columns = pl.ds(pl.multiple_of(512 * core, 512), 512)
-    fetch = pltpu.make_async_copy(grad_hbm.at[:, columns], grad, sem)
-    fetch.start()
+    fetches = [
+        pltpu.make_async_copy(grad_hbm.at[rows, columns], grad.at[rows], sems.at[i])
+        for i, rows in enumerate((pl.ds(0, 128), pl.ds(128, 128)))
+    ]
+    for fetch in fetches:
+        fetch.start()
     new_rows = []
     for half in range(2):
         total = got_ref[half]
@@ -148,7 +174,8 @@
     lanes = lax.broadcasted_iota(jnp.int32, (1, 128), 1)
     rows_sum = jnp.sum(own + other, axis=1, keepdims=True)
     scalars = jnp.where(lanes == 0, rows_sum, jnp.where(lanes == 1, weight_sq_ref[0, 0], 0.0))
-    fetch.wait()
+    for fetch in fetches:
+        fetch.wait()
     squares, weighted = [], []
     for j in range(4):
         here = slice(128 * j, 128 * (j + 1))
@@ -171,7 +198,7 @@
             jax.ShapeDtypeStruct((256, 128), jnp.float32),
             jax.ShapeDtypeStruct((NZ, 1, 1152), jnp.float32),
         ],
-        scratch_shapes=[pltpu.VMEM((256, 512), jnp.float32), pltpu.SemaphoreType.DMA],
+        scratch_shapes=[pltpu.VMEM((256, 512), jnp.float32), pltpu.SemaphoreType.DMA((2,))],
         compiler_params=STREAM,
         name="rows",
     )(core, row_sums, row_moment, weight_sq, gradient, swapped)

time: 171 us -> 170 us (level)
  no operation moved by 1% of the time
where the time goes in v5:
time: 170 us; the launch traced here: 169 us
  starting transfers between devices  57.2 us (34%)
  waiting for transfers between devices  41.8 us (25%)
  blocking collectives  31.2 us (18%)
  between operations  14.3 us (8%)
  Pallas kernels  13.5 us (8%)
  other arithmetic  6.6 us (4%)
  local copies, waits for them, and re-layouts  4.55 us (3%)
    ppermute x6, starting transfers between devices, swap(): return lax.ppermute(block, 'y', pairs(NY, flip))  18.7 us
    all_to_all x1, starting transfers between devices, features_of_rows(): part = lax.all_to_all(part.transpose(1, 0, 2), 'z', 0, 0)  15.7 us
    all_to_all x1, blocking collectives, on_device(): row_sums = lax.all_to_all(row_sums, ('x', 'y', 'c'), 0, 0)  14.8 us
    ppermute x6, waiting for transfers between devices, swap(): return lax.ppermute(block, 'y', pairs(NY, flip))  12.9 us
    all_gather x1, blocking collectives, features_of_rows(): part = lax.all_gather(part, 'x', axis=0)  12.1 us
    all_to_all x1, waiting for transfers between devices, on_device(): packed = lax.all_to_all(packed, 'z', 0, 0)  11.7 us
    ppermute x1, starting transfers between devices, features_of_rows(): other = lax.ppermute(jnp.where(c == 0, high, low), 'c', pairs(2, 1))  8.58 us
    pallas_call x1, Pallas kernels, gradient_of(): pl.pallas_call(gradient_kernel, in_specs=[SMEM, HBM, HBM, HBM], out_specs...  7.71 us
  transfers between devices with their start and end apart: 12, of which 9 were waited for; matrix products, arithmetic and copies ran while one was open for 6% of the time, Pallas kernels for 0%

profile of v5, /device:TPU:1, one launch (start us, length us, event | category | flops | bytes accessed | tf_op | source)
XLA Modules:
  0.0 169.2 jit_solution(11655413628761247322)
XLA Ops:
  7.2 0.0 copy-start
  7.2 0.0 copy-start.2
  7.2 0.0 all-gather.8.cloned.1.call-start
  7.2 0.7 all-gather.8.cloned.1.call-update
  7.9 1.0 copy-done
  9.0 1.3 reshape.24
  10.3 1.4 constant_dynamic-slice_fusion
  11.7 0.8 copy.16
  12.5 15.7 %all-to-all-start = ((bf16[16,40,128]{2,1,0:T(8,128)(2,1)}), bf16[16,40,128]{2,1,0:T(8,128)(2,1)S(1)}, u32[]{:S(2)}, u32[]{:S(2)}) async-start(bf16[16,40,128]{2,1,0:T(8,128)(2,1)} %bitcast.15), calls=%async_computation | async-start | bytes 327680 | tf_op jit(solution)/shard_map/all_to_all | solution.py:38
  28.2 0.0 copy-done.2
  28.2 2.4 %all-gather.4.moment_ref = f32[2,1,256]{2,1,0:T(1,128)S(1)} all-gather(f32[1,1,256]{2,1,0:T(1,128)S(1)} %bitcast.21), channel_id=2, replica_groups=mesh['x'=4,'y'=4,'z'=16,'c'=2] {'c'}, dimensions={0}, use_global_device_ids=true | all-gather | bytes 3072 | tf_op jit(solution)/shard_map/all_gather | solution.py:309
  30.7 2.1 %multiply_reduce_fusion = f32[]{:T(128)} fusion(f32[256,1024]{1,0:T(8,128)} %weight_hbm.1), kind=kLoop, calls=%fused_computation.2 | loop fusion | flops 524287 | bytes 1048580 | tf_op jit(solution)/shard_map/reduce_sum | solution.py:309
  32.8 7.7 %all-to-all-done = bf16[16,40,128]{2,1,0:T(8,128)(2,1)S(1)} async-done(((bf16[16,40,128]{2,1,0:T(8,128)(2,1)}), bf16[16,40,128]{2,1,0:T(8,128)(2,1)S(1)}, u32[]{:S(2)}, u32[]{:S(2)}) %all-to-all-start) | async-done | bytes 163872 | tf_op jit(solution)/shard_map/all_to_all | solution.py:38
  40.5 12.1 %all-gather.1 = bf16[64,40,128]{2,1,0:T(8,128)(2,1)S(1)} all-gather(bf16[16,40,128]{2,1,0:T(8,128)(2,1)S(1)} %all-to-all-done), channel_id=3, replica_groups=mesh['x'=4,'y'=4,'z'=16,'c'=2] {'x'}, dimensions={0}, use_global_device_ids=true | all-gather | bytes 819200 | tf_op jit(solution)/shard_map/all_gather | solution.py:40
  52.6 8.6 %collective-permute-start = (bf16[2,16,40,128]{3,2,1,0:T(8,128)(2,1)S(1)}, bf16[2,16,40,128]{3,2,1,0:T(8,128)(2,1)S(1)}, u32[]{:S(2)}, u32[]{:S(2)}) collective-permute-start(bf16[2,16,40,128]{3,2,1,0:T(8,128)(2,1)S(1)} %bitcast.20), channel_id=1, source_target_pairs={{0,1},{1,0},{2,3},{3,2},{4,5},{5,4},{6,7},{7,6},{8,9},{9,8},{10,11... | collective-permute-start | bytes 983048 | tf_op jit(solution)/shard_map/ppermute | solution.py:43
  61.2 1.2 collective-permute-done
  62.5 5.1 %collective-permute-start.4 = (bf16[2,16,40,128]{3,2,1,0:T(8,128)(2,1)S(1)}, bf16[2,16,40,128]{3,2,1,0:T(8,128)(2,1)}, u32[]{:S(2)}, u32[]{:S(2)}) collective-permute-start(bf16[2,16,40,128]{3,2,1,0:T(8,128)(2,1)S(1)} %get-tuple-element.42), channel_id=1, source_target_pairs={{0,96},{32,64},{64,32},{96,0},{1,97},{33,65},{65,33},{97,1},{2,98}... | collective-permute-start | bytes 983048 | tf_op jit(solution)/shard_map/ppermute | solution.py:47
  67.6 1.9 %collective-permute-start.2 = (bf16[2,16,40,128]{3,2,1,0:T(8,128)(2,1)S(1)}, bf16[2,16,40,128]{3,2,1,0:T(8,128)(2,1)}, u32[]{:S(2)}, u32[]{:S(2)}) collective-permute-start(bf16[2,16,40,128]{3,2,1,0:T(8,128)(2,1)S(1)} %get-tuple-element.43), channel_id=1, source_target_pairs={{0,32},{32,0},{64,96},{96,64},{1,33},{33,1},{65,97},{97,65},{2,34}... | collective-permute-start | bytes 983048 | tf_op jit(solution)/shard_map/ppermute | solution.py:47
  69.5 3.4 %collective-permute-start.6 = (bf16[2,16,40,128]{3,2,1,0:T(8,128)(2,1)S(1)}, bf16[2,16,40,128]{3,2,1,0:T(8,128)(2,1)}, u32[]{:S(2)}, u32[]{:S(2)}) collective-permute-start(bf16[2,16,40,128]{3,2,1,0:T(8,128)(2,1)S(1)} %get-tuple-element.42), channel_id=1, source_target_pairs={{0,32},{32,0},{64,96},{96,64},{1,33},{33,1},{65,97},{97,65},{2,34}... | collective-permute-start | bytes 983048 | tf_op jit(solution)/shard_map/ppermute | solution.py:47
  72.9 2.6 %collective-permute-done.4 = bf16[2,16,40,128]{3,2,1,0:T(8,128)(2,1)} collective-permute-done((bf16[2,16,40,128]{3,2,1,0:T(8,128)(2,1)S(1)}, bf16[2,16,40,128]{3,2,1,0:T(8,128)(2,1)}, u32[]{:S(2)}, u32[]{:S(2)}) %collective-permute-start.4) | collective-permute-done | bytes 327712 | tf_op jit(solution)/shard_map/ppermute | solution.py:47
  75.4 1.9 %collective-permute-start.5 = (bf16[2,16,40,128]{3,2,1,0:T(8,128)(2,1)}, bf16[2,16,40,128]{3,2,1,0:T(8,128)(2,1)}, u32[]{:S(2)}, u32[]{:S(2)}) collective-permute-start(bf16[2,16,40,128]{3,2,1,0:T(8,128)(2,1)} %collective-permute-done.4), channel_id=1, source_target_pairs={{0,32},{32,0},{64,96},{96,64},{1,33},{33,1},{65,97},{97,65},{2,34}... | collective-permute-start | bytes 983048 | tf_op jit(solution)/shard_map/ppermute | solution.py:47
  77.4 4.3 %collective-permute-start.1 = (bf16[2,16,40,128]{3,2,1,0:T(8,128)(2,1)S(1)}, bf16[2,16,40,128]{3,2,1,0:T(8,128)(2,1)}, u32[]{:S(2)}, u32[]{:S(2)}) collective-permute-start(bf16[2,16,40,128]{3,2,1,0:T(8,128)(2,1)S(1)} %get-tuple-element.43), channel_id=1, source_target_pairs={{0,96},{32,64},{64,32},{96,0},{1,97},{33,65},{65,33},{97,1},{2,98}... | collective-permute-start | bytes 983048 | tf_op jit(solution)/shard_map/ppermute | solution.py:47
  81.6 0.0 collective-permute-done.2
  81.6 2.2 %collective-permute-start.3 = (bf16[2,16,40,128]{3,2,1,0:T(8,128)(2,1)}, bf16[2,16,40,128]{3,2,1,0:T(8,128)(2,1)}, u32[]{:S(2)}, u32[]{:S(2)}) collective-permute-start(bf16[2,16,40,128]{3,2,1,0:T(8,128)(2,1)} %collective-permute-done.2), channel_id=1, source_target_pairs={{0,96},{32,64},{64,32},{96,0},{1,97},{33,65},{65,33},{97,1},{2,98}... | collective-permute-start | bytes 983048 | tf_op jit(solution)/shard_map/ppermute | solution.py:47
  83.9 1.3 collective-permute-done.6
  85.2 7.0 %collective-permute-done.5 = bf16[2,16,40,128]{3,2,1,0:T(8,128)(2,1)} collective-permute-done((bf16[2,16,40,128]{3,2,1,0:T(8,128)(2,1)}, bf16[2,16,40,128]{3,2,1,0:T(8,128)(2,1)}, u32[]{:S(2)}, u32[]{:S(2)}) %collective-permute-start.5) | collective-permute-done | bytes 327712 | tf_op jit(solution)/shard_map/ppermute | solution.py:47
  92.2 1.3 broadcast_select_fusion.15
  93.6 0.0 collective-permute-done.1
  93.6 2.0 %collective-permute-done.3 = bf16[2,16,40,128]{3,2,1,0:T(8,128)(2,1)} collective-permute-done((bf16[2,16,40,128]{3,2,1,0:T(8,128)(2,1)}, bf16[2,16,40,128]{3,2,1,0:T(8,128)(2,1)}, u32[]{:S(2)}, u32[]{:S(2)}) %collective-permute-start.3) | collective-permute-done | bytes 327712 | tf_op jit(solution)/shard_map/ppermute | solution.py:47
  95.6 1.3 broadcast_select_fusion.19
  96.9 1.7 %pad_maximum_fusion = (bf16[2,16,160,128]{3,2,1,0:T(8,128)(2,1)}, bf16[2,16,160,128]{3,2,1,0:T(8,128)(2,1)}) fusion(bf16[2,16,40,128]{3,2,1,0:T(8,128)(2,1)S(1)} %get-tuple-element.41, bf16[2,16,40,128]{3,2,1,0:T(8,128)(2,1)S(1)} %get-tuple-element.40, bf16[2,16,40,128]{3,2,1,0:T(8,128)(2,1)S(1)} %get-tuple-element.39, ...), kind=kLoop, calls=%fused_computation | loop fusion | flops 10485760 | bytes 5242880 | tf_op jit(solution)/shard_map/concatenate | solution.py:29
  98.6 2.4 %all-gather.8.cloned.1.call-done = bf16[5120,1024]{1,0:T(8,128)(2,1)} async-done(((bf16[160,1024]{1,0:T(8,128)(2,1)}), bf16[5120,1024]{1,0:T(8,128)(2,1)}) %all-gather.8.cloned.1.call-update) | async-done | bytes 10485776 | tf_op jit(solution)/shard_map/all_gather | solution.py:308
  101.1 0.0 copy-start.1
  101.1 7.7 %gradient.1 = (f32[256,1024]{1,0:T(8,128)}, f32[32,1,256]{2,1,0:T(1,128)}, f32[256,512]{1,0:T(8,128)}) custom-call(s32[1,1]{1,0:T(1,128)} %bitcast.core_ref, bf16[2,16,160,128]{3,2,1,0:T(8,128)(2,1)} %get-tuple-element.46.first_hbm, bf16[2,16,160,128]{3,2,1,0:T(8,128)(2,1)} %get-tuple-element.47.second_hbm, bf16[16,2,160,1024]{3,2,1,0:T(8,128)(2,1)} %bitcast.18), custom_call_target="tpu_custom_call" | custom-call | flops 2684354560 | bytes 15000000 | tf_op jit(solution)/shard_map/gradient/pallas_call | solution.py:125
  108.8 2.2 %collective-permute-start.7 = (f32[256,512]{1,0:T(8,128)}, f32[256,512]{1,0:T(8,128)S(1)}, u32[]{:S(2)}, u32[]{:S(2)}) collective-permute-start(f32[256,512]{1,0:T(8,128)} %get-tuple-element.24), channel_id=1, source_target_pairs={{0,1},{1,0},{2,3},{3,2},{4,5},{5,4},{6,7},{7,6},{8,9},{9,8},{10,11... | collective-permute-start | bytes 1572872 | tf_op jit(solution)/shard_map/ppermute | solution.py:313
  111.0 14.8 %all_to_all.20.got_ref = f32[32,1,256]{2,1,0:T(1,128)S(1)} all-to-all(f32[32,1,256]{2,1,0:T(1,128)} %get-tuple-element.20), channel_id=1, replica_groups=mesh['x'=4,'y'=4,'z'=16,'c'=2] {'x','y','c'}, dimensions={0} | all-to-all | bytes 65536 | tf_op jit(solution)/shard_map/all_to_all | solution.py:312
  125.8 0.0 collective-permute-done.7.swapped_ref
  125.8 2.6 %rows.1 = (f32[1,256]{1,0:T(1,128)}, f32[256,128]{1,0:T(8,128)S(1)}, f32[16,1,1152]{2,1,0:T(1,128)}) custom-call(s32[1,1]{1,0:T(1,128)} %bitcast.core_ref, f32[32,1,256]{2,1,0:T(1,128)S(1)} %all_to_all.20.got_ref, f32[2,1,256]{2,1,0:T(1,128)S(1)} %all-gather.4.moment_ref, f32[1,1]{1,0:T(1,128)} %bitcast.6.weight_sq_ref, ...), custom_call_target="tpu_custom_call" | custom-call | tf_op jit(solution)/shard_map/rows/pallas_call | solution.py:192
  128.3 6.5 %all-to-all-start.2 = ((f32[16,1,1152]{2,1,0:T(1,128)}), f32[16,1,1152]{2,1,0:T(1,128)S(1)}, u32[]{:S(2)}, u32[]{:S(2)}) async-start(f32[16,1,1152]{2,1,0:T(1,128)} %get-tuple-element.25), calls=%async_computation.2 | async-start | bytes 147456 | tf_op jit(solution)/shard_map/all_to_all | solution.py:317
  134.8 0.0 copy-done.1
  134.8 11.7 %all-to-all-done.2.got_ref = f32[16,1,1152]{2,1,0:T(1,128)S(1)} async-done(((f32[16,1,1152]{2,1,0:T(1,128)}), f32[16,1,1152]{2,1,0:T(1,128)S(1)}, u32[]{:S(2)}, u32[]{:S(2)}) %all-to-all-start.2) | async-done | bytes 73760 | tf_op jit(solution)/shard_map/all_to_all | solution.py:317
  146.5 0.8 columns.1
  147.4 5.5 %all-to-all-start.3 = ((f32[32,1,128]{2,1,0:T(1,128)}), f32[32,1,128]{2,1,0:T(1,128)S(1)}, u32[]{:S(2)}, u32[]{:S(2)}) async-start(f32[32,1,128]{2,1,0:T(1,128)} %get-tuple-element.26), calls=%async_computation.3 | async-start | bytes 32768 | tf_op jit(solution)/shard_map/all_to_all | solution.py:320
  152.9 1.8 %all-gather.5.cols_ref = f32[2,1,512]{2,1,0:T(1,128)S(1)} all-gather(f32[1,1,512]{2,1,0:T(1,128)S(1)} %bitcast.17), channel_id=5, replica_groups=mesh['x'=4,'y'=4,'z'=16,'c'=2] {'c'}, dimensions={0}, use_global_device_ids=true | all-gather | bytes 6144 | tf_op jit(solution)/shard_map/all_gather | solution.py:321
  154.7 5.2 %all-to-all-done.3.got_ref = f32[32,1,128]{2,1,0:T(1,128)S(1)} async-done(((f32[32,1,128]{2,1,0:T(1,128)}), f32[32,1,128]{2,1,0:T(1,128)S(1)}, u32[]{:S(2)}, u32[]{:S(2)}) %all-to-all-start.3) | async-done | bytes 16416 | tf_op jit(solution)/shard_map/all_to_all | solution.py:320
  159.8 2.4 %update.1 = (f32[256,1024]{1,0:T(8,128)}, bf16[256,1024]{1,0:T(8,128)(2,1)}, f32[2,1,512]{2,1,0:T(1,128)}) custom-call(f32[32,1,128]{2,1,0:T(1,128)S(1)} %all-to-all-done.3.got_ref, f32[1,128]{1,0:T(1,128)S(1)} %get-tuple-element.27.mean_ref, f32[256,128]{1,0:T(8,128)S(1)} %get-tuple-element.28.factor_ref, f32[2,1,512]{2,1,0:T(1,128)S(1)} %all-gather.5.cols_ref, ...), custom_call_target="tpu_custom_call" | custom-call | tf_op jit(solution)/shard_map/update/pallas_call | solution.py:282
  (4 shorter events, 0.1 us)
Async XLA Ops:
  7.2 1.7 %copy-start = (bf16[160,8192]{1,0:T(8,128)(2,1)S(1)}, bf16[160,8192]{1,0:T(8,128)(2,1)}, u32[]{:S(2)}) copy-start(bf16[160,8192]{1,0:T(8,128)(2,1)} %param.5) | copy-start | bytes 7864324
  7.2 21.1 %copy-start.2 = (f32[256]{0:T(256)S(1)}, f32[256]{0:T(256)}, u32[]{:S(2)}) copy-start(f32[256]{0:T(256)} %param.8) | copy-start | bytes 3076
  7.2 93.9 %all-gather.8.cloned.1.call-start = ((), (), s32[]{:S(2)}) async-start(), calls=%async_computation.4 | async-start | bytes 10813440 | tf_op jit(solution)/shard_map/all_gather | solution.py:308
  12.5 28.0 %all-to-all-start = ((bf16[16,40,128]{2,1,0:T(8,128)(2,1)}), bf16[16,40,128]{2,1,0:T(8,128)(2,1)S(1)}, u32[]{:S(2)}, u32[]{:S(2)}) async-start(bf16[16,40,128]{2,1,0:T(8,128)(2,1)} %bitcast.15), calls=%async_computation | async-start | bytes 327680 | tf_op jit(solution)/shard_map/all_to_all | solution.py:38
  52.6 9.8 %collective-permute-start = (bf16[2,16,40,128]{3,2,1,0:T(8,128)(2,1)S(1)}, bf16[2,16,40,128]{3,2,1,0:T(8,128)(2,1)S(1)}, u32[]{:S(2)}, u32[]{:S(2)}) collective-permute-start(bf16[2,16,40,128]{3,2,1,0:T(8,128)(2,1)S(1)} %bitcast.20), channel_id=1, source_target_pairs={{0,1},{1,0},{2,3},{3,2},{4,5},{5,4},{6,7},{7,6},{8,9},{9,8},{10,11... | collective-permute-start | bytes 983048 | tf_op jit(solution)/shard_map/ppermute | solution.py:43
  62.5 12.9 %collective-permute-start.4 = (bf16[2,16,40,128]{3,2,1,0:T(8,128)(2,1)S(1)}, bf16[2,16,40,128]{3,2,1,0:T(8,128)(2,1)}, u32[]{:S(2)}, u32[]{:S(2)}) collective-permute-start(bf16[2,16,40,128]{3,2,1,0:T(8,128)(2,1)S(1)} %get-tuple-element.42), channel_id=1, source_target_pairs={{0,96},{32,64},{64,32},{96,0},{1,97},{33,65},{65,33},{97,1},{2,98}... | collective-permute-start | bytes 983048 | tf_op jit(solution)/shard_map/ppermute | solution.py:47
  67.6 14.1 %collective-permute-start.2 = (bf16[2,16,40,128]{3,2,1,0:T(8,128)(2,1)S(1)}, bf16[2,16,40,128]{3,2,1,0:T(8,128)(2,1)}, u32[]{:S(2)}, u32[]{:S(2)}) collective-permute-start(bf16[2,16,40,128]{3,2,1,0:T(8,128)(2,1)S(1)} %get-tuple-element.43), channel_id=1, source_target_pairs={{0,32},{32,0},{64,96},{96,64},{1,33},{33,1},{65,97},{97,65},{2,34}... | collective-permute-start | bytes 983048 | tf_op jit(solution)/shard_map/ppermute | solution.py:47
  69.5 15.7 %collective-permute-start.6 = (bf16[2,16,40,128]{3,2,1,0:T(8,128)(2,1)S(1)}, bf16[2,16,40,128]{3,2,1,0:T(8,128)(2,1)}, u32[]{:S(2)}, u32[]{:S(2)}) collective-permute-start(bf16[2,16,40,128]{3,2,1,0:T(8,128)(2,1)S(1)} %get-tuple-element.42), channel_id=1, source_target_pairs={{0,32},{32,0},{64,96},{96,64},{1,33},{33,1},{65,97},{97,65},{2,34}... | collective-permute-start | bytes 983048 | tf_op jit(solution)/shard_map/ppermute | solution.py:47
  75.4 16.8 %collective-permute-start.5 = (bf16[2,16,40,128]{3,2,1,0:T(8,128)(2,1)}, bf16[2,16,40,128]{3,2,1,0:T(8,128)(2,1)}, u32[]{:S(2)}, u32[]{:S(2)}) collective-permute-start(bf16[2,16,40,128]{3,2,1,0:T(8,128)(2,1)} %collective-permute-done.4), channel_id=1, source_target_pairs={{0,32},{32,0},{64,96},{96,64},{1,33},{33,1},{65,97},{97,65},{2,34}... | collective-permute-start | bytes 983048 | tf_op jit(solution)/shard_map/ppermute | solution.py:47
  77.4 16.2 %collective-permute-start.1 = (bf16[2,16,40,128]{3,2,1,0:T(8,128)(2,1)S(1)}, bf16[2,16,40,128]{3,2,1,0:T(8,128)(2,1)}, u32[]{:S(2)}, u32[]{:S(2)}) collective-permute-start(bf16[2,16,40,128]{3,2,1,0:T(8,128)(2,1)S(1)} %get-tuple-element.43), channel_id=1, source_target_pairs={{0,96},{32,64},{64,32},{96,0},{1,97},{33,65},{65,33},{97,1},{2,98}... | collective-permute-start | bytes 983048 | tf_op jit(solution)/shard_map/ppermute | solution.py:47
  81.6 14.0 %collective-permute-start.3 = (bf16[2,16,40,128]{3,2,1,0:T(8,128)(2,1)}, bf16[2,16,40,128]{3,2,1,0:T(8,128)(2,1)}, u32[]{:S(2)}, u32[]{:S(2)}) collective-permute-start(bf16[2,16,40,128]{3,2,1,0:T(8,128)(2,1)} %collective-permute-done.2), channel_id=1, source_target_pairs={{0,96},{32,64},{64,32},{96,0},{1,97},{33,65},{65,33},{97,1},{2,98}... | collective-permute-start | bytes 983048 | tf_op jit(solution)/shard_map/ppermute | solution.py:47
  101.1 33.7 %copy-start.1 = (f32[1024]{0:T(1024)S(1)}, f32[1024]{0:T(1024)}, u32[]{:S(2)}) copy-start(f32[1024]{0:T(1024)} %param.9) | copy-start | bytes 12292
  108.8 17.0 %collective-permute-start.7 = (f32[256,512]{1,0:T(8,128)}, f32[256,512]{1,0:T(8,128)S(1)}, u32[]{:S(2)}, u32[]{:S(2)}) collective-permute-start(f32[256,512]{1,0:T(8,128)} %get-tuple-element.24), channel_id=1, source_target_pairs={{0,1},{1,0},{2,3},{3,2},{4,5},{5,4},{6,7},{7,6},{8,9},{9,8},{10,11... | collective-permute-start | bytes 1572872 | tf_op jit(solution)/shard_map/ppermute | solution.py:313
  128.3 18.2 %all-to-all-start.2 = ((f32[16,1,1152]{2,1,0:T(1,128)}), f32[16,1,1152]{2,1,0:T(1,128)S(1)}, u32[]{:S(2)}, u32[]{:S(2)}) async-start(f32[16,1,1152]{2,1,0:T(1,128)} %get-tuple-element.25), calls=%async_computation.2 | async-start | bytes 147456 | tf_op jit(solution)/shard_map/all_to_all | solution.py:317
  147.4 12.5 %all-to-all-start.3 = ((f32[32,1,128]{2,1,0:T(1,128)}), f32[32,1,128]{2,1,0:T(1,128)S(1)}, u32[]{:S(2)}, u32[]{:S(2)}) async-start(f32[32,1,128]{2,1,0:T(1,128)} %get-tuple-element.26), calls=%async_computation.3 | async-start | bytes 32768 | tf_op jit(solution)/shard_map/all_to_all | solution.py:320
Sparse Core Ops, SparseCore 0:
  10.1 90.8 all-gather.7

commit v6 on v5

--- a/solution.py
+++ b/solution.py
@@ -60,7 +60,7 @@
 
 
 def gradient_kernel(
-    core_ref, first_hbm, second_hbm, cot_hbm, grad_hbm, rows_ref, other_hbm,
+    core_ref, first_hbm, second_hbm, cot_hbm, grad_hbm, rows_ref, other_hbm, mine_ref,
     first, second, cot, grad, in_sems, out_sems,
 ):
     fetches = []
@@ -100,6 +100,7 @@
     ]
     for store in stores:
         store.start()
+    mine_ref[...] = grad[:, pl.ds(pl.multiple_of(512 * core_ref[0, 0], 512), 512)]
     squares = jnp.zeros((256, 128), jnp.float32)
     for j in range(8):
         part = grad[:, j * 128 : (j + 1) * 128]
@@ -125,10 +126,11 @@
     return pl.pallas_call(
         gradient_kernel,
         in_specs=[SMEM, HBM, HBM, HBM],
-        out_specs=[HBM, VMEM, HBM],
+        out_specs=[HBM, VMEM, HBM, VMEM],
         out_shape=[
             jax.ShapeDtypeStruct((256, 1024), jnp.float32),
             jax.ShapeDtypeStruct((2 * NX * NY, 1, 256), jnp.float32),
+            jax.ShapeDtypeStruct((256, 512), jnp.float32),
             jax.ShapeDtypeStruct((256, 512), jnp.float32),
         ],
         scratch_shapes=[
@@ -142,22 +144,15 @@
         cost_estimate=pl.CostEstimate(
             flops=2 * 256 * 1024 * 5120, bytes_accessed=15_000_000, transcendentals=0
         ),
-        compiler_params=LARGE,
+        compiler_params=STREAM,
         name="gradient",
     )(core, first, second, all_cotangent)
 
 
 def rows_kernel(
-    core_ref, got_ref, moment_ref, weight_sq_ref, grad_hbm, swapped_ref, new_rows_ref, factor_ref, out_ref, grad, sems
+    core_ref, got_ref, moment_ref, weight_sq_ref, mine_ref, swapped_ref, new_rows_ref, factor_ref, out_ref
 ):
     core = core_ref[0, 0]
-    columns = pl.ds(pl.multiple_of(512 * core, 512), 512)
-    fetches = [
-        pltpu.make_async_copy(grad_hbm.at[rows, columns], grad.at[rows], sems.at[i])
-        for i, rows in enumerate((pl.ds(0, 128), pl.ds(128, 128)))
-    ]
-    for fetch in fetches:
-        fetch.start()
     new_rows = []
     for half in range(2):
         total = got_ref[half]
@@ -174,12 +169,10 @@
     lanes = lax.broadcasted_iota(jnp.int32, (1, 128), 1)
     rows_sum = jnp.sum(own + other, axis=1, keepdims=True)
     scalars = jnp.where(lanes == 0, rows_sum, jnp.where(lanes == 1, weight_sq_ref[0, 0], 0.0))
-    for fetch in fetches:
-        fetch.wait()
     squares, weighted = [], []
     for j in range(4):
         here = slice(128 * j, 128 * (j + 1))
-        mine, theirs = grad[:, here], swapped_ref[:, here]
+        mine, theirs = mine_ref[:, here], swapped_ref[:, here]
         mine, theirs = mine * mine, theirs * theirs
         squares.append(jnp.sum((mine + tiny_eps) + (theirs + tiny_eps), axis=0, keepdims=True))
         weighted.append(jnp.sum(mine * inverse + theirs * inverse_other, axis=0, keepdims=True))
@@ -188,20 +181,19 @@
         out_ref[i] = row
 
 
-def rows_call(core, row_sums, row_moment, weight_sq, gradient, swapped):
+def rows_call(core, row_sums, row_moment, weight_sq, mine, swapped):
     return pl.pallas_call(
         rows_kernel,
-        in_specs=[SMEM, VMEM, VMEM, SMEM, HBM, VMEM],
+        in_specs=[SMEM, VMEM, VMEM, SMEM, VMEM, VMEM],
         out_specs=[VMEM] * 3,
         out_shape=[
             jax.ShapeDtypeStruct((1, 256), jnp.float32),
             jax.ShapeDtypeStruct((256, 128), jnp.float32),
             jax.ShapeDtypeStruct((NZ, 1, 1152), jnp.float32),
         ],
-        scratch_shapes=[pltpu.VMEM((256, 512), jnp.float32), pltpu.SemaphoreType.DMA((2,))],
         compiler_params=STREAM,
         name="rows",
-    )(core, row_sums, row_moment, weight_sq, gradient, swapped)
+    )(core, row_sums, row_moment, weight_sq, mine, swapped)
 
 
 def columns_kernel(got_ref, moment_ref, new_cols_ref, scalars_ref, out_ref):
@@ -308,11 +300,11 @@
     all_cotangent = lax.all_gather(cotangent, ZC, axis=0).reshape(NZ, 2, *cotangent.shape)
     early = (jnp.sum(weight * weight), lax.all_gather(row_moment[None], "c", axis=0))
     first, second, (weight_sq, row_moments) = features_of_rows(inputs, early)
-    gradient, row_sums, swapped = gradient_of(core, first, second, all_cotangent)
+    gradient, row_sums, swapped, mine = gradient_of(core, first, second, all_cotangent)
     row_sums = lax.all_to_all(row_sums, ("x", "y", "c"), 0, 0)
     swapped = lax.ppermute(swapped, "c", pairs(2, 1))
     new_rows, row_factor, packed = rows_call(
-        core, row_sums, row_moments, weight_sq.reshape(1, 1), gradient, swapped
+        core, row_sums, row_moments, weight_sq.reshape(1, 1), mine, swapped
     )
     packed = lax.all_to_all(packed, "z", 0, 0)
     half_moment = jnp.where(c == 0, col_moment[:512], col_moment[512:])

time: 170 us -> 170 us (level)
  no operation moved by 1% of the time
where the time goes in v6:
time: 170 us; the launch traced here: 169 us
  starting transfers between devices  57.2 us (34%)
  waiting for transfers between devices  41.8 us (25%)
  blocking collectives  30.9 us (18%)
  between operations  14.2 us (8%)
  Pallas kernels  12.8 us (8%)
  other arithmetic  6.62 us (4%)
  local copies, waits for them, and re-layouts  5.34 us (3%)
    ppermute x6, starting transfers between devices, swap(): return lax.ppermute(block, 'y', pairs(NY, flip))  18.7 us
    all_to_all x1, starting transfers between devices, features_of_rows(): part = lax.all_to_all(part.transpose(1, 0, 2), 'z', 0, 0)  15.7 us
    all_to_all x1, blocking collectives, on_device(): row_sums = lax.all_to_all(row_sums, ('x', 'y', 'c'), 0, 0)  14.6 us
    ppermute x6, waiting for transfers between devices, swap(): return lax.ppermute(block, 'y', pairs(NY, flip))  12.9 us
    all_gather x1, blocking collectives, features_of_rows(): part = lax.all_gather(part, 'x', axis=0)  12.1 us
    all_to_all x1, waiting for transfers between devices, on_device(): packed = lax.all_to_all(packed, 'z', 0, 0)  11.7 us
    ppermute x1, starting transfers between devices, features_of_rows(): other = lax.ppermute(jnp.where(c == 0, high, low), 'c', pairs(2, 1))  8.58 us
    all_to_all x1, waiting for transfers between devices, features_of_rows(): part = lax.all_to_all(part.transpose(1, 0, 2), 'z', 0, 0)  7.67 us
  transfers between devices with their start and end apart: 12, of which 9 were waited for; matrix products, arithmetic and copies ran while one was open for 6% of the time, Pallas kernels for 0%

profile of v6, /device:TPU:1, one launch (start us, length us, event | category | flops | bytes accessed | tf_op | source)
XLA Modules:
  0.0 169.0 jit_solution(1505434657746580910)
XLA Ops:
  7.2 0.0 copy-start
  7.2 0.0 copy-start.3
  7.2 0.0 all-gather.8.cloned.1.call-start
  7.2 0.7 all-gather.8.cloned.1.call-update
  7.9 1.0 copy-done
  9.0 1.3 reshape.24
  10.3 1.4 constant_dynamic-slice_fusion
  11.7 0.8 copy.16
  12.5 15.7 %all-to-all-start = ((bf16[16,40,128]{2,1,0:T(8,128)(2,1)}), bf16[16,40,128]{2,1,0:T(8,128)(2,1)S(1)}, u32[]{:S(2)}, u32[]{:S(2)}) async-start(bf16[16,40,128]{2,1,0:T(8,128)(2,1)} %bitcast.15), calls=%async_computation | async-start | bytes 327680 | tf_op jit(solution)/shard_map/all_to_all | solution.py:38
  28.2 0.0 copy-done.3
  28.2 2.4 %all-gather.4.moment_ref = f32[2,1,256]{2,1,0:T(1,128)S(1)} all-gather(f32[1,1,256]{2,1,0:T(1,128)S(1)} %bitcast.21), channel_id=2, replica_groups=mesh['x'=4,'y'=4,'z'=16,'c'=2] {'c'}, dimensions={0}, use_global_device_ids=true | all-gather | bytes 3072 | tf_op jit(solution)/shard_map/all_gather | solution.py:301
  30.7 2.1 %multiply_reduce_fusion = f32[]{:T(128)} fusion(f32[256,1024]{1,0:T(8,128)} %weight_hbm.1), kind=kLoop, calls=%fused_computation.2 | loop fusion | flops 524287 | bytes 1048580 | tf_op jit(solution)/shard_map/reduce_sum | solution.py:301
  32.8 7.7 %all-to-all-done = bf16[16,40,128]{2,1,0:T(8,128)(2,1)S(1)} async-done(((bf16[16,40,128]{2,1,0:T(8,128)(2,1)}), bf16[16,40,128]{2,1,0:T(8,128)(2,1)S(1)}, u32[]{:S(2)}, u32[]{:S(2)}) %all-to-all-start) | async-done | bytes 163872 | tf_op jit(solution)/shard_map/all_to_all | solution.py:38
  40.5 12.1 %all-gather.1 = bf16[64,40,128]{2,1,0:T(8,128)(2,1)S(1)} all-gather(bf16[16,40,128]{2,1,0:T(8,128)(2,1)S(1)} %all-to-all-done), channel_id=3, replica_groups=mesh['x'=4,'y'=4,'z'=16,'c'=2] {'x'}, dimensions={0}, use_global_device_ids=true | all-gather | bytes 819200 | tf_op jit(solution)/shard_map/all_gather | solution.py:40
  52.6 8.6 %collective-permute-start = (bf16[2,16,40,128]{3,2,1,0:T(8,128)(2,1)S(1)}, bf16[2,16,40,128]{3,2,1,0:T(8,128)(2,1)S(1)}, u32[]{:S(2)}, u32[]{:S(2)}) collective-permute-start(bf16[2,16,40,128]{3,2,1,0:T(8,128)(2,1)S(1)} %bitcast.20), channel_id=1, source_target_pairs={{0,1},{1,0},{2,3},{3,2},{4,5},{5,4},{6,7},{7,6},{8,9},{9,8},{10,11... | collective-permute-start | bytes 983048 | tf_op jit(solution)/shard_map/ppermute | solution.py:43
  61.2 1.2 collective-permute-done
  62.5 5.1 %collective-permute-start.4 = (bf16[2,16,40,128]{3,2,1,0:T(8,128)(2,1)S(1)}, bf16[2,16,40,128]{3,2,1,0:T(8,128)(2,1)}, u32[]{:S(2)}, u32[]{:S(2)}) collective-permute-start(bf16[2,16,40,128]{3,2,1,0:T(8,128)(2,1)S(1)} %get-tuple-element.44), channel_id=1, source_target_pairs={{0,96},{32,64},{64,32},{96,0},{1,97},{33,65},{65,33},{97,1},{2,98}... | collective-permute-start | bytes 983048 | tf_op jit(solution)/shard_map/ppermute | solution.py:47
  67.6 1.9 %collective-permute-start.2 = (bf16[2,16,40,128]{3,2,1,0:T(8,128)(2,1)S(1)}, bf16[2,16,40,128]{3,2,1,0:T(8,128)(2,1)}, u32[]{:S(2)}, u32[]{:S(2)}) collective-permute-start(bf16[2,16,40,128]{3,2,1,0:T(8,128)(2,1)S(1)} %get-tuple-element.45), channel_id=1, source_target_pairs={{0,32},{32,0},{64,96},{96,64},{1,33},{33,1},{65,97},{97,65},{2,34}... | collective-permute-start | bytes 983048 | tf_op jit(solution)/shard_map/ppermute | solution.py:47
  69.5 3.4 %collective-permute-start.6 = (bf16[2,16,40,128]{3,2,1,0:T(8,128)(2,1)S(1)}, bf16[2,16,40,128]{3,2,1,0:T(8,128)(2,1)}, u32[]{:S(2)}, u32[]{:S(2)}) collective-permute-start(bf16[2,16,40,128]{3,2,1,0:T(8,128)(2,1)S(1)} %get-tuple-element.44), channel_id=1, source_target_pairs={{0,32},{32,0},{64,96},{96,64},{1,33},{33,1},{65,97},{97,65},{2,34}... | collective-permute-start | bytes 983048 | tf_op jit(solution)/shard_map/ppermute | solution.py:47
  72.9 2.6 %collective-permute-done.4 = bf16[2,16,40,128]{3,2,1,0:T(8,128)(2,1)} collective-permute-done((bf16[2,16,40,128]{3,2,1,0:T(8,128)(2,1)S(1)}, bf16[2,16,40,128]{3,2,1,0:T(8,128)(2,1)}, u32[]{:S(2)}, u32[]{:S(2)}) %collective-permute-start.4) | collective-permute-done | bytes 327712 | tf_op jit(solution)/shard_map/ppermute | solution.py:47
  75.4 1.9 %collective-permute-start.5 = (bf16[2,16,40,128]{3,2,1,0:T(8,128)(2,1)}, bf16[2,16,40,128]{3,2,1,0:T(8,128)(2,1)}, u32[]{:S(2)}, u32[]{:S(2)}) collective-permute-start(bf16[2,16,40,128]{3,2,1,0:T(8,128)(2,1)} %collective-permute-done.4), channel_id=1, source_target_pairs={{0,32},{32,0},{64,96},{96,64},{1,33},{33,1},{65,97},{97,65},{2,34}... | collective-permute-start | bytes 983048 | tf_op jit(solution)/shard_map/ppermute | solution.py:47
  77.4 4.3 %collective-permute-start.1 = (bf16[2,16,40,128]{3,2,1,0:T(8,128)(2,1)S(1)}, bf16[2,16,40,128]{3,2,1,0:T(8,128)(2,1)}, u32[]{:S(2)}, u32[]{:S(2)}) collective-permute-start(bf16[2,16,40,128]{3,2,1,0:T(8,128)(2,1)S(1)} %get-tuple-element.45), channel_id=1, source_target_pairs={{0,96},{32,64},{64,32},{96,0},{1,97},{33,65},{65,33},{97,1},{2,98}... | collective-permute-start | bytes 983048 | tf_op jit(solution)/shard_map/ppermute | solution.py:47
  81.6 0.0 collective-permute-done.2
  81.6 2.2 %collective-permute-start.3 = (bf16[2,16,40,128]{3,2,1,0:T(8,128)(2,1)}, bf16[2,16,40,128]{3,2,1,0:T(8,128)(2,1)}, u32[]{:S(2)}, u32[]{:S(2)}) collective-permute-start(bf16[2,16,40,128]{3,2,1,0:T(8,128)(2,1)} %collective-permute-done.2), channel_id=1, source_target_pairs={{0,96},{32,64},{64,32},{96,0},{1,97},{33,65},{65,33},{97,1},{2,98}... | collective-permute-start | bytes 983048 | tf_op jit(solution)/shard_map/ppermute | solution.py:47
  83.9 1.3 collective-permute-done.6
  85.2 7.0 %collective-permute-done.5 = bf16[2,16,40,128]{3,2,1,0:T(8,128)(2,1)} collective-permute-done((bf16[2,16,40,128]{3,2,1,0:T(8,128)(2,1)}, bf16[2,16,40,128]{3,2,1,0:T(8,128)(2,1)}, u32[]{:S(2)}, u32[]{:S(2)}) %collective-permute-start.5) | collective-permute-done | bytes 327712 | tf_op jit(solution)/shard_map/ppermute | solution.py:47
  92.2 1.3 broadcast_select_fusion.15
  93.6 0.0 collective-permute-done.1
  93.6 2.0 %collective-permute-done.3 = bf16[2,16,40,128]{3,2,1,0:T(8,128)(2,1)} collective-permute-done((bf16[2,16,40,128]{3,2,1,0:T(8,128)(2,1)}, bf16[2,16,40,128]{3,2,1,0:T(8,128)(2,1)}, u32[]{:S(2)}, u32[]{:S(2)}) %collective-permute-start.3) | collective-permute-done | bytes 327712 | tf_op jit(solution)/shard_map/ppermute | solution.py:47
  95.6 1.3 broadcast_select_fusion.19
  96.9 1.7 %pad_maximum_fusion = (bf16[2,16,160,128]{3,2,1,0:T(8,128)(2,1)}, bf16[2,16,160,128]{3,2,1,0:T(8,128)(2,1)}) fusion(bf16[2,16,40,128]{3,2,1,0:T(8,128)(2,1)S(1)} %get-tuple-element.43, bf16[2,16,40,128]{3,2,1,0:T(8,128)(2,1)S(1)} %get-tuple-element.42, bf16[2,16,40,128]{3,2,1,0:T(8,128)(2,1)S(1)} %get-tuple-element.41, ...), kind=kLoop, calls=%fused_computation | loop fusion | flops 10485760 | bytes 5242880 | tf_op jit(solution)/shard_map/concatenate | solution.py:29
  98.6 2.5 %all-gather.8.cloned.1.call-done = bf16[5120,1024]{1,0:T(8,128)(2,1)} async-done(((bf16[160,1024]{1,0:T(8,128)(2,1)}), bf16[5120,1024]{1,0:T(8,128)(2,1)}) %all-gather.8.cloned.1.call-update) | async-done | bytes 10485776 | tf_op jit(solution)/shard_map/all_gather | solution.py:300
  101.1 0.0 copy-start.2
  101.1 7.0 %gradient.1 = (f32[256,1024]{1,0:T(8,128)}, f32[32,1,256]{2,1,0:T(1,128)S(1)}, f32[256,512]{1,0:T(8,128)S(1)}, f32[256,512]{1,0:T(8,128)S(1)}) custom-call(s32[1,1]{1,0:T(1,128)} %bitcast.core_ref, bf16[2,16,160,128]{3,2,1,0:T(8,128)(2,1)} %get-tuple-element.48.first_hbm, bf16[2,16,160,128]{3,2,1,0:T(8,128)(2,1)} %get-tuple-element.49.second_hbm, ...), custom_call_target="tpu_custom_call" | custom-call | flops 2684354560 | bytes 15000000 | tf_op jit(solution)/shard_map/gradient/pallas_call | solution.py:126
  108.1 2.2 %collective-permute-start.7 = (f32[256,512]{1,0:T(8,128)S(1)}, f32[256,512]{1,0:T(8,128)S(1)}, u32[]{:S(2)}, u32[]{:S(2)}) collective-permute-start(f32[256,512]{1,0:T(8,128)S(1)} %get-tuple-element.25), channel_id=1, source_target_pairs={{0,1},{1,0},{2,3},{3,2},{4,5},{5,4},{6,7},{7,6},{8,9},{9,8},{10,11... | collective-permute-start | bytes 1572872 | tf_op jit(solution)/shard_map/ppermute | solution.py:305
  110.3 14.6 %all_to_all.20.got_ref = f32[32,1,256]{2,1,0:T(1,128)S(1)} all-to-all(f32[32,1,256]{2,1,0:T(1,128)S(1)} %get-tuple-element.21), channel_id=1, replica_groups=mesh['x'=4,'y'=4,'z'=16,'c'=2] {'x','y','c'}, dimensions={0} | all-to-all | bytes 65536 | tf_op jit(solution)/shard_map/all_to_all | solution.py:304
  124.9 0.0 collective-permute-done.7.swapped_ref
  124.9 0.0 copy-start.1
  124.9 0.8 copy-done.1
  125.7 2.5 %rows.1 = (f32[1,256]{1,0:T(1,128)}, f32[256,128]{1,0:T(8,128)S(1)}, f32[16,1,1152]{2,1,0:T(1,128)}) custom-call(s32[1,1]{1,0:T(1,128)} %bitcast.core_ref, f32[32,1,256]{2,1,0:T(1,128)S(1)} %all_to_all.20.got_ref, f32[2,1,256]{2,1,0:T(1,128)S(1)} %all-gather.4.moment_ref, f32[1,1]{1,0:T(1,128)} %bitcast.6.weight_sq_ref, ...), custom_call_target="tpu_custom_call" | custom-call | tf_op jit(solution)/shard_map/rows/pallas_call | solution.py:185
  128.2 6.4 %all-to-all-start.2 = ((f32[16,1,1152]{2,1,0:T(1,128)}), f32[16,1,1152]{2,1,0:T(1,128)S(1)}, u32[]{:S(2)}, u32[]{:S(2)}) async-start(f32[16,1,1152]{2,1,0:T(1,128)} %get-tuple-element.26), calls=%async_computation.2 | async-start | bytes 147456 | tf_op jit(solution)/shard_map/all_to_all | solution.py:309
  134.7 0.0 copy-done.2
  134.7 11.7 %all-to-all-done.2.got_ref = f32[16,1,1152]{2,1,0:T(1,128)S(1)} async-done(((f32[16,1,1152]{2,1,0:T(1,128)}), f32[16,1,1152]{2,1,0:T(1,128)S(1)}, u32[]{:S(2)}, u32[]{:S(2)}) %all-to-all-start.2) | async-done | bytes 73760 | tf_op jit(solution)/shard_map/all_to_all | solution.py:309
  146.4 0.8 columns.1
  147.2 5.5 %all-to-all-start.3 = ((f32[32,1,128]{2,1,0:T(1,128)}), f32[32,1,128]{2,1,0:T(1,128)S(1)}, u32[]{:S(2)}, u32[]{:S(2)}) async-start(f32[32,1,128]{2,1,0:T(1,128)} %get-tuple-element.27), calls=%async_computation.3 | async-start | bytes 32768 | tf_op jit(solution)/shard_map/all_to_all | solution.py:312
  152.7 1.8 %all-gather.5.cols_ref = f32[2,1,512]{2,1,0:T(1,128)S(1)} all-gather(f32[1,1,512]{2,1,0:T(1,128)S(1)} %bitcast.17), channel_id=5, replica_groups=mesh['x'=4,'y'=4,'z'=16,'c'=2] {'c'}, dimensions={0}, use_global_device_ids=true | all-gather | bytes 6144 | tf_op jit(solution)/shard_map/all_gather | solution.py:313
  154.5 5.2 %all-to-all-done.3.got_ref = f32[32,1,128]{2,1,0:T(1,128)S(1)} async-done(((f32[32,1,128]{2,1,0:T(1,128)}), f32[32,1,128]{2,1,0:T(1,128)S(1)}, u32[]{:S(2)}, u32[]{:S(2)}) %all-to-all-start.3) | async-done | bytes 16416 | tf_op jit(solution)/shard_map/all_to_all | solution.py:312
  159.7 2.4 %update.1 = (f32[256,1024]{1,0:T(8,128)}, bf16[256,1024]{1,0:T(8,128)(2,1)}, f32[2,1,512]{2,1,0:T(1,128)}) custom-call(f32[32,1,128]{2,1,0:T(1,128)S(1)} %all-to-all-done.3.got_ref, f32[1,128]{1,0:T(1,128)S(1)} %get-tuple-element.28.mean_ref, f32[256,128]{1,0:T(8,128)S(1)} %get-tuple-element.29.factor_ref, f32[2,1,512]{2,1,0:T(1,128)S(1)} %all-gather.5.cols_ref, ...), custom_call_target="tpu_custom_call" | custom-call | tf_op jit(solution)/shard_map/update/pallas_call | solution.py:274
  (4 shorter events, 0.1 us)
Async XLA Ops:
  7.2 1.7 %copy-start = (bf16[160,8192]{1,0:T(8,128)(2,1)S(1)}, bf16[160,8192]{1,0:T(8,128)(2,1)}, u32[]{:S(2)}) copy-start(bf16[160,8192]{1,0:T(8,128)(2,1)} %param.5) | copy-start | bytes 7864324
  7.2 21.1 %copy-start.3 = (f32[256]{0:T(256)S(1)}, f32[256]{0:T(256)}, u32[]{:S(2)}) copy-start(f32[256]{0:T(256)} %param.8) | copy-start | bytes 3076
  7.2 93.9 %all-gather.8.cloned.1.call-start = ((), (), s32[]{:S(2)}) async-start(), calls=%async_computation.4 | async-start | bytes 10813440 | tf_op jit(solution)/shard_map/all_gather | solution.py:300
  12.5 28.0 %all-to-all-start = ((bf16[16,40,128]{2,1,0:T(8,128)(2,1)}), bf16[16,40,128]{2,1,0:T(8,128)(2,1)S(1)}, u32[]{:S(2)}, u32[]{:S(2)}) async-start(bf16[16,40,128]{2,1,0:T(8,128)(2,1)} %bitcast.15), calls=%async_computation | async-start | bytes 327680 | tf_op jit(solution)/shard_map/all_to_all | solution.py:38
  52.6 9.8 %collective-permute-start = (bf16[2,16,40,128]{3,2,1,0:T(8,128)(2,1)S(1)}, bf16[2,16,40,128]{3,2,1,0:T(8,128)(2,1)S(1)}, u32[]{:S(2)}, u32[]{:S(2)}) collective-permute-start(bf16[2,16,40,128]{3,2,1,0:T(8,128)(2,1)S(1)} %bitcast.20), channel_id=1, source_target_pairs={{0,1},{1,0},{2,3},{3,2},{4,5},{5,4},{6,7},{7,6},{8,9},{9,8},{10,11... | collective-permute-start | bytes 983048 | tf_op jit(solution)/shard_map/ppermute | solution.py:43
  62.5 12.9 %collective-permute-start.4 = (bf16[2,16,40,128]{3,2,1,0:T(8,128)(2,1)S(1)}, bf16[2,16,40,128]{3,2,1,0:T(8,128)(2,1)}, u32[]{:S(2)}, u32[]{:S(2)}) collective-permute-start(bf16[2,16,40,128]{3,2,1,0:T(8,128)(2,1)S(1)} %get-tuple-element.44), channel_id=1, source_target_pairs={{0,96},{32,64},{64,32},{96,0},{1,97},{33,65},{65,33},{97,1},{2,98}... | collective-permute-start | bytes 983048 | tf_op jit(solution)/shard_map/ppermute | solution.py:47
  67.6 14.1 %collective-permute-start.2 = (bf16[2,16,40,128]{3,2,1,0:T(8,128)(2,1)S(1)}, bf16[2,16,40,128]{3,2,1,0:T(8,128)(2,1)}, u32[]{:S(2)}, u32[]{:S(2)}) collective-permute-start(bf16[2,16,40,128]{3,2,1,0:T(8,128)(2,1)S(1)} %get-tuple-element.45), channel_id=1, source_target_pairs={{0,32},{32,0},{64,96},{96,64},{1,33},{33,1},{65,97},{97,65},{2,34}... | collective-permute-start | bytes 983048 | tf_op jit(solution)/shard_map/ppermute | solution.py:47
  69.5 15.7 %collective-permute-start.6 = (bf16[2,16,40,128]{3,2,1,0:T(8,128)(2,1)S(1)}, bf16[2,16,40,128]{3,2,1,0:T(8,128)(2,1)}, u32[]{:S(2)}, u32[]{:S(2)}) collective-permute-start(bf16[2,16,40,128]{3,2,1,0:T(8,128)(2,1)S(1)} %get-tuple-element.44), channel_id=1, source_target_pairs={{0,32},{32,0},{64,96},{96,64},{1,33},{33,1},{65,97},{97,65},{2,34}... | collective-permute-start | bytes 983048 | tf_op jit(solution)/shard_map/ppermute | solution.py:47
  75.4 16.8 %collective-permute-start.5 = (bf16[2,16,40,128]{3,2,1,0:T(8,128)(2,1)}, bf16[2,16,40,128]{3,2,1,0:T(8,128)(2,1)}, u32[]{:S(2)}, u32[]{:S(2)}) collective-permute-start(bf16[2,16,40,128]{3,2,1,0:T(8,128)(2,1)} %collective-permute-done.4), channel_id=1, source_target_pairs={{0,32},{32,0},{64,96},{96,64},{1,33},{33,1},{65,97},{97,65},{2,34}... | collective-permute-start | bytes 983048 | tf_op jit(solution)/shard_map/ppermute | solution.py:47
  77.4 16.2 %collective-permute-start.1 = (bf16[2,16,40,128]{3,2,1,0:T(8,128)(2,1)S(1)}, bf16[2,16,40,128]{3,2,1,0:T(8,128)(2,1)}, u32[]{:S(2)}, u32[]{:S(2)}) collective-permute-start(bf16[2,16,40,128]{3,2,1,0:T(8,128)(2,1)S(1)} %get-tuple-element.45), channel_id=1, source_target_pairs={{0,96},{32,64},{64,32},{96,0},{1,97},{33,65},{65,33},{97,1},{2,98}... | collective-permute-start | bytes 983048 | tf_op jit(solution)/shard_map/ppermute | solution.py:47
  81.6 14.0 %collective-permute-start.3 = (bf16[2,16,40,128]{3,2,1,0:T(8,128)(2,1)}, bf16[2,16,40,128]{3,2,1,0:T(8,128)(2,1)}, u32[]{:S(2)}, u32[]{:S(2)}) collective-permute-start(bf16[2,16,40,128]{3,2,1,0:T(8,128)(2,1)} %collective-permute-done.2), channel_id=1, source_target_pairs={{0,96},{32,64},{64,32},{96,0},{1,97},{33,65},{65,33},{97,1},{2,98}... | collective-permute-start | bytes 983048 | tf_op jit(solution)/shard_map/ppermute | solution.py:47
  101.1 33.6 %copy-start.2 = (f32[1024]{0:T(1024)S(1)}, f32[1024]{0:T(1024)}, u32[]{:S(2)}) copy-start(f32[1024]{0:T(1024)} %param.9) | copy-start | bytes 12292
  108.1 16.7 %collective-permute-start.7 = (f32[256,512]{1,0:T(8,128)S(1)}, f32[256,512]{1,0:T(8,128)S(1)}, u32[]{:S(2)}, u32[]{:S(2)}) collective-permute-start(f32[256,512]{1,0:T(8,128)S(1)} %get-tuple-element.25), channel_id=1, source_target_pairs={{0,1},{1,0},{2,3},{3,2},{4,5},{5,4},{6,7},{7,6},{8,9},{9,8},{10,11... | collective-permute-start | bytes 1572872 | tf_op jit(solution)/shard_map/ppermute | solution.py:305
  124.9 0.8 copy-start.1
  128.2 18.2 %all-to-all-start.2 = ((f32[16,1,1152]{2,1,0:T(1,128)}), f32[16,1,1152]{2,1,0:T(1,128)S(1)}, u32[]{:S(2)}, u32[]{:S(2)}) async-start(f32[16,1,1152]{2,1,0:T(1,128)} %get-tuple-element.26), calls=%async_computation.2 | async-start | bytes 147456 | tf_op jit(solution)/shard_map/all_to_all | solution.py:309
  147.2 12.5 %all-to-all-start.3 = ((f32[32,1,128]{2,1,0:T(1,128)}), f32[32,1,128]{2,1,0:T(1,128)S(1)}, u32[]{:S(2)}, u32[]{:S(2)}) async-start(f32[32,1,128]{2,1,0:T(1,128)} %get-tuple-element.27), calls=%async_computation.3 | async-start | bytes 32768 | tf_op jit(solution)/shard_map/all_to_all | solution.py:312
Sparse Core Ops, SparseCore 0:
  10.1 90.8 all-gather.7
